TPU v7x, 128 devices: a whole 4x4x4 slice. The times are simulated.
128 devices in a mesh: tm: 4 (over z), space: 32 (over x, y, core).
Axes of the slice: x: 4, y: 4, z: 4, core: 2. Of those that a mesh axis runs over, the one named last changes fastest.
Arguments:
- thickness: float32 [4, 1024, 2048], P('tm', 'space'), may hold values from 0 to 2
- bed_class: int32 [1024, 2048], P('space'), may hold values from 0 to 15
- ice_mask: int32 [1024, 2048], P('space'), may hold values 0 or 1
- zone_index: int32 [1024, 2048], P('space'), may hold values from 0 to 7
- bed_levels: float32 [16], replicated, may hold values from -1 to 1
- balance_rates: float32 [8], replicated, may hold values from -0.3 to 0.3
Outputs:
- end_state: float32 [4, 1024, 2048], P('tm', 'space')
- next_start: float32 [4, 1024, 2048], P('tm', 'space')
All inputs are finite; a program needn't handle non-finite values. No bound on the sum of `ice_mask` on one device may be relied on, other than what follows from the above.
Results may differ from a plain program's by a relative error of at most 0.0001.
Values sent between devices are 32-bit elements; how exact they have to be, the bound alone decides.
No kernel may reach another device: no remote copies, remote signals or barrier semaphores. Data moves between devices by JAX's collectives and lax.ppermute only.
A program may use at most 128 MiB of HBM per device.

v0:
```python
import jax
import jax.numpy as jnp
from jax import lax
from jax.experimental import pallas as pl
from jax.experimental.pallas import tpu as pltpu
from jax.sharding import PartitionSpec as P

ROWS = 32
CH = 16
CROWS = ROWS // 2
CCH = CH // 2
HALO = 8
WIN = ROWS + 2 * HALO
CHALO = 12
CWIN = CROWS + 2 * CHALO
F32 = jnp.float32
BF16 = jnp.bfloat16
VMEM_LIMIT = 40 * 1024 * 1024

FINE_GAIN, FINE_CAP = 0.5 / 4.0 * 0.1, 0.1
COARSE_GAIN, COARSE_CAP = 0.5 / 16.0 * 0.05, 0.05
FINE_TAU, COARSE_TAU = 0.2, 0.4


def column_masks(chunks):
    lane = lax.broadcasted_iota(jnp.int32, (chunks, 128), 1)
    sub = lax.broadcasted_iota(jnp.int32, (chunks, 128), 0)
    return (
        lane == 0,
        (lane == 0) & (sub == 0),
        lane == 127,
        (lane == 127) & (sub == chunks - 1),
    )


def from_left(x, masks, fill):
    a = pltpu.roll(x, 1, axis=2)
    b = pltpu.roll(a, 1, axis=1)
    return jnp.where(masks[1][None], fill, jnp.where(masks[0][None], b, a))


def from_right(x, masks, fill):
    chunks = x.shape[1]
    a = pltpu.roll(x, 127, axis=2)
    b = pltpu.roll(a, chunks - 1, axis=1)
    return jnp.where(masks[3][None], fill, jnp.where(masks[2][None], b, a))


def flow(h, s, d, dy, g, c, ta, lo, hi, masks, gain, cap, block, emit):
    for a in range(lo - 1, hi + 1, block):
        b = min(a + block, hi + 1)
        level = s[a:b]
        right = from_right(level, masks, 0.0)
        left = from_left(level, masks, 0.0)
        sx = s[a + 1 : b + 1] - s[a - 1 : b - 1]
        sy = right - left
        t = h[a:b]
        t2 = t * t
        fifth = t2 * t2 * t
        d[a:b] = jnp.minimum(fifth * gain * (sx * sx + sy * sy), cap)
        dy[a:b] = right - level
    for a in range(lo, hi, block):
        b = min(a + block, hi)
        dd = d[a - 1 : b + 1]
        ss = s[a - 1 : b + 1]
        fx = (dd[1:] + dd[:-1]) * (ss[1:] - ss[:-1])
        mid = dd[1:-1]
        fy = (mid + from_right(mid, masks, 0.0)) * dy[a:b]
        fy_left = from_left(fy, masks, mid * ss[1:-1])
        new = h[a:b] + (fx[1:] - fx[:-1] + fy - fy_left + ta[a:b])
        emit(a, b, jnp.maximum(new, 0.0) * c[a:b])


def split3(x):
    hi = x.astype(BF16)
    r = x - hi.astype(F32)
    mid = r.astype(BF16)
    lo = (r - mid.astype(F32)).astype(BF16)
    return hi, mid, lo


def times(x, m):
    parts = [jnp.dot(p, m, preferred_element_type=F32) for p in split3(x)]
    return parts[0] + (parts[1] + parts[2])


def restrict_mats():
    i = lax.broadcasted_iota(jnp.int32, (128, 128), 0)
    j = lax.broadcasted_iota(jnp.int32, (128, 128), 1)
    half = lax.shift_right_logical(i, 1)
    lo = jnp.where(j == half, 0.25, 0.0).astype(BF16)
    hi = jnp.where(j == half + 64, 0.25, 0.0).astype(BF16)
    return lo, hi


def prolong_mats():
    i = lax.broadcasted_iota(jnp.int32, (128, 128), 0)
    j = lax.broadcasted_iota(jnp.int32, (128, 128), 1)
    half = lax.shift_right_logical(j, 1)
    lo = jnp.where(i == half, 1.0, 0.0).astype(BF16)
    hi = jnp.where(i == half + 64, 1.0, 0.0).astype(BF16)
    return lo, hi


def restrict(x, pair, mats):
    n = x.shape[0] // 2
    y = x.reshape(n, 2, CH, 128)
    pair[0 : n * CH] = (y[:, 0] + y[:, 1]).reshape(n * CH, 128)
    even = pair[pl.ds(0, n * CCH, stride=2), :]
    odd = pair[pl.ds(1, n * CCH, stride=2), :]
    return (times(even, mats[0]) + times(odd, mats[1])).reshape(n, CCH, 128)


def look_up(index, table, size):
    values = [table[k] for k in range(size)]
    bit = 0
    while len(values) > 1:
        on = (lax.shift_right_logical(index, bit) & 1) == 1
        values = [jnp.where(on, values[k + 1], values[k]) for k in range(0, len(values), 2)]
        bit += 1
    return values[0]


def prepare_kernel(thick, bed, mask, zone, levels, rates, h, g, c, ta, up, dn, cg, cc, cta, cup, cdn, pair):
    for r in range(0, ROWS, 8):
        for k in range(CH):
            here = (slice(r, r + 8), slice(k * 128, k * 128 + 128))
            there = (pl.ds(r * CH + k, 8, stride=CH), slice(None))
            h[there] = thick[here]
            g[there] = look_up(bed[here], levels, 16)
            c[there] = mask[here].astype(F32)
            ta[there] = look_up(zone[here], rates, 8) * FINE_TAU
    at = 0
    for ref, count in ((h, 8), (g, 8), (c, 6), (ta, 6)):
        n = count * CH
        up[at : at + n] = ref[ROWS * CH - n : ROWS * CH]
        dn[at : at + n] = ref[0:n]
        at += n
    mats = restrict_mats()
    at = 0
    n = CHALO * CCH
    for ref, coarse, scale in ((g, cg, None), (c, cc, None), (ta, cta, COARSE_TAU / FINE_TAU)):
        value = restrict(ref[...].reshape(ROWS, CH, 128), pair, mats).reshape(CROWS * CCH, 128)
        if scale is not None:
            value = value * scale
        coarse[...] = value
        cup[at : at + n] = value[CROWS * CCH - n :]
        cdn[at : at + n] = value[0:n]
        at += n


def fine_kernel(place, h0, g0, c0, ta0, up, dn, cg0, cc0, cta0, end, prev, payload,
                h, s, s2, g, c, ta, d, dy, ch, cs, cs2, cg, cc, cta, pair):
    at = 0
    for ref, own, count in ((h, h0, 8), (g, g0, 8), (c, c0, 6), (ta, ta0, 6)):
        n = count * CH
        ref[HALO - count : HALO] = up[at : at + n].reshape(count, CH, 128)
        ref[HALO : HALO + ROWS] = own[...].reshape(ROWS, CH, 128)
        ref[HALO + ROWS : HALO + ROWS + count] = dn[at : at + n].reshape(count, CH, 128)
        at += n
    s[...] = g[...] + h[...]
    mats = restrict_mats()
    ch[...] = restrict(h[...], pair, mats)
    cg[0:4] = restrict(g[0:8], pair, mats)
    cg[4:20] = cg0[...].reshape(CROWS, CCH, 128)
    cg[20:24] = restrict(g[40:48], pair, mats)
    for ref, own, fine, scale in ((cc, cc0, c, None), (cta, cta0, ta, COARSE_TAU / FINE_TAU)):
        top = restrict(fine[4:8], pair, mats)
        bottom = restrict(fine[40:44], pair, mats)
        if scale is not None:
            top, bottom = top * scale, bottom * scale
        ref[2:4] = top
        ref[4:20] = own[...].reshape(CROWS, CCH, 128)
        ref[20:22] = bottom
    cs[...] = cg[...] + ch[...]
    cmasks = column_masks(CCH)

    def store_coarse(a, b, value):
        ch[a:b] = value
        cs2[a:b] = value + cg[a:b]

    def store_prev(a, b, value):
        prev[(a - 4) * CCH : (b - 4) * CCH] = value.reshape((b - a) * CCH, 128)

    cd, cdy = d.at[0:24, 0:CCH], dy.at[0:24, 0:CCH]
    flow(ch, cs, cd, cdy, cg, cc, cta, 2, 22, cmasks, COARSE_GAIN, COARSE_CAP, 8, store_coarse)
    flow(ch, cs2, cd, cdy, cg, cc, cta, 4, 20, cmasks, COARSE_GAIN, COARSE_CAP, 8, store_prev)

    masks = column_masks(CH)

    def store_in(target):
        def store(a, b, value):
            h[a:b] = value
            target[a:b] = value + g[a:b]

        return store

    def store_end(a, b, value):
        end[(a - HALO) * CH : (b - HALO) * CH] = value.reshape((b - a) * CH, 128)

    for k in range(4):
        edge = 2 * (k + 1)
        now, later = (s, s2) if k % 2 == 0 else (s2, s)
        flow(h, now, d, dy, g, c, ta, edge, WIN - edge, masks, FINE_GAIN, FINE_CAP, 4,
             store_in(later) if k < 3 else store_end)
    value = restrict(end[...].reshape(ROWS, CH, 128), pair, mats).reshape(CROWS * CCH, 128)
    first = place[0] == 0
    payload[...] = value - jnp.where(first, 0.0, prev[...])


def gather_kernel(place, d1, d2, d3, base, j1, j2, up, dn):
    m = place[0]
    base[...] = jnp.where(m == 1, d1[...], jnp.where(m == 2, d2[...], d3[...]))
    j1[...] = jnp.where(m == 2, d1[...], d2[...])
    j2[...] = d1[...]
    at = 0
    for ref, count in ((base, 12), (j1, 8), (j2, 4)):
        n = count * CCH
        up[at : at + n] = ref[CROWS * CCH - n :]
        dn[at : at + n] = ref[0:n]
        at += n


def chain_kernel(place, own, end, prev, before, base, j1, j2, up, dn, cg0, cc0, cta0, cup, cdn, out, nxt,
                 h, s, s2, g, c, ta, d, dy, jump1, jump2, fix, fixb, fine, pair):
    m = place[0]
    n = CHALO * CCH
    for at, ref, mid in ((0, g, cg0), (1, c, cc0), (2, ta, cta0)):
        ref[0:CHALO] = cup[at * n : at * n + n].reshape(CHALO, CCH, 128)
        ref[CHALO : CHALO + CROWS] = mid[...].reshape(CROWS, CCH, 128)
        ref[CHALO + CROWS : CWIN] = cdn[at * n : at * n + n].reshape(CHALO, CCH, 128)
    at = 0
    for ref, mid, count in ((h, base, 12), (jump1, j1, 8), (jump2, j2, 4)):
        k = count * CCH
        ref[CHALO - count : CHALO] = up[at : at + k].reshape(count, CCH, 128)
        ref[CHALO : CHALO + CROWS] = mid[...].reshape(CROWS, CCH, 128)
        ref[CHALO + CROWS : CHALO + CROWS + count] = dn[at : at + k].reshape(count, CCH, 128)
        at += k
    s[...] = g[...] + h[...]
    masks = column_masks(CCH)
    mats = restrict_mats()
    mine = slice(CHALO, CHALO + CROWS)
    last_prev = restrict(before[...].reshape(ROWS, CH, 128), pair, mats) - j2[...].reshape(CROWS, CCH, 128)
    fix[...] = jnp.zeros_like(fix)
    fixb[...] = jnp.zeros_like(fixb)

    def store_in(target):
        def store(a, b, value):
            h[a:b] = value
            target[a:b] = value + g[a:b]

        return store

    edge = 0
    for k, jump in ((1, jump1), (2, jump2), (3, None)):
        for now, later in ((s, s2), (s2, s)):
            edge += 2
            flow(h, now, d, dy, g, c, ta, edge, CWIN - edge, masks, COARSE_GAIN, COARSE_CAP, 8, store_in(later))

        @pl.when(m == k)
        def _():
            fix[...] = h[mine] - prev[...].reshape(CROWS, CCH, 128)

        if jump is not None:

            @pl.when(m == k + 1)
            def _():
                fixb[...] = h[mine] - last_prev

            for a in range(edge, CWIN - edge, 8):
                b = min(a + 8, CWIN - edge)
                store_in(s)(a, b, h[a:b] + jump[a:b])

    lo, hi = prolong_mats()
    for delta, field, target in ((fix, end, out), (fixb, before, nxt)):
        value = delta[...].reshape(CROWS * CCH, 128)
        pair[pl.ds(0, CROWS * CCH, stride=2), :] = times(value, lo)
        pair[pl.ds(1, CROWS * CCH, stride=2), :] = times(value, hi)
        wide = pair[0 : CROWS * CH].reshape(CROWS, 1, CH, 128)
        total = field[...].reshape(CROWS, 2, CH, 128) + wide
        fine[...] = total.reshape(ROWS * CH, 128)
        for r in range(0, ROWS, 8):
            for k in range(CH):
                target[r : r + 8, k * 128 : k * 128 + 128] = fine[pl.ds(r * CH + k, 8, stride=CH), :]

    @pl.when(m == 0)
    def _():
        nxt[...] = own[...]


def lines(n):
    return jax.ShapeDtypeStruct((n, 128), F32)


def call(kernel, ins, outs, scratch, name, smem=()):
    specs = [
        pl.BlockSpec(memory_space=pltpu.SMEM if i in smem else pltpu.VMEM) for i in range(len(ins))
    ]
    return pl.pallas_call(
        kernel,
        out_shape=outs,
        in_specs=specs,
        out_specs=[pl.BlockSpec(memory_space=pltpu.VMEM)] * len(outs),
        scratch_shapes=[pltpu.VMEM(shape, F32) for shape in scratch],
        compiler_params=pltpu.CompilerParams(vmem_limit_bytes=VMEM_LIMIT),
        name=name,
    )(*ins)


def shifted(x, axis, by):
    devices = lax.axis_size(axis)
    pairs = [(i, i + by) for i in range(devices) if 0 <= i + by < devices]
    return lax.ppermute(x, axis, pairs)


def per_device(thickness, bed_class, ice_mask, zone_index, bed_levels, balance_rates):
    own = thickness[0]
    place = lax.axis_index("tm").astype(jnp.int32).reshape(1)
    fine_lines, coarse_lines = ROWS * CH, CROWS * CCH
    edge_lines, cedge_lines = 28 * CH, 3 * CHALO * CCH
    h, g, c, ta, up, dn, cg, cc, cta, cup, cdn = call(
        prepare_kernel,
        (own, bed_class, ice_mask, zone_index, bed_levels, balance_rates),
        [lines(fine_lines)] * 4 + [lines(edge_lines)] * 2 + [lines(coarse_lines)] * 3 + [lines(cedge_lines)] * 2,
        [(ROWS * CH, 128)],
        "prepare",
        smem=(4, 5),
    )
    up, dn = shifted(up, "space", 1), shifted(dn, "space", -1)
    cup, cdn = shifted(cup, "space", 1), shifted(cdn, "space", -1)
    end, prev, payload = call(
        fine_kernel,
        (place, h, g, c, ta, up, dn, cg, cc, cta),
        [lines(fine_lines), lines(coarse_lines), lines(coarse_lines)],
        [(WIN, CH, 128)] * 8 + [(24, CCH, 128)] * 6 + [(ROWS * CH, 128)],
        "fine",
        smem=(0,),
    )
    d1, d2, d3 = (shifted(payload, "tm", k) for k in (1, 2, 3))
    before = shifted(end, "tm", 1)
    base, j1, j2, jup, jdn = call(
        gather_kernel,
        (place, d1, d2, d3),
        [lines(coarse_lines)] * 3 + [lines(24 * CCH)] * 2,
        [],
        "gather",
        smem=(0,),
    )
    jup, jdn = shifted(jup, "space", 1), shifted(jdn, "space", -1)
    out, nxt = call(
        chain_kernel,
        (place, own, end, prev, before, base, j1, j2, jup, jdn, cg, cc, cta, cup, cdn),
        [jax.ShapeDtypeStruct((ROWS, CH * 128), F32)] * 2,
        [(CWIN, CCH, 128)] * 10 + [(CROWS, CCH, 128)] * 2 + [(ROWS * CH, 128)] * 2,
        "chain",
        smem=(0,),
    )
    return out[None], nxt[None]


def solution(mesh):
    placed = (
        P("tm", "space", None),
        P("space", None),
        P("space", None),
        P("space", None),
        P(),
        P(),
    )
    return jax.shard_map(
        per_device,
        mesh=mesh,
        in_specs=placed,
        out_specs=(P("tm", "space", None), P("tm", "space", None)),
        check_vma=False,
    )
```

profile of v0, /device:TPU:27, one launch (start us, length us, event | category | flops | bytes accessed | tf_op | source)
XLA Modules:
  0.0 54.6 jit_solution(12446600093399911215)
XLA Ops:
  0.6 0.0 copy-start.6
  0.6 0.0 copy-start.5
  0.7 0.6 %copy-done.6 = f32[8]{0:T(128)S(1)} copy-done((f32[8]{0:T(128)S(1)}, f32[8]{0:T(128)}, u32[]{:S(2)}) %copy-start.6) | copy-done | bytes 56
  1.3 0.0 copy-done.5
  1.3 0.0 copy-start
  1.3 0.9 %copy-done = f32[1,32,2048]{2,1,0:T(8,128)S(1)} copy-done((f32[1,32,2048]{2,1,0:T(8,128)S(1)}, f32[1,32,2048]{2,1,0:T(8,128)}, u32[]{:S(2)}) %copy-start) | copy-done | bytes 262168
  2.3 0.0 copy-start.2
  2.3 0.9 %copy-done.2 = s32[32,2048]{1,0:T(8,128)S(1)} copy-done((s32[32,2048]{1,0:T(8,128)S(1)}, s32[32,2048]{1,0:T(8,128)}, u32[]{:S(2)}) %copy-start.2) | copy-done | bytes 262168
  3.2 0.0 copy-start.3
  3.2 0.9 %copy-done.3 = s32[32,2048]{1,0:T(8,128)S(1)} copy-done((s32[32,2048]{1,0:T(8,128)S(1)}, s32[32,2048]{1,0:T(8,128)}, u32[]{:S(2)}) %copy-start.3) | copy-done | bytes 262168
  4.2 0.0 copy-start.4
  4.2 0.9 %copy-done.4 = s32[32,2048]{1,0:T(8,128)S(1)} copy-done((s32[32,2048]{1,0:T(8,128)S(1)}, s32[32,2048]{1,0:T(8,128)}, u32[]{:S(2)}) %copy-start.4) | copy-done | bytes 262168
  5.1 1.5 %prepare.1 = (f32[512,128]{1,0:T(8,128)S(1)}, f32[512,128]{1,0:T(8,128)S(1)}, f32[512,128]{1,0:T(8,128)S(1)}, f32[512,128]{1,0:T(8,128)S(1)}, f32[448,128]{1,0:T...) custom-call(f32[32,2048]{1,0:T(8,128)S(1)} %bitcast.4, ...), custom_call_target="tpu_custom_call" | custom-call | tf_op jit(solution)/shard_map/prepare/pallas_call | solution.py:299
  6.6 3.3 %collective-permute-start = (f32[448,128]{1,0:T(8,128)S(1)}, f32[448,128]{1,0:T(8,128)S(1)}, u32[]{:S(2)}, u32[]{:S(2)}) collective-permute-start(f32[448,128]{1,0:T(8,128)S(1)} %get-tuple-element.27), channel_id=1, source_target_pairs={{0,1},{1,2},{2,3},{3,4},{4,5},{5,6},{6,7},{7,8},{8,9},{9,10},{10,1... | collective-permute-start | bytes 688136 | tf_op jit(solution)/shard_map/ppermute | solution.py:313
  9.9 1.9 %collective-permute-start.1 = (f32[448,128]{1,0:T(8,128)S(1)}, f32[448,128]{1,0:T(8,128)S(1)}, u32[]{:S(2)}, u32[]{:S(2)}) collective-permute-start(f32[448,128]{1,0:T(8,128)S(1)} %get-tuple-element.28), channel_id=1, source_target_pairs={{1,0},{2,1},{3,2},{4,3},{5,4},{6,5},{7,6},{8,7},{9,8},{10,9},{11,1... | collective-permute-start | bytes 688136 | tf_op jit(solution)/shard_map/ppermute | solution.py:313
  11.8 1.0 %collective-permute-done.up = f32[448,128]{1,0:T(8,128)S(1)} collective-permute-done((f32[448,128]{1,0:T(8,128)S(1)}, f32[448,128]{1,0:T(8,128)S(1)}, u32[]{:S(2)}, u32[]{:S(2)}) %collective-permute-start) | collective-permute-done | bytes 229408 | tf_op jit(solution)/shard_map/ppermute | solution.py:313
  12.9 6.5 %collective-permute-done.1.dn = f32[448,128]{1,0:T(8,128)S(1)} collective-permute-done((f32[448,128]{1,0:T(8,128)S(1)}, f32[448,128]{1,0:T(8,128)S(1)}, u32[]{:S(2)}, u32[]{:S(2)}) %collective-permute-start.1) | collective-permute-done | bytes 229408 | tf_op jit(solution)/shard_map/ppermute | solution.py:313
  19.4 0.0 copy-start.1
  19.4 3.5 %fine.1 = (f32[512,128]{1,0:T(8,128)S(1)}, f32[128,128]{1,0:T(8,128)S(1)}, f32[128,128]{1,0:T(8,128)S(1)}) custom-call(s32[1]{0:T(128)} %bitcast.place, f32[512,128]{1,0:T(8,128)S(1)} %get-tuple-element.23.h0, f32[512,128]{1,0:T(8,128)S(1)} %get-tuple-element.24.g0, f32[512,128]{1,0:T(8,128)S(1)} %get-tuple-element.25.c0, ...), custom_call_target="tpu_custom_call" | custom-call | tf_op jit(solution)/shard_map/fine/pallas_call | solution.py:299
  22.8 3.6 %collective-permute-start.2 = (f32[512,128]{1,0:T(8,128)S(1)}, f32[512,128]{1,0:T(8,128)S(1)}, u32[]{:S(2)}, u32[]{:S(2)}) collective-permute-start(f32[512,128]{1,0:T(8,128)S(1)} %get-tuple-element.32.end), channel_id=1, source_target_pairs={{0,32},{32,64},{64,96},{1,33},{33,65},{65,97},{2,34},{34,66},{66,9... | collective-permute-start | bytes 786440 | tf_op jit(solution)/shard_map/ppermute | solution.py:313
  26.4 3.4 %collective-permute-start.5 = (f32[128,128]{1,0:T(8,128)S(1)}, f32[128,128]{1,0:T(8,128)S(1)}, u32[]{:S(2)}, u32[]{:S(2)}) collective-permute-start(f32[128,128]{1,0:T(8,128)S(1)} %get-tuple-element.34), channel_id=1, source_target_pairs={{0,96},{1,97},{2,98},{3,99},{4,100},{5,101},{6,102},{7,103},{8,104... | collective-permute-start | bytes 196616 | tf_op jit(solution)/shard_map/ppermute | solution.py:313
  29.8 2.5 %collective-permute-start.4 = (f32[128,128]{1,0:T(8,128)S(1)}, f32[128,128]{1,0:T(8,128)S(1)}, u32[]{:S(2)}, u32[]{:S(2)}) collective-permute-start(f32[128,128]{1,0:T(8,128)S(1)} %get-tuple-element.34), channel_id=1, source_target_pairs={{0,64},{32,96},{1,65},{33,97},{2,66},{34,98},{3,67},{35,99},{4,68}... | collective-permute-start | bytes 196616 | tf_op jit(solution)/shard_map/ppermute | solution.py:313
  32.3 1.3 %collective-permute-start.3 = (f32[128,128]{1,0:T(8,128)S(1)}, f32[128,128]{1,0:T(8,128)S(1)}, u32[]{:S(2)}, u32[]{:S(2)}) collective-permute-start(f32[128,128]{1,0:T(8,128)S(1)} %get-tuple-element.34), channel_id=1, source_target_pairs={{0,32},{32,64},{64,96},{1,33},{33,65},{65,97},{2,34},{34,66},{66,9... | collective-permute-start | bytes 196616 | tf_op jit(solution)/shard_map/ppermute | solution.py:313
  33.6 2.3 %collective-permute-start.8 = (f32[288,128]{1,0:T(8,128)S(1)}, f32[288,128]{1,0:T(8,128)S(1)}, u32[]{:S(2)}, u32[]{:S(2)}) collective-permute-start(f32[288,128]{1,0:T(8,128)S(1)} %get-tuple-element.40), channel_id=1, source_target_pairs={{0,1},{1,2},{2,3},{3,4},{4,5},{5,6},{6,7},{7,8},{8,9},{9,10},{10,1... | collective-permute-start | bytes 442376 | tf_op jit(solution)/shard_map/ppermute | solution.py:313
  35.9 0.0 collective-permute-done.5.d3
  35.9 2.0 %collective-permute-start.9 = (f32[288,128]{1,0:T(8,128)S(1)}, f32[288,128]{1,0:T(8,128)S(1)}, u32[]{:S(2)}, u32[]{:S(2)}) collective-permute-start(f32[288,128]{1,0:T(8,128)S(1)} %get-tuple-element.41), channel_id=1, source_target_pairs={{1,0},{2,1},{3,2},{4,3},{5,4},{6,5},{7,6},{8,7},{9,8},{10,9},{11,1... | collective-permute-start | bytes 442376 | tf_op jit(solution)/shard_map/ppermute | solution.py:313
  38.0 0.0 collective-permute-done.4.d2
  38.0 0.0 collective-permute-done.3.d1
  38.0 5.7 %collective-permute-start.6 = (f32[192,128]{1,0:T(8,128)S(1)}, f32[192,128]{1,0:T(8,128)S(1)}, u32[]{:S(2)}, u32[]{:S(2)}) collective-permute-start(f32[192,128]{1,0:T(8,128)S(1)} %get-tuple-element.38), channel_id=1, source_target_pairs={{0,1},{1,2},{2,3},{3,4},{4,5},{5,6},{6,7},{7,8},{8,9},{9,10},{10,1... | collective-permute-start | bytes 294920 | tf_op jit(solution)/shard_map/ppermute | solution.py:313
  43.7 1.9 %collective-permute-start.7 = (f32[192,128]{1,0:T(8,128)S(1)}, f32[192,128]{1,0:T(8,128)S(1)}, u32[]{:S(2)}, u32[]{:S(2)}) collective-permute-start(f32[192,128]{1,0:T(8,128)S(1)} %get-tuple-element.39), channel_id=1, source_target_pairs={{1,0},{2,1},{3,2},{4,3},{5,4},{6,5},{7,6},{8,7},{9,8},{10,9},{11,1... | collective-permute-start | bytes 294920 | tf_op jit(solution)/shard_map/ppermute | solution.py:313
  45.6 0.0 collective-permute-done.8.cup
  45.6 0.0 collective-permute-done.9.cdn
  45.6 0.0 collective-permute-done.6.up
  45.6 6.1 %collective-permute-done.7.dn = f32[192,128]{1,0:T(8,128)S(1)} collective-permute-done((f32[192,128]{1,0:T(8,128)S(1)}, f32[192,128]{1,0:T(8,128)S(1)}, u32[]{:S(2)}, u32[]{:S(2)}) %collective-permute-start.7) | collective-permute-done | bytes 98336 | tf_op jit(solution)/shard_map/ppermute | solution.py:313
  51.7 0.0 collective-permute-done.2.before
  51.7 0.0 copy-done.1
  51.7 2.9 %chain.1 = (f32[32,2048]{1,0:T(8,128)}, f32[32,2048]{1,0:T(8,128)}) custom-call(s32[1]{0:T(128)} %bitcast.place, f32[32,2048]{1,0:T(8,128)S(1)} %bitcast.5, f32[512,128]{1,0:T(8,128)S(1)} %get-tuple-element.32.end, f32[128,128]{1,0:T(8,128)S(1)} %get-tuple-element.33.prev, f32[512,128]{1,0:T(8,128)S(1)} %collective-permute-done.2.before, ...), custom_call_target="tpu_custom_call" | custom-call | tf_op jit(solution)/shard_map/chain/pallas_call | solution.py:299
  (1 shorter events, 0.0 us)
Async XLA Ops:
  0.6 0.7 %copy-start.6 = (f32[8]{0:T(128)S(1)}, f32[8]{0:T(128)}, u32[]{:S(2)}) copy-start(f32[8]{0:T(128)} %rates.1) | copy-start | bytes 100
  0.6 0.7 %copy-start.5 = (f32[16]{0:T(128)S(1)}, f32[16]{0:T(128)}, u32[]{:S(2)}) copy-start(f32[16]{0:T(128)} %levels.1) | copy-start | bytes 196
  1.3 0.9 %copy-start = (f32[1,32,2048]{2,1,0:T(8,128)S(1)}, f32[1,32,2048]{2,1,0:T(8,128)}, u32[]{:S(2)}) copy-start(f32[1,32,2048]{2,1,0:T(8,128)} %param.6) | copy-start | bytes 786436
  2.3 0.9 %copy-start.2 = (s32[32,2048]{1,0:T(8,128)S(1)}, s32[32,2048]{1,0:T(8,128)}, u32[]{:S(2)}) copy-start(s32[32,2048]{1,0:T(8,128)} %bed.1) | copy-start | bytes 786436
  3.2 0.9 %copy-start.3 = (s32[32,2048]{1,0:T(8,128)S(1)}, s32[32,2048]{1,0:T(8,128)}, u32[]{:S(2)}) copy-start(s32[32,2048]{1,0:T(8,128)} %mask.1) | copy-start | bytes 786436
  4.2 0.9 %copy-start.4 = (s32[32,2048]{1,0:T(8,128)S(1)}, s32[32,2048]{1,0:T(8,128)}, u32[]{:S(2)}) copy-start(s32[32,2048]{1,0:T(8,128)} %zone.1) | copy-start | bytes 786436
  6.6 6.3 %collective-permute-start = (f32[448,128]{1,0:T(8,128)S(1)}, f32[448,128]{1,0:T(8,128)S(1)}, u32[]{:S(2)}, u32[]{:S(2)}) collective-permute-start(f32[448,128]{1,0:T(8,128)S(1)} %get-tuple-element.27), channel_id=1, source_target_pairs={{0,1},{1,2},{2,3},{3,4},{4,5},{5,6},{6,7},{7,8},{8,9},{9,10},{10,1... | collective-permute-start | bytes 688136 | tf_op jit(solution)/shard_map/ppermute | solution.py:313
  9.9 9.4 %collective-permute-start.1 = (f32[448,128]{1,0:T(8,128)S(1)}, f32[448,128]{1,0:T(8,128)S(1)}, u32[]{:S(2)}, u32[]{:S(2)}) collective-permute-start(f32[448,128]{1,0:T(8,128)S(1)} %get-tuple-element.28), channel_id=1, source_target_pairs={{1,0},{2,1},{3,2},{4,3},{5,4},{6,5},{7,6},{8,7},{9,8},{10,9},{11,1... | collective-permute-start | bytes 688136 | tf_op jit(solution)/shard_map/ppermute | solution.py:313
  19.4 32.4 %copy-start.1 = (f32[1,32,2048]{2,1,0:T(8,128)S(1)}, f32[1,32,2048]{2,1,0:T(8,128)}, u32[]{:S(2)}) copy-start(f32[1,32,2048]{2,1,0:T(8,128)} %param.6) | copy-start | bytes 786436
  22.8 28.9 %collective-permute-start.2 = (f32[512,128]{1,0:T(8,128)S(1)}, f32[512,128]{1,0:T(8,128)S(1)}, u32[]{:S(2)}, u32[]{:S(2)}) collective-permute-start(f32[512,128]{1,0:T(8,128)S(1)} %get-tuple-element.32.end), channel_id=1, source_target_pairs={{0,32},{32,64},{64,96},{1,33},{33,65},{65,97},{2,34},{34,66},{66,9... | collective-permute-start | bytes 786440 | tf_op jit(solution)/shard_map/ppermute | solution.py:313
  26.4 9.5 %collective-permute-start.5 = (f32[128,128]{1,0:T(8,128)S(1)}, f32[128,128]{1,0:T(8,128)S(1)}, u32[]{:S(2)}, u32[]{:S(2)}) collective-permute-start(f32[128,128]{1,0:T(8,128)S(1)} %get-tuple-element.34), channel_id=1, source_target_pairs={{0,96},{1,97},{2,98},{3,99},{4,100},{5,101},{6,102},{7,103},{8,104... | collective-permute-start | bytes 196616 | tf_op jit(solution)/shard_map/ppermute | solution.py:313
  29.8 8.1 %collective-permute-start.4 = (f32[128,128]{1,0:T(8,128)S(1)}, f32[128,128]{1,0:T(8,128)S(1)}, u32[]{:S(2)}, u32[]{:S(2)}) collective-permute-start(f32[128,128]{1,0:T(8,128)S(1)} %get-tuple-element.34), channel_id=1, source_target_pairs={{0,64},{32,96},{1,65},{33,97},{2,66},{34,98},{3,67},{35,99},{4,68}... | collective-permute-start | bytes 196616 | tf_op jit(solution)/shard_map/ppermute | solution.py:313
  32.3 5.7 %collective-permute-start.3 = (f32[128,128]{1,0:T(8,128)S(1)}, f32[128,128]{1,0:T(8,128)S(1)}, u32[]{:S(2)}, u32[]{:S(2)}) collective-permute-start(f32[128,128]{1,0:T(8,128)S(1)} %get-tuple-element.34), channel_id=1, source_target_pairs={{0,32},{32,64},{64,96},{1,33},{33,65},{65,97},{2,34},{34,66},{66,9... | collective-permute-start | bytes 196616 | tf_op jit(solution)/shard_map/ppermute | solution.py:313
  33.6 12.0 %collective-permute-start.8 = (f32[288,128]{1,0:T(8,128)S(1)}, f32[288,128]{1,0:T(8,128)S(1)}, u32[]{:S(2)}, u32[]{:S(2)}) collective-permute-start(f32[288,128]{1,0:T(8,128)S(1)} %get-tuple-element.40), channel_id=1, source_target_pairs={{0,1},{1,2},{2,3},{3,4},{4,5},{5,6},{6,7},{7,8},{8,9},{9,10},{10,1... | collective-permute-start | bytes 442376 | tf_op jit(solution)/shard_map/ppermute | solution.py:313
  35.9 9.7 %collective-permute-start.9 = (f32[288,128]{1,0:T(8,128)S(1)}, f32[288,128]{1,0:T(8,128)S(1)}, u32[]{:S(2)}, u32[]{:S(2)}) collective-permute-start(f32[288,128]{1,0:T(8,128)S(1)} %get-tuple-element.41), channel_id=1, source_target_pairs={{1,0},{2,1},{3,2},{4,3},{5,4},{6,5},{7,6},{8,7},{9,8},{10,9},{11,1... | collective-permute-start | bytes 442376 | tf_op jit(solution)/shard_map/ppermute | solution.py:313
  38.0 7.6 %collective-permute-start.6 = (f32[192,128]{1,0:T(8,128)S(1)}, f32[192,128]{1,0:T(8,128)S(1)}, u32[]{:S(2)}, u32[]{:S(2)}) collective-permute-start(f32[192,128]{1,0:T(8,128)S(1)} %get-tuple-element.38), channel_id=1, source_target_pairs={{0,1},{1,2},{2,3},{3,4},{4,5},{5,6},{6,7},{7,8},{8,9},{9,10},{10,1... | collective-permute-start | bytes 294920 | tf_op jit(solution)/shard_map/ppermute | solution.py:313
  43.7 8.0 %collective-permute-start.7 = (f32[192,128]{1,0:T(8,128)S(1)}, f32[192,128]{1,0:T(8,128)S(1)}, u32[]{:S(2)}, u32[]{:S(2)}) collective-permute-start(f32[192,128]{1,0:T(8,128)S(1)} %get-tuple-element.39), channel_id=1, source_target_pairs={{1,0},{2,1},{3,2},{4,3},{5,4},{6,5},{7,6},{8,7},{9,8},{10,9},{11,1... | collective-permute-start | bytes 294920 | tf_op jit(solution)/shard_map/ppermute | solution.py:313
where the time goes:
time: 55.1 us; the launch traced here: 54.6 us
  starting transfers between devices  27.9 us (51%)
  waiting for transfers between devices  13.6 us (25%)
  Pallas kernels  7.83 us (14%)
  local copies, waits for them, and re-layouts  4.46 us (8%)
  between operations  0.81 us (1%)
    ppermute x10, starting transfers between devices, shifted(): return lax.ppermute(x, axis, pairs)  27.9 us
    ppermute x10, waiting for transfers between devices, shifted(): return lax.ppermute(x, axis, pairs)  13.6 us
    pallas_call x4, Pallas kernels, call(): pl.pallas_call(kernel, out_shape=outs, in_specs=specs, out_specs=[pl.Bloc...  7.83 us
    unnamed x14, local copies, waits for them, and re-layouts  4.46 us
  transfers between devices with their start and end apart: 10, of which 3 were waited for; matrix products, arithmetic and copies ran while one was open for 0% of the time, Pallas kernels for 0%

commit v1 on v0

v1 whole, which is shorter than its diff:
```python
import jax
import jax.numpy as jnp
from jax import lax
from jax.experimental import pallas as pl
from jax.experimental.pallas import tpu as pltpu
from jax.sharding import PartitionSpec as P

ROWS = 32
CH = 16
CROWS = ROWS // 2
CCH = CH // 2
HALO = 8
WIN = ROWS + 2 * HALO
RIM = 10
CHALO = 12
CWIN = CROWS + 2 * CHALO
F32 = jnp.float32
BF16 = jnp.bfloat16

FINE_GAIN, FINE_CAP = 0.5 / 4.0 * 0.1, 0.1
COARSE_GAIN, COARSE_CAP = 0.5 / 16.0 * 0.05, 0.05
FINE_TAU, COARSE_TAU = 0.2, 0.4


def column_masks(chunks):
    lane = lax.broadcasted_iota(jnp.int32, (chunks, 128), 1)
    sub = lax.broadcasted_iota(jnp.int32, (chunks, 128), 0)
    return (
        lane == 0,
        (lane == 0) & (sub == 0),
        lane == 127,
        (lane == 127) & (sub == chunks - 1),
    )


def from_left(x, masks, fill):
    a = pltpu.roll(x, 1, axis=2)
    b = pltpu.roll(a, 1, axis=1)
    return jnp.where(masks[1][None], fill, jnp.where(masks[0][None], b, a))


def from_right(x, masks, fill):
    chunks = x.shape[1]
    a = pltpu.roll(x, 127, axis=2)
    b = pltpu.roll(a, chunks - 1, axis=1)
    return jnp.where(masks[3][None], fill, jnp.where(masks[2][None], b, a))


def flow(h, s, g, c, ta, d, dy, lo, hi, masks, gain, cap, block, emit):
    for a in range(lo - 1, hi + 1, block):
        b = min(a + block, hi + 1)
        level = s[a:b]
        right = from_right(level, masks, 0.0)
        left = from_left(level, masks, 0.0)
        sx = s[a + 1 : b + 1] - s[a - 1 : b - 1]
        sy = right - left
        t = h[a:b]
        t2 = t * t
        fifth = t2 * t2 * t
        d[a:b] = jnp.minimum(fifth * gain * (sx * sx + sy * sy), cap)
        dy[a:b] = right - level
    for a in range(lo, hi, block):
        b = min(a + block, hi)
        dd = d[a - 1 : b + 1]
        ss = s[a - 1 : b + 1]
        fx = (dd[1:] + dd[:-1]) * (ss[1:] - ss[:-1])
        mid = dd[1:-1]
        fy = (mid + from_right(mid, masks, 0.0)) * dy[a:b]
        fy_left = from_left(fy, masks, mid * ss[1:-1])
        new = h[a:b] + (fx[1:] - fx[:-1] + fy - fy_left + ta[a:b])
        emit(a, b, jnp.maximum(new, 0.0) * c[a:b])


def split3(x):
    hi = x.astype(BF16)
    r = x - hi.astype(F32)
    mid = r.astype(BF16)
    lo = (r - mid.astype(F32)).astype(BF16)
    return hi, mid, lo


def times(x, m):
    parts = [jnp.dot(p, m, preferred_element_type=F32) for p in split3(x)]
    return parts[0] + (parts[1] + parts[2])


def restrict_mats():
    i = lax.broadcasted_iota(jnp.int32, (128, 128), 0)
    j = lax.broadcasted_iota(jnp.int32, (128, 128), 1)
    half = lax.shift_right_logical(i, 1)
    lo = jnp.where(j == half, 0.25, 0.0).astype(BF16)
    hi = jnp.where(j == half + 64, 0.25, 0.0).astype(BF16)
    return lo, hi


def prolong_mats():
    i = lax.broadcasted_iota(jnp.int32, (128, 128), 0)
    j = lax.broadcasted_iota(jnp.int32, (128, 128), 1)
    half = lax.shift_right_logical(j, 1)
    lo = jnp.where(i == half, 1.0, 0.0).astype(BF16)
    hi = jnp.where(i == half + 64, 1.0, 0.0).astype(BF16)
    return lo, hi


def restrict(x, pair, mats):
    n = x.shape[0] // 2
    y = x.reshape(n, 2, CH, 128)
    pair[0 : n * CH] = (y[:, 0] + y[:, 1]).reshape(n * CH, 128)
    even = pair[pl.ds(0, n * CCH, stride=2), :]
    odd = pair[pl.ds(1, n * CCH, stride=2), :]
    return (times(even, mats[0]) + times(odd, mats[1])).reshape(n, CCH, 128)


def look_up(index, table, size):
    values = [table[k] for k in range(size)]
    bit = 0
    while len(values) > 1:
        on = (lax.shift_right_logical(index, bit) & 1) == 1
        values = [jnp.where(on, values[k + 1], values[k]) for k in range(0, len(values), 2)]
        bit += 1
    return values[0]


EDGE = (8, 8, 6, 6)
EDGE_LINES = sum(EDGE) * CH
STATIC_LINES = 3 * CHALO * CCH
JUMPS = (12, 8, 4)
JUMP_LINES = sum(JUMPS) * CCH
H0, S0, G, C, TA = 0, 5, 9, 10, 11
CH0, CS0, CG, CC, CTA = 0, 2, 4, 5, 6


def fetch(pairs, sems):
    copies = [pltpu.make_async_copy(src, dst, sems.at[i]) for i, (src, dst) in enumerate(pairs)]
    for copy in copies:
        copy.start()
    return copies


def edge_kernel(space, thick, bed, mask, zone, levels, rates, off, inside,
                tv, bv, mv, zv, lev, rat, hx, gx, cx, tx, sems):
    pairs = [(levels, lev), (rates, rat)]
    for src, dst in ((bed, bv), (zone, zv), (thick, tv), (mask, mv)):
        pairs += [(src.at[0:8], dst.at[0:8]), (src.at[ROWS - 8 : ROWS], dst.at[8:16])]
    for copy in fetch(pairs, sems):
        copy.wait()
    for half in range(2):
        r = slice(half * 8, half * 8 + 8)
        for k in range(CH):
            cols = slice(k * 128, k * 128 + 128)
            there = (half, pl.ds(k, 8, stride=CH), slice(None))
            hx[there] = tv[r, cols]
            gx[there] = look_up(bv[r, cols], lev, 16)
            cx[there] = mv[r, cols].astype(F32)
            tx[there] = look_up(zv[r, cols], rat, 8) * FINE_TAU
    odd = space[0] & 1
    at = 0
    for ref, count in zip((hx, gx, cx, tx), EDGE):
        n = count * CH
        skip = (8 - count) * CH
        off[at : at + n] = ref[odd, pl.ds(odd * skip, n)]
        inside[at : at + n] = ref[1 - odd, pl.ds((1 - odd) * skip, n)]
        at += n


def inner_kernel(space, thick, bed, mask, zone, levels, rates, own, mid, rims, cstate, off, inside,
                 tv, bv, mv, zv, lev, rat, gl, cl, tl, state, d, dy, pair, sems):
    pairs = [(levels, lev), (rates, rat)]
    for r in range(0, ROWS, 8):
        for src, dst in ((bed, bv), (zone, zv), (thick, tv), (mask, mv)):
            pairs.append((src.at[r : r + 8], dst.at[r : r + 8]))
    copies = fetch(pairs, sems)
    copies[0].wait()
    copies[1].wait()
    for r in range(0, ROWS, 8):
        for copy in copies[2 + r // 2 : 6 + r // 2]:
            copy.wait()
        for k in range(CH):
            here = (slice(r, r + 8), slice(k * 128, k * 128 + 128))
            there = (pl.ds(r * CH + k, 8, stride=CH), slice(None))
            own[there] = tv[here]
            gl[there] = look_up(bv[here], lev, 16)
            cl[there] = mv[here].astype(F32)
            tl[there] = look_up(zv[here], rat, 8) * FINE_TAU
    mats = restrict_mats()
    mine = slice(HALO, HALO + ROWS)
    ratio = COARSE_TAU / FINE_TAU
    odd = space[0] & 1
    n = CHALO * CCH
    coarse = {}
    for ref, slot, cslot in ((own, H0, CH0), (gl, G, CG), (cl, C, CC), (tl, TA, CTA)):
        fine = ref[...].reshape(ROWS, CH, 128)
        state[slot, mine] = fine
        value = restrict(fine, pair, mats)
        coarse[cslot] = value * ratio if cslot == CTA else value
        cstate[cslot, 4:20] = coarse[cslot]
    cstate[CS0, 4:20] = coarse[CG] + coarse[CH0]
    state[S0, mine] = state[G, mine] + state[H0, mine]
    for at, cslot in enumerate((CG, CC, CTA)):
        off[at * n : at * n + n] = cstate[cslot, pl.ds(4 + odd * (CROWS - CHALO), CHALO)].reshape(n, 128)
        inside[at * n : at * n + n] = cstate[cslot, pl.ds(4 + (1 - odd) * (CROWS - CHALO), CHALO)].reshape(n, 128)
    coarse_steps(cstate, d, dy, ((6, 18), (8, 16)))
    fine_steps(state, d, dy, [(HALO + 2 * k, WIN - HALO - 2 * k) for k in (1, 2, 3, 4)])
    mid[...] = state[H0 + 4, 2 * HALO : WIN - 2 * HALO].reshape(16 * CH, 128)
    rims[:, 0:RIM] = state[:, HALO : HALO + RIM]
    rims[:, RIM:] = state[:, WIN - HALO - RIM : WIN - HALO]


def coarse_steps(cstate, d, dy, spans):
    masks = column_masks(CCH)
    cd, cdy = d.at[0:24, 0:CCH], dy.at[0:24, 0:CCH]
    for step, (lo, hi) in enumerate(spans):

        def emit(a, b, value, step=step):
            if step == 0:
                cstate[CH0 + 1, a:b] = value
                cstate[CS0 + 1, a:b] = value + cstate[CG, a:b]
            else:
                cstate[CH0, a:b] = value

        flow(cstate.at[CH0 + step], cstate.at[CS0 + step], cstate.at[CG], cstate.at[CC], cstate.at[CTA], cd, cdy,
             lo, hi, masks, COARSE_GAIN, COARSE_CAP, 8, emit)


def fine_steps(state, d, dy, spans):
    masks = column_masks(CH)
    for step, (lo, hi) in enumerate(spans):

        def emit(a, b, value, step=step):
            state[H0 + step + 1, a:b] = value
            if step < 3:
                state[S0 + step + 1, a:b] = value + state[G, a:b]

        flow(state.at[H0 + step], state.at[S0 + step], state.at[G], state.at[C], state.at[TA], d, dy,
             lo, hi, masks, FINE_GAIN, FINE_CAP, 4, emit)


def outer_kernel(place, space, last, off, inside, mid, rims, cstate_in, end, prev, payload, state, cstate, d, dy, pair):
    state[:, HALO : HALO + RIM] = rims[:, 0:RIM]
    state[:, WIN - HALO - RIM : WIN - HALO] = rims[:, RIM:]
    cstate[:, 4:20] = cstate_in[:, 4:20]
    odd = space[0] & 1
    at_border = (space[0] == 0) | (space[0] == last[0])
    at = 0
    for slot, count in zip((H0, G, C, TA), EDGE):
        n = count * CH
        far = jnp.where(at_border, 0.0, off[at : at + n]).reshape(count, CH, 128)
        near = inside[at : at + n].reshape(count, CH, 128)
        state[slot, HALO - count : HALO] = jnp.where(odd == 1, near, far)
        state[slot, HALO + ROWS : HALO + ROWS + count] = jnp.where(odd == 1, far, near)
        at += n
    mats = restrict_mats()
    ratio = COARSE_TAU / FINE_TAU
    for lo, clo in ((0, 0), (40, 20)):
        state[S0, lo : lo + 8] = state[G, lo : lo + 8] + state[H0, lo : lo + 8]
        ground = restrict(state[G, lo : lo + 8], pair, mats)
        thick = restrict(state[H0, lo : lo + 8], pair, mats)
        cstate[CG, clo : clo + 4] = ground
        cstate[CH0, clo : clo + 4] = thick
        cstate[CS0, clo : clo + 4] = ground + thick
    for lo, clo in ((4, 2), (40, 20)):
        cstate[CC, clo : clo + 2] = restrict(state[C, lo : lo + 4], pair, mats)
        cstate[CTA, clo : clo + 2] = restrict(state[TA, lo : lo + 4], pair, mats) * ratio
    coarse_steps(cstate, d, dy, ((2, 6), (4, 8)))
    coarse_steps(cstate, d, dy, ((18, 22), (16, 20)))
    prev[...] = cstate[CH0, 4:20].reshape(CROWS * CCH, 128)
    fine_steps(state, d, dy, [(2 * k, HALO + 2 * k) for k in (1, 2, 3, 4)])
    fine_steps(state, d, dy, [(WIN - HALO - 2 * k, WIN - 2 * k) for k in (1, 2, 3, 4)])
    end[0 : 8 * CH] = state[H0 + 4, 8:16].reshape(8 * CH, 128)
    end[8 * CH : 24 * CH] = mid[...]
    end[24 * CH : 32 * CH] = state[H0 + 4, 32:40].reshape(8 * CH, 128)
    value = restrict(end[...].reshape(ROWS, CH, 128), pair, mats).reshape(CROWS * CCH, 128)
    payload[...] = value - jnp.where(place[0] == 0, 0.0, prev[...])


def gather_kernel(place, space, d1, d2, d3, base, j1, j2, off, inside):
    m = place[0]
    base[...] = jnp.where(m == 1, d1[...], jnp.where(m == 2, d2[...], d3[...]))
    j1[...] = jnp.where(m == 2, d1[...], d2[...])
    j2[...] = d1[...]
    odd = space[0] & 1
    at = 0
    for ref, count in zip((base, j1, j2), JUMPS):
        n = count * CCH
        skip = CROWS * CCH - n
        off[at : at + n] = ref[pl.ds(odd * skip, n)]
        inside[at : at + n] = ref[pl.ds((1 - odd) * skip, n)]
        at += n


def chain_kernel(place, space, last, own, cstate, end, prev, before, base, j1, j2, off, inside, soff, sinside,
                 out_hbm, nxt_hbm, h, s, s2, g, c, ta, d, dy, jump1, jump2, fix, now_m, fine, pair, out, nxt, sems):
    m = place[0]
    odd = space[0] & 1
    at_border = (space[0] == 0) | (space[0] == last[0])
    bottom = CHALO + CROWS

    def window(ref, own, count, far_ref, near_ref, at):
        n = count * CCH
        far = jnp.where(at_border, 0.0, far_ref[at : at + n]).reshape(count, CCH, 128)
        near = near_ref[at : at + n].reshape(count, CCH, 128)
        ref[CHALO - count : CHALO] = jnp.where(odd == 1, near, far)
        ref[CHALO:bottom] = own
        ref[bottom : bottom + count] = jnp.where(odd == 1, far, near)
        return at + n

    at = 0
    for ref, slot in ((g, CG), (c, CC), (ta, CTA)):
        at = window(ref, cstate[slot, 4:20], CHALO, soff, sinside, at)
    at = 0
    for ref, held, count in zip((h, jump1, jump2), (base, j1, j2), JUMPS):
        at = window(ref, held[...].reshape(CROWS, CCH, 128), count, off, inside, at)
    s[...] = g[...] + h[...]
    masks = column_masks(CCH)
    mats = restrict_mats()
    mine = slice(CHALO, bottom)
    fix[...] = jnp.zeros_like(fix)
    now_m[...] = h[mine]
    lo_mat, hi_mat = prolong_mats()

    def spread_out(value, field, target, target_hbm, first, keep=None):
        value = value.reshape(CROWS * CCH, 128)
        pair[pl.ds(0, CROWS * CCH, stride=2), :] = times(value, lo_mat)
        pair[pl.ds(1, CROWS * CCH, stride=2), :] = times(value, hi_mat)
        wide = pair[0 : CROWS * CH].reshape(CROWS, 1, CH, 128)
        total = (field[...].reshape(CROWS, 2, CH, 128) + wide).reshape(ROWS, CH, 128)
        if keep is not None:
            total = jnp.where(m == 0, keep, total)
        fine[...] = total.reshape(ROWS * CH, 128)
        copies = []
        for r in range(0, ROWS, 8):
            for k in range(CH):
                target[r : r + 8, k * 128 : k * 128 + 128] = fine[pl.ds(r * CH + k, 8, stride=CH), :]
            copy = pltpu.make_async_copy(target.at[r : r + 8], target_hbm.at[r : r + 8], sems.at[first + r // 8])
            copy.start()
            copies.append(copy)
        return copies

    edge = 0
    waits = []
    for k, jump in ((1, jump1), (2, jump2), (3, None)):
        if k == 3:
            coarse_before = restrict(before[...].reshape(ROWS, CH, 128), pair, mats)
            waits += spread_out(now_m[...] - coarse_before, before, nxt, nxt_hbm, 0,
                                own[...].reshape(ROWS, CH, 128))
        for now, later in ((s, s2), (s2, s)):
            edge += 2

            def emit(a, b, value, later=later):
                h[a:b] = value
                later[a:b] = value + g[a:b]

            flow(h, now, g, c, ta, d, dy, edge, CWIN - edge, masks, COARSE_GAIN, COARSE_CAP, 8, emit)

        @pl.when(m == k)
        def _():
            fix[...] = h[mine] - prev[...].reshape(CROWS, CCH, 128)

        if jump is not None:
            for a in range(edge, CWIN - edge, 8):
                b = min(a + 8, CWIN - edge)
                emit_value = h[a:b] + jump[a:b]
                h[a:b] = emit_value
                s[a:b] = emit_value + g[a:b]

            @pl.when(m == k + 1)
            def _():
                now_m[...] = h[mine]

    waits += spread_out(fix[...], end, out, out_hbm, 4)
    for copy in waits:
        copy.wait()


def lines(n):
    return jax.ShapeDtypeStruct((n, 128), F32)


VMEM, SMEM, HBM = pltpu.VMEM, pltpu.SMEM, pltpu.HBM


def call(kernel, name, ins, outs, scratch=(), in_spaces=None, out_space=VMEM, limit=16):
    spaces = {"s": SMEM, "h": HBM, "v": VMEM}
    return pl.pallas_call(
        kernel,
        out_shape=outs,
        in_specs=[pl.BlockSpec(memory_space=spaces[letter]) for letter in in_spaces],
        out_specs=[pl.BlockSpec(memory_space=out_space)] * len(outs),
        scratch_shapes=[pltpu.VMEM(item, F32) if isinstance(item, tuple) else item for item in scratch],
        compiler_params=pltpu.CompilerParams(vmem_limit_bytes=limit * 2**20),
        name=name,
    )(*ins)


def shifted(x, by):
    devices = lax.axis_size("tm")
    return lax.ppermute(x, "tm", [(i, (i + by) % devices) for i in range(devices)])


def swapped(off, inside):
    devices = lax.axis_size("space")
    far = [(i, (i + 1) % devices) for i in range(1, devices, 2)]
    near = [(i, i + 1) for i in range(0, devices, 2)]
    both = [pairs + [(j, i) for i, j in pairs] for pairs in (far, near)]
    return lax.ppermute(off, "space", both[0]), lax.ppermute(inside, "space", both[1])


def per_device(thickness, bed_class, ice_mask, zone_index, bed_levels, balance_rates):
    place = lax.axis_index("tm").astype(jnp.int32).reshape(1)
    space = lax.axis_index("space").astype(jnp.int32).reshape(1)
    last = jnp.full((1,), lax.axis_size("space") - 1, jnp.int32)
    raw = (space, thickness[0], bed_class, ice_mask, zone_index, bed_levels, balance_rates)
    coarse_lines = CROWS * CCH
    tables = [pltpu.SMEM((16,), F32), pltpu.SMEM((8,), F32)]
    maps = [pltpu.VMEM((16, 2048), t) for t in (F32, jnp.int32, jnp.int32, jnp.int32)]
    whole = [pltpu.VMEM((ROWS, 2048), t) for t in (F32, jnp.int32, jnp.int32, jnp.int32)]
    off, inside = call(
        edge_kernel, "edges", raw, [lines(EDGE_LINES)] * 2,
        maps + tables + [(2, 8 * CH, 128)] * 4 + [pltpu.SemaphoreType.DMA((10,))],
        "shhhhhh", limit=54,
    )
    off, inside = swapped(off, inside)
    own, mid, rims, cstate, soff, sinside = call(
        inner_kernel, "inner", raw,
        [lines(ROWS * CH), lines(16 * CH), jax.ShapeDtypeStruct((12, 2 * RIM, CH, 128), F32)]
        + [jax.ShapeDtypeStruct((7, 24, CCH, 128), F32)] + [lines(STATIC_LINES)] * 2,
        whole + tables + [(ROWS * CH, 128)] * 3 + [(12, WIN, CH, 128)] + [(WIN, CH, 128)] * 2 + [(ROWS * CH, 128), pltpu.SemaphoreType.DMA((18,))],
        "shhhhhh",
    )
    end, prev, payload = call(
        outer_kernel, "outer", (place, space, last, off, inside, mid, rims, cstate),
        [lines(ROWS * CH)] + [lines(coarse_lines)] * 2,
        [(12, WIN, CH, 128), (7, 24, CCH, 128)] + [(WIN, CH, 128)] * 2 + [(ROWS * CH, 128)],
        "sssvvvvv",
    )
    d1, d2, d3 = (shifted(payload, k) for k in (1, 2, 3))
    base, j1, j2, off, inside = call(
        gather_kernel, "gather", (place, space, d1, d2, d3),
        [lines(coarse_lines)] * 3 + [lines(JUMP_LINES)] * 2, (), "ssvvv",
    )
    before = shifted(lax.optimization_barrier((end, d1, d2, d3))[0], 1)
    soff, sinside = swapped(soff, sinside)
    off, inside = swapped(off, inside)
    out, nxt = call(
        chain_kernel, "chain",
        (place, space, last, own, cstate, end, prev, before, base, j1, j2, off, inside, soff, sinside),
        [jax.ShapeDtypeStruct((ROWS, CH * 128), F32)] * 2,
        [(CWIN, CCH, 128)] * 10 + [(CROWS, CCH, 128)] * 2 + [(ROWS * CH, 128)] * 2
        + [(ROWS, CH * 128)] * 2 + [pltpu.SemaphoreType.DMA((8,))],
        "sss" + "v" * 12, out_space=HBM,
    )
    return out[None], nxt[None]


def solution(mesh):
    placed = (
        P("tm", "space", None),
        P("space", None),
        P("space", None),
        P("space", None),
        P(),
        P(),
    )
    return jax.shard_map(
        per_device,
        mesh=mesh,
        in_specs=placed,
        out_specs=(P("tm", "space", None), P("tm", "space", None)),
        check_vma=False,
    )
```

time: 55.1 us -> 43.3 us (0.79)
  the two profiles are of different devices: /device:TPU:27 before, /device:TPU:0 now
where the time goes in v1:
time: 43.3 us; the launch traced here: 43 us
  starting transfers between devices  15.3 us (35%)
  Pallas kernels  11 us (25%)
  waiting for transfers between devices  9.57 us (22%)
  local copies, waits for them, and re-layouts  6.4 us (15%)
  between operations  0.7 us (2%)
    pallas_call x5, Pallas kernels, call(): pl.pallas_call(kernel, out_shape=outs, in_specs=[pl.BlockSpec(memory_spac...  11 us
    ppermute x3, starting transfers between devices, swapped(): lax.ppermute(off, 'space', both[0])  9.95 us
    unnamed x20, local copies, waits for them, and re-layouts  6.4 us
    ppermute x4, waiting for transfers between devices, shifted(): lax.ppermute(x, 'tm', [(i, (i + by) % devices) for i in range(devices)])  5.81 us
    ppermute x4, starting transfers between devices, shifted(): lax.ppermute(x, 'tm', [(i, (i + by) % devices) for i in range(devices)])  5.37 us
    ppermute x3, waiting for transfers between devices, swapped(): lax.ppermute(off, 'space', both[0])  3.75 us
  transfers between devices with their start and end apart: 10, of which 6 were waited for; matrix products, arithmetic and copies ran while one was open for 0% of the time, Pallas kernels for 10%

profile of v1, /device:TPU:0, one launch (start us, length us, event | category | flops | bytes accessed | tf_op | source)
XLA Modules:
  0.0 43.0 jit_solution(16363465879928854031)
XLA Ops:
  0.6 2.2 %edges.1 = (f32[448,128]{1,0:T(8,128)}, f32[448,128]{1,0:T(8,128)}) custom-call(s32[1]{0:T(128)} %bitcast.1.space, f32[32,2048]{1,0:T(8,128)} %bitcast.5, s32[32,2048]{1,0:T(8,128)} %bed.3, s32[32,2048]{1,0:T(8,128)} %mask.3, s32[32,2048]{1,0:T(8,128)} %zone.3, f32[16]{0:T(128)} %levels.3, f32[8]{0:T(128)} %rates.3), custom_call_target="tpu_custom_call" | custom-call | tf_op jit(solution)/shard_map/edges/pallas_call | solution.py:384
  2.8 4.8 %collective-permute-start = (f32[448,128]{1,0:T(8,128)}, f32[448,128]{1,0:T(8,128)S(1)}, u32[]{:S(2)}, u32[]{:S(2)}) collective-permute-start(f32[448,128]{1,0:T(8,128)} %get-tuple-element.23), channel_id=1, source_target_pairs={{1,2},{3,4},{5,6},{7,8},{9,10},{11,12},{13,14},{15,16},{17,18},{19... | collective-permute-start | bytes 688136 | tf_op jit(solution)/shard_map/ppermute | solution.py:405
  7.6 0.0 collective-permute-start.1
  7.6 0.0 copy-start
  7.6 0.9 %copy-done = f32[1,32,2048]{2,1,0:T(8,128)S(1)} copy-done((f32[1,32,2048]{2,1,0:T(8,128)S(1)}, f32[1,32,2048]{2,1,0:T(8,128)}, u32[]{:S(2)}) %copy-start) | copy-done | bytes 262168
  8.6 0.0 copy-start.1
  8.6 0.9 %copy-done.1 = s32[32,2048]{1,0:T(8,128)S(1)} copy-done((s32[32,2048]{1,0:T(8,128)S(1)}, s32[32,2048]{1,0:T(8,128)}, u32[]{:S(2)}) %copy-start.1) | copy-done | bytes 262168
  9.5 0.0 copy-start.2
  9.5 0.9 %copy-done.2 = s32[32,2048]{1,0:T(8,128)S(1)} copy-done((s32[32,2048]{1,0:T(8,128)S(1)}, s32[32,2048]{1,0:T(8,128)}, u32[]{:S(2)}) %copy-start.2) | copy-done | bytes 262168
  10.5 0.0 copy-start.3
  10.5 0.9 %copy-done.3 = s32[32,2048]{1,0:T(8,128)S(1)} copy-done((s32[32,2048]{1,0:T(8,128)S(1)}, s32[32,2048]{1,0:T(8,128)}, u32[]{:S(2)}) %copy-start.3) | copy-done | bytes 262168
  11.4 0.0 copy-start.4
  11.4 0.7 %copy-done.4 = f32[16]{0:T(128)S(1)} copy-done((f32[16]{0:T(128)S(1)}, f32[16]{0:T(128)}, u32[]{:S(2)}) %copy-start.4) | copy-done | bytes 88
  12.1 0.0 copy-start.5
  12.1 0.7 %copy-done.5 = f32[8]{0:T(128)S(1)} copy-done((f32[8]{0:T(128)S(1)}, f32[8]{0:T(128)}, u32[]{:S(2)}) %copy-start.5) | copy-done | bytes 56
  12.8 4.3 %inner.1 = (f32[512,128]{1,0:T(8,128)S(1)}, f32[256,128]{1,0:T(8,128)S(1)}, f32[12,20,16,128]{3,2,1,0:T(8,128)S(1)}, f32[7,24,8,128]{3,2,1,0:T(8,128)S(1)}, f32[...) custom-call(s32[1]{0:T(128)} %bitcast.1.space, f32[32,2048]{1,0:T(8,128)S(1)} %bitcast.6, s32[32,2048]{1,0:T(8,128)S(1)} %copy-done.1, ...), custom_call_target="tpu_custom_call" | custom-call | tf_op jit(solution)/shard_map/inner/pallas_call | solution.py:384
  17.1 0.0 copy-start.6
  17.1 0.6 %copy-done.6 = f32[288,128]{1,0:T(8,128)} copy-done((f32[288,128]{1,0:T(8,128)}, f32[288,128]{1,0:T(8,128)S(1)}, u32[]{:S(2)}) %copy-start.6) | copy-done | bytes 147480
  17.7 0.0 copy-start.8
  17.7 0.6 %copy-done.8 = f32[288,128]{1,0:T(8,128)} copy-done((f32[288,128]{1,0:T(8,128)}, f32[288,128]{1,0:T(8,128)S(1)}, u32[]{:S(2)}) %copy-start.8) | copy-done | bytes 147480
  18.4 0.0 copy-start.9
  18.4 0.0 copy-start.7
  18.4 0.0 collective-permute-done.off
  18.4 0.0 collective-permute-done.1.inside
  18.4 1.7 %outer.1 = (f32[512,128]{1,0:T(8,128)S(1)}, f32[128,128]{1,0:T(8,128)S(1)}, f32[128,128]{1,0:T(8,128)S(1)}) custom-call(s32[1]{0:T(128)} %bitcast.place, s32[1]{0:T(128)} %bitcast.1.space, s32[1]{0:T(128)} %constant.10.clone.1.last, f32[448,128]{1,0:T(8,128)S(1)} %collective-permute-done.off, f32[448,128]{1,0:T(8,128)S(1)} %collective-permute-done.1.inside, ...), custom_call_target="tpu_custom_call" | custom-call | tf_op jit(solution)/shard_map/outer/pallas_call | solution.py:384
  20.1 4.1 %collective-permute-start.4 = (f32[128,128]{1,0:T(8,128)S(1)}, f32[128,128]{1,0:T(8,128)S(1)}, u32[]{:S(2)}, u32[]{:S(2)}) collective-permute-start(f32[128,128]{1,0:T(8,128)S(1)} %get-tuple-element.29), channel_id=1, source_target_pairs={{0,96},{32,0},{64,32},{96,64},{1,97},{33,1},{65,33},{97,65},{2,98}... | collective-permute-start | bytes 196616 | tf_op jit(solution)/shard_map/ppermute | solution.py:397
  24.2 0.0 collective-permute-start.3
  24.2 1.3 %collective-permute-start.2 = (f32[128,128]{1,0:T(8,128)S(1)}, f32[128,128]{1,0:T(8,128)S(1)}, u32[]{:S(2)}, u32[]{:S(2)}) collective-permute-start(f32[128,128]{1,0:T(8,128)S(1)} %get-tuple-element.29), channel_id=1, source_target_pairs={{0,32},{32,64},{64,96},{96,0},{1,33},{33,65},{65,97},{97,1},{2,34}... | collective-permute-start | bytes 196616 | tf_op jit(solution)/shard_map/ppermute | solution.py:397
  25.4 2.2 %collective-permute-done.4.d3 = f32[128,128]{1,0:T(8,128)S(1)} collective-permute-done((f32[128,128]{1,0:T(8,128)S(1)}, f32[128,128]{1,0:T(8,128)S(1)}, u32[]{:S(2)}, u32[]{:S(2)}) %collective-permute-start.4) | collective-permute-done | bytes 65568 | tf_op jit(solution)/shard_map/ppermute | solution.py:397
  27.6 3.0 %collective-permute-done.3.d2 = f32[128,128]{1,0:T(8,128)S(1)} collective-permute-done((f32[128,128]{1,0:T(8,128)S(1)}, f32[128,128]{1,0:T(8,128)S(1)}, u32[]{:S(2)}, u32[]{:S(2)}) %collective-permute-start.3) | collective-permute-done | bytes 65568 | tf_op jit(solution)/shard_map/ppermute | solution.py:397
  30.6 0.4 collective-permute-done.2.d1
  31.0 0.0 collective-permute-start.5
  31.0 0.0 copy-done.9
  31.0 0.1 collective-permute-start.8
  31.1 0.0 copy-done.7
  31.1 0.0 collective-permute-start.9
  31.2 5.0 %collective-permute-start.6 = (f32[192,128]{1,0:T(8,128)S(1)}, f32[192,128]{1,0:T(8,128)S(1)}, u32[]{:S(2)}, u32[]{:S(2)}) collective-permute-start(f32[192,128]{1,0:T(8,128)S(1)} %get-tuple-element.34), channel_id=1, source_target_pairs={{1,2},{3,4},{5,6},{7,8},{9,10},{11,12},{13,14},{15,16},{17,18},{19... | collective-permute-start | bytes 294920 | tf_op jit(solution)/shard_map/ppermute | solution.py:405
  36.2 0.0 collective-permute-start.7
  36.2 2.7 %collective-permute-done.8.soff = f32[288,128]{1,0:T(8,128)S(1)} collective-permute-done((f32[288,128]{1,0:T(8,128)S(1)}, f32[288,128]{1,0:T(8,128)S(1)}, u32[]{:S(2)}, u32[]{:S(2)}) %collective-permute-start.8) | collective-permute-done | bytes 147488 | tf_op jit(solution)/shard_map/ppermute | solution.py:405
  38.9 0.0 collective-permute-done.9.sinside
  38.9 1.1 %collective-permute-done.6.off = f32[192,128]{1,0:T(8,128)S(1)} collective-permute-done((f32[192,128]{1,0:T(8,128)S(1)}, f32[192,128]{1,0:T(8,128)S(1)}, u32[]{:S(2)}, u32[]{:S(2)}) %collective-permute-start.6) | collective-permute-done | bytes 98336 | tf_op jit(solution)/shard_map/ppermute | solution.py:405
  40.0 0.0 collective-permute-done.7.inside
  40.0 0.2 collective-permute-done.5.before
  40.2 2.8 %chain.1 = (f32[32,2048]{1,0:T(8,128)}, f32[32,2048]{1,0:T(8,128)}) custom-call(s32[1]{0:T(128)} %bitcast.place, s32[1]{0:T(128)} %bitcast.1.space, s32[1]{0:T(128)} %constant.10.clone.1.last, f32[512,128]{1,0:T(8,128)S(1)} %get-tuple-element.21.own, f32[7,24,8,128]{3,2,1,0:T(8,128)S(1)} %get-tuple-element.22.cstate_in.cstate, ...), custom_call_target="tpu_custom_call" | custom-call | tf_op jit(solution)/shard_map/chain/pallas_call | solution.py:384
  (1 shorter events, 0.0 us)
Async XLA Ops:
  2.8 15.5 %collective-permute-start = (f32[448,128]{1,0:T(8,128)}, f32[448,128]{1,0:T(8,128)S(1)}, u32[]{:S(2)}, u32[]{:S(2)}) collective-permute-start(f32[448,128]{1,0:T(8,128)} %get-tuple-element.23), channel_id=1, source_target_pairs={{1,2},{3,4},{5,6},{7,8},{9,10},{11,12},{13,14},{15,16},{17,18},{19... | collective-permute-start | bytes 688136 | tf_op jit(solution)/shard_map/ppermute | solution.py:405
  7.6 10.7 %collective-permute-start.1 = (f32[448,128]{1,0:T(8,128)}, f32[448,128]{1,0:T(8,128)S(1)}, u32[]{:S(2)}, u32[]{:S(2)}) collective-permute-start(f32[448,128]{1,0:T(8,128)} %get-tuple-element.24), channel_id=1, source_target_pairs={{0,1},{2,3},{4,5},{6,7},{8,9},{10,11},{12,13},{14,15},{16,17},{18,... | collective-permute-start | bytes 688136 | tf_op jit(solution)/shard_map/ppermute | solution.py:405
  7.6 1.0 %copy-start = (f32[1,32,2048]{2,1,0:T(8,128)S(1)}, f32[1,32,2048]{2,1,0:T(8,128)}, u32[]{:S(2)}) copy-start(f32[1,32,2048]{2,1,0:T(8,128)} %param.6) | copy-start | bytes 786436
  8.6 0.9 %copy-start.1 = (s32[32,2048]{1,0:T(8,128)S(1)}, s32[32,2048]{1,0:T(8,128)}, u32[]{:S(2)}) copy-start(s32[32,2048]{1,0:T(8,128)} %bed.3) | copy-start | bytes 786436
  9.5 0.9 %copy-start.2 = (s32[32,2048]{1,0:T(8,128)S(1)}, s32[32,2048]{1,0:T(8,128)}, u32[]{:S(2)}) copy-start(s32[32,2048]{1,0:T(8,128)} %mask.3) | copy-start | bytes 786436
  10.5 0.9 %copy-start.3 = (s32[32,2048]{1,0:T(8,128)S(1)}, s32[32,2048]{1,0:T(8,128)}, u32[]{:S(2)}) copy-start(s32[32,2048]{1,0:T(8,128)} %zone.3) | copy-start | bytes 786436
  11.4 0.7 %copy-start.4 = (f32[16]{0:T(128)S(1)}, f32[16]{0:T(128)}, u32[]{:S(2)}) copy-start(f32[16]{0:T(128)} %levels.3) | copy-start | bytes 196
  12.1 0.7 %copy-start.5 = (f32[8]{0:T(128)S(1)}, f32[8]{0:T(128)}, u32[]{:S(2)}) copy-start(f32[8]{0:T(128)} %rates.3) | copy-start | bytes 100
  17.1 0.6 %copy-start.6 = (f32[288,128]{1,0:T(8,128)}, f32[288,128]{1,0:T(8,128)S(1)}, u32[]{:S(2)}) copy-start(f32[288,128]{1,0:T(8,128)S(1)} %get-tuple-element.37) | copy-start | bytes 442372
  17.7 0.7 %copy-start.8 = (f32[288,128]{1,0:T(8,128)}, f32[288,128]{1,0:T(8,128)S(1)}, u32[]{:S(2)}) copy-start(f32[288,128]{1,0:T(8,128)S(1)} %get-tuple-element.36) | copy-start | bytes 442372
  18.4 12.7 %copy-start.9 = (f32[288,128]{1,0:T(8,128)S(1)}, f32[288,128]{1,0:T(8,128)}, u32[]{:S(2)}) copy-start(f32[288,128]{1,0:T(8,128)} %copy-done.8) | copy-start | bytes 442372
  18.4 12.8 %copy-start.7 = (f32[288,128]{1,0:T(8,128)S(1)}, f32[288,128]{1,0:T(8,128)}, u32[]{:S(2)}) copy-start(f32[288,128]{1,0:T(8,128)} %copy-done.6) | copy-start | bytes 442372
  20.1 7.6 %collective-permute-start.4 = (f32[128,128]{1,0:T(8,128)S(1)}, f32[128,128]{1,0:T(8,128)S(1)}, u32[]{:S(2)}, u32[]{:S(2)}) collective-permute-start(f32[128,128]{1,0:T(8,128)S(1)} %get-tuple-element.29), channel_id=1, source_target_pairs={{0,96},{32,0},{64,32},{96,64},{1,97},{33,1},{65,33},{97,65},{2,98}... | collective-permute-start | bytes 196616 | tf_op jit(solution)/shard_map/ppermute | solution.py:397
  24.2 6.4 %collective-permute-start.3 = (f32[128,128]{1,0:T(8,128)S(1)}, f32[128,128]{1,0:T(8,128)S(1)}, u32[]{:S(2)}, u32[]{:S(2)}) collective-permute-start(f32[128,128]{1,0:T(8,128)S(1)} %get-tuple-element.29), channel_id=1, source_target_pairs={{0,64},{32,96},{64,0},{96,32},{1,65},{33,97},{65,1},{97,33},{2,66}... | collective-permute-start | bytes 196616 | tf_op jit(solution)/shard_map/ppermute | solution.py:397
  24.2 6.8 %collective-permute-start.2 = (f32[128,128]{1,0:T(8,128)S(1)}, f32[128,128]{1,0:T(8,128)S(1)}, u32[]{:S(2)}, u32[]{:S(2)}) collective-permute-start(f32[128,128]{1,0:T(8,128)S(1)} %get-tuple-element.29), channel_id=1, source_target_pairs={{0,32},{32,64},{64,96},{96,0},{1,33},{33,65},{65,97},{97,1},{2,34}... | collective-permute-start | bytes 196616 | tf_op jit(solution)/shard_map/ppermute | solution.py:397
  31.0 9.2 %collective-permute-start.5 = (f32[512,128]{1,0:T(8,128)S(1)}, f32[512,128]{1,0:T(8,128)S(1)}, u32[]{:S(2)}, u32[]{:S(2)}) collective-permute-start(f32[512,128]{1,0:T(8,128)S(1)} %get-tuple-element.30.end), channel_id=1, source_target_pairs={{0,32},{32,64},{64,96},{96,0},{1,33},{33,65},{65,97},{97,1},{2,34}... | collective-permute-start | bytes 786440 | tf_op jit(solution)/shard_map/ppermute | solution.py:397
  31.0 7.9 %collective-permute-start.8 = (f32[288,128]{1,0:T(8,128)S(1)}, f32[288,128]{1,0:T(8,128)S(1)}, u32[]{:S(2)}, u32[]{:S(2)}) collective-permute-start(f32[288,128]{1,0:T(8,128)S(1)} %copy-done.9), channel_id=1, source_target_pairs={{1,2},{3,4},{5,6},{7,8},{9,10},{11,12},{13,14},{15,16},{17,18},{19... | collective-permute-start | bytes 442376 | tf_op jit(solution)/shard_map/ppermute | solution.py:405
  31.1 7.8 %collective-permute-start.9 = (f32[288,128]{1,0:T(8,128)S(1)}, f32[288,128]{1,0:T(8,128)S(1)}, u32[]{:S(2)}, u32[]{:S(2)}) collective-permute-start(f32[288,128]{1,0:T(8,128)S(1)} %copy-done.7), channel_id=1, source_target_pairs={{0,1},{2,3},{4,5},{6,7},{8,9},{10,11},{12,13},{14,15},{16,17},{18,... | collective-permute-start | bytes 442376 | tf_op jit(solution)/shard_map/ppermute | solution.py:405
  31.2 8.8 %collective-permute-start.6 = (f32[192,128]{1,0:T(8,128)S(1)}, f32[192,128]{1,0:T(8,128)S(1)}, u32[]{:S(2)}, u32[]{:S(2)}) collective-permute-start(f32[192,128]{1,0:T(8,128)S(1)} %get-tuple-element.34), channel_id=1, source_target_pairs={{1,2},{3,4},{5,6},{7,8},{9,10},{11,12},{13,14},{15,16},{17,18},{19... | collective-permute-start | bytes 294920 | tf_op jit(solution)/shard_map/ppermute | solution.py:405
  36.2 3.8 %collective-permute-start.7 = (f32[192,128]{1,0:T(8,128)S(1)}, f32[192,128]{1,0:T(8,128)S(1)}, u32[]{:S(2)}, u32[]{:S(2)}) collective-permute-start(f32[192,128]{1,0:T(8,128)S(1)} %get-tuple-element.35), channel_id=1, source_target_pairs={{0,1},{2,3},{4,5},{6,7},{8,9},{10,11},{12,13},{14,15},{16,17},{18,... | collective-permute-start | bytes 294920 | tf_op jit(solution)/shard_map/ppermute | solution.py:405

commit v2 on v1

--- a/solution.py
+++ b/solution.py
@@ -23,27 +23,36 @@
 
 
 def column_masks(chunks):
-    lane = lax.broadcasted_iota(jnp.int32, (chunks, 128), 1)
-    sub = lax.broadcasted_iota(jnp.int32, (chunks, 128), 0)
-    return (
-        lane == 0,
-        (lane == 0) & (sub == 0),
-        lane == 127,
-        (lane == 127) & (sub == chunks - 1),
-    )
+    lane = lax.broadcasted_iota(jnp.int32, (8, 128), 1)
+    sub = lax.broadcasted_iota(jnp.int32, (8, 128), 0)
+    left, right = lane == 0, lane == 127
+    return chunks, left, left & (sub == 0), right, right & (sub == 7)
+
+
+def line_of(k):
+    return (k % 2) * 8 + k // 2
 
 
 def from_left(x, masks, fill):
+    chunks, edge, border, _, _ = masks
     a = pltpu.roll(x, 1, axis=2)
-    b = pltpu.roll(a, 1, axis=1)
-    return jnp.where(masks[1][None], fill, jnp.where(masks[0][None], b, a))
+    if chunks == CCH:
+        return jnp.where(border[None], fill, jnp.where(edge[None], pltpu.roll(a, 1, axis=1), a))
+    even, odd = a[:, :8], a[:, 8:]
+    if not isinstance(fill, float):
+        fill = fill[:, :8]
+    first = jnp.where(border[None], fill, jnp.where(edge[None], pltpu.roll(odd, 1, axis=1), even))
+    return jnp.concatenate([first, jnp.where(edge[None], even, odd)], axis=1)
 
 
 def from_right(x, masks, fill):
-    chunks = x.shape[1]
+    chunks, _, _, edge, border = masks
     a = pltpu.roll(x, 127, axis=2)
-    b = pltpu.roll(a, chunks - 1, axis=1)
-    return jnp.where(masks[3][None], fill, jnp.where(masks[2][None], b, a))
+    if chunks == CCH:
+        return jnp.where(border[None], fill, jnp.where(edge[None], pltpu.roll(a, 7, axis=1), a))
+    even, odd = a[:, :8], a[:, 8:]
+    second = jnp.where(border[None], fill, jnp.where(edge[None], pltpu.roll(even, 7, axis=1), odd))
+    return jnp.concatenate([jnp.where(edge[None], odd, even), second], axis=1)
 
 
 def flow(h, s, g, c, ta, d, dy, lo, hi, masks, gain, cap, block, emit):
@@ -102,12 +111,11 @@
     return lo, hi
 
 
-def restrict(x, pair, mats):
+def restrict(x, mats):
     n = x.shape[0] // 2
     y = x.reshape(n, 2, CH, 128)
-    pair[0 : n * CH] = (y[:, 0] + y[:, 1]).reshape(n * CH, 128)
-    even = pair[pl.ds(0, n * CCH, stride=2), :]
-    odd = pair[pl.ds(1, n * CCH, stride=2), :]
+    y = y[:, 0] + y[:, 1]
+    even, odd = y[:, :8].reshape(n * CCH, 128), y[:, 8:].reshape(n * CCH, 128)
     return (times(even, mats[0]) + times(odd, mats[1])).reshape(n, CCH, 128)
 
 
@@ -127,6 +135,7 @@
 JUMPS = (12, 8, 4)
 JUMP_LINES = sum(JUMPS) * CCH
 H0, S0, G, C, TA = 0, 5, 9, 10, 11
+KEPT = (0, 1, 2, 3, 4, 9, 10, 11)
 CH0, CS0, CG, CC, CTA = 0, 2, 4, 5, 6
 
 
@@ -137,18 +146,24 @@
     return copies
 
 
-def edge_kernel(space, thick, bed, mask, zone, levels, rates, off, inside,
-                tv, bv, mv, zv, lev, rat, hx, gx, cx, tx, sems):
+def edge_kernel(space, thick, bed, mask, zone, levels, rates, off, inside, tv, bv, mv, zv, tab,
+                lev, rat, hx, gx, cx, tx, sems):
     pairs = [(levels, lev), (rates, rat)]
-    for src, dst in ((bed, bv), (zone, zv), (thick, tv), (mask, mv)):
-        pairs += [(src.at[0:8], dst.at[0:8]), (src.at[ROWS - 8 : ROWS], dst.at[8:16])]
-    for copy in fetch(pairs, sems):
+    maps = ((bed, bv), (zone, zv), (thick, tv), (mask, mv))
+    for r, count in ((0, 8), (ROWS - 8, 8), (8, ROWS - 16)):
+        pairs += [(src.at[r : r + count], dst.at[r : r + count]) for src, dst in maps]
+    copies = fetch(pairs, sems)
+    for copy in copies[:10]:
         copy.wait()
+    for k in range(16):
+        tab[k : k + 1] = jnp.full((1, 128), lev[k], F32)
+    for k in range(8):
+        tab[16 + k : 17 + k] = jnp.full((1, 128), rat[k], F32)
     for half in range(2):
-        r = slice(half * 8, half * 8 + 8)
+        r = slice(half * (ROWS - 8), half * (ROWS - 8) + 8)
         for k in range(CH):
             cols = slice(k * 128, k * 128 + 128)
-            there = (half, pl.ds(k, 8, stride=CH), slice(None))
+            there = (half, pl.ds(line_of(k), 8, stride=CH), slice(None))
             hx[there] = tv[r, cols]
             gx[there] = look_up(bv[r, cols], lev, 16)
             cx[there] = mv[r, cols].astype(F32)
@@ -161,23 +176,17 @@
         off[at : at + n] = ref[odd, pl.ds(odd * skip, n)]
         inside[at : at + n] = ref[1 - odd, pl.ds((1 - odd) * skip, n)]
         at += n
-
-
-def inner_kernel(space, thick, bed, mask, zone, levels, rates, own, mid, rims, cstate, off, inside,
-                 tv, bv, mv, zv, lev, rat, gl, cl, tl, state, d, dy, pair, sems):
-    pairs = [(levels, lev), (rates, rat)]
+    for copy in copies[10:]:
+        copy.wait()
+
+
+def inner_kernel(space, tv, bv, mv, zv, tab, own, mid, rims, cstate, off, gl, cl, tl, state, d, dy):
+    table = [jnp.broadcast_to(tab[k : k + 1], (8, 128)) for k in range(24)]
+    lev, rat = table[:16], table[16:]
     for r in range(0, ROWS, 8):
-        for src, dst in ((bed, bv), (zone, zv), (thick, tv), (mask, mv)):
-            pairs.append((src.at[r : r + 8], dst.at[r : r + 8]))
-    copies = fetch(pairs, sems)
-    copies[0].wait()
-    copies[1].wait()
-    for r in range(0, ROWS, 8):
-        for copy in copies[2 + r // 2 : 6 + r // 2]:
-            copy.wait()
         for k in range(CH):
             here = (slice(r, r + 8), slice(k * 128, k * 128 + 128))
-            there = (pl.ds(r * CH + k, 8, stride=CH), slice(None))
+            there = (pl.ds(r * CH + line_of(k), 8, stride=CH), slice(None))
             own[there] = tv[here]
             gl[there] = look_up(bv[here], lev, 16)
             cl[there] = mv[here].astype(F32)
@@ -191,19 +200,19 @@
     for ref, slot, cslot in ((own, H0, CH0), (gl, G, CG), (cl, C, CC), (tl, TA, CTA)):
         fine = ref[...].reshape(ROWS, CH, 128)
         state[slot, mine] = fine
-        value = restrict(fine, pair, mats)
+        value = restrict(fine, mats)
         coarse[cslot] = value * ratio if cslot == CTA else value
         cstate[cslot, 4:20] = coarse[cslot]
     cstate[CS0, 4:20] = coarse[CG] + coarse[CH0]
     state[S0, mine] = state[G, mine] + state[H0, mine]
     for at, cslot in enumerate((CG, CC, CTA)):
         off[at * n : at * n + n] = cstate[cslot, pl.ds(4 + odd * (CROWS - CHALO), CHALO)].reshape(n, 128)
-        inside[at * n : at * n + n] = cstate[cslot, pl.ds(4 + (1 - odd) * (CROWS - CHALO), CHALO)].reshape(n, 128)
     coarse_steps(cstate, d, dy, ((6, 18), (8, 16)))
     fine_steps(state, d, dy, [(HALO + 2 * k, WIN - HALO - 2 * k) for k in (1, 2, 3, 4)])
     mid[...] = state[H0 + 4, 2 * HALO : WIN - 2 * HALO].reshape(16 * CH, 128)
-    rims[:, 0:RIM] = state[:, HALO : HALO + RIM]
-    rims[:, RIM:] = state[:, WIN - HALO - RIM : WIN - HALO]
+    for at, slot in enumerate(KEPT):
+        rims[at, 0:RIM] = state[slot, HALO : HALO + RIM]
+        rims[at, RIM:] = state[slot, WIN - HALO - RIM : WIN - HALO]
 
 
 def coarse_steps(cstate, d, dy, spans):
@@ -235,9 +244,13 @@
              lo, hi, masks, FINE_GAIN, FINE_CAP, 4, emit)
 
 
-def outer_kernel(place, space, last, off, inside, mid, rims, cstate_in, end, prev, payload, state, cstate, d, dy, pair):
-    state[:, HALO : HALO + RIM] = rims[:, 0:RIM]
-    state[:, WIN - HALO - RIM : WIN - HALO] = rims[:, RIM:]
+def outer_kernel(place, space, last, off, inside, mid, rims, cstate_in, end, prev, payload, state, cstate, d, dy):
+    for at, slot in enumerate(KEPT):
+        state[slot, HALO : HALO + RIM] = rims[at, 0:RIM]
+        state[slot, WIN - HALO - RIM : WIN - HALO] = rims[at, RIM:]
+    for rim in (slice(HALO, HALO + RIM), slice(WIN - HALO - RIM, WIN - HALO)):
+        for step in range(4):
+            state[S0 + step, rim] = state[H0 + step, rim] + state[G, rim]
     cstate[:, 4:20] = cstate_in[:, 4:20]
     odd = space[0] & 1
     at_border = (space[0] == 0) | (space[0] == last[0])
@@ -253,14 +266,14 @@
     ratio = COARSE_TAU / FINE_TAU
     for lo, clo in ((0, 0), (40, 20)):
         state[S0, lo : lo + 8] = state[G, lo : lo + 8] + state[H0, lo : lo + 8]
-        ground = restrict(state[G, lo : lo + 8], pair, mats)
-        thick = restrict(state[H0, lo : lo + 8], pair, mats)
+        ground = restrict(state[G, lo : lo + 8], mats)
+        thick = restrict(state[H0, lo : lo + 8], mats)
         cstate[CG, clo : clo + 4] = ground
         cstate[CH0, clo : clo + 4] = thick
         cstate[CS0, clo : clo + 4] = ground + thick
     for lo, clo in ((4, 2), (40, 20)):
-        cstate[CC, clo : clo + 2] = restrict(state[C, lo : lo + 4], pair, mats)
-        cstate[CTA, clo : clo + 2] = restrict(state[TA, lo : lo + 4], pair, mats) * ratio
+        cstate[CC, clo : clo + 2] = restrict(state[C, lo : lo + 4], mats)
+        cstate[CTA, clo : clo + 2] = restrict(state[TA, lo : lo + 4], mats) * ratio
     coarse_steps(cstate, d, dy, ((2, 6), (4, 8)))
     coarse_steps(cstate, d, dy, ((18, 22), (16, 20)))
     prev[...] = cstate[CH0, 4:20].reshape(CROWS * CCH, 128)
@@ -269,11 +282,15 @@
     end[0 : 8 * CH] = state[H0 + 4, 8:16].reshape(8 * CH, 128)
     end[8 * CH : 24 * CH] = mid[...]
     end[24 * CH : 32 * CH] = state[H0 + 4, 32:40].reshape(8 * CH, 128)
-    value = restrict(end[...].reshape(ROWS, CH, 128), pair, mats).reshape(CROWS * CCH, 128)
+    value = restrict(end[...].reshape(ROWS, CH, 128), mats).reshape(CROWS * CCH, 128)
     payload[...] = value - jnp.where(place[0] == 0, 0.0, prev[...])
 
 
-def gather_kernel(place, space, d1, d2, d3, base, j1, j2, off, inside):
+def pack_kernel(source, target):
+    target[...] = source[...]
+
+
+def gather_kernel(place, space, cstate, d1, d2, d3, base, j1, j2, off, inside):
     m = place[0]
     base[...] = jnp.where(m == 1, d1[...], jnp.where(m == 2, d2[...], d3[...]))
     j1[...] = jnp.where(m == 2, d1[...], d2[...])
@@ -286,19 +303,23 @@
         off[at : at + n] = ref[pl.ds(odd * skip, n)]
         inside[at : at + n] = ref[pl.ds((1 - odd) * skip, n)]
         at += n
-
-
-def chain_kernel(place, space, last, own, cstate, end, prev, before, base, j1, j2, off, inside, soff, sinside,
-                 out_hbm, nxt_hbm, h, s, s2, g, c, ta, d, dy, jump1, jump2, fix, now_m, fine, pair, out, nxt, sems):
+    n = CHALO * CCH
+    for cslot in (CG, CC, CTA):
+        inside[at : at + n] = cstate[cslot, pl.ds(4 + (1 - odd) * (CROWS - CHALO), CHALO)].reshape(n, 128)
+        at += n
+
+
+def chain_kernel(place, space, last, own, cstate, end, prev, before, base, j1, j2, off, inside, soff,
+                 out_hbm, nxt_hbm, h, s, s2, g, c, ta, d, dy, jump1, jump2, fix, now_m, fine, out, nxt, sems):
     m = place[0]
     odd = space[0] & 1
     at_border = (space[0] == 0) | (space[0] == last[0])
     bottom = CHALO + CROWS
 
-    def window(ref, own, count, far_ref, near_ref, at):
+    def window(ref, own, count, far_ref, at, skip):
         n = count * CCH
         far = jnp.where(at_border, 0.0, far_ref[at : at + n]).reshape(count, CCH, 128)
-        near = near_ref[at : at + n].reshape(count, CCH, 128)
+        near = inside[skip + at : skip + at + n].reshape(count, CCH, 128)
         ref[CHALO - count : CHALO] = jnp.where(odd == 1, near, far)
         ref[CHALO:bottom] = own
         ref[bottom : bottom + count] = jnp.where(odd == 1, far, near)
@@ -306,10 +327,10 @@
 
     at = 0
     for ref, slot in ((g, CG), (c, CC), (ta, CTA)):
-        at = window(ref, cstate[slot, 4:20], CHALO, soff, sinside, at)
+        at = window(ref, cstate[slot, 4:20], CHALO, soff, at, JUMP_LINES)
     at = 0
     for ref, held, count in zip((h, jump1, jump2), (base, j1, j2), JUMPS):
-        at = window(ref, held[...].reshape(CROWS, CCH, 128), count, off, inside, at)
+        at = window(ref, held[...].reshape(CROWS, CCH, 128), count, off, at, 0)
     s[...] = g[...] + h[...]
     masks = column_masks(CCH)
     mats = restrict_mats()
@@ -320,9 +341,8 @@
 
     def spread_out(value, field, target, target_hbm, first, keep=None):
         value = value.reshape(CROWS * CCH, 128)
-        pair[pl.ds(0, CROWS * CCH, stride=2), :] = times(value, lo_mat)
-        pair[pl.ds(1, CROWS * CCH, stride=2), :] = times(value, hi_mat)
-        wide = pair[0 : CROWS * CH].reshape(CROWS, 1, CH, 128)
+        halves = [times(value, mat).reshape(CROWS, CCH, 128) for mat in (lo_mat, hi_mat)]
+        wide = jnp.concatenate(halves, axis=1).reshape(CROWS, 1, CH, 128)
         total = (field[...].reshape(CROWS, 2, CH, 128) + wide).reshape(ROWS, CH, 128)
         if keep is not None:
             total = jnp.where(m == 0, keep, total)
@@ -330,7 +350,7 @@
         copies = []
         for r in range(0, ROWS, 8):
             for k in range(CH):
-                target[r : r + 8, k * 128 : k * 128 + 128] = fine[pl.ds(r * CH + k, 8, stride=CH), :]
+                target[r : r + 8, k * 128 : k * 128 + 128] = fine[pl.ds(r * CH + line_of(k), 8, stride=CH), :]
             copy = pltpu.make_async_copy(target.at[r : r + 8], target_hbm.at[r : r + 8], sems.at[first + r // 8])
             copy.start()
             copies.append(copy)
@@ -340,7 +360,7 @@
     waits = []
     for k, jump in ((1, jump1), (2, jump2), (3, None)):
         if k == 3:
-            coarse_before = restrict(before[...].reshape(ROWS, CH, 128), pair, mats)
+            coarse_before = restrict(before[...].reshape(ROWS, CH, 128), mats)
             waits += spread_out(now_m[...] - coarse_before, before, nxt, nxt_hbm, 0,
                                 own[...].reshape(ROWS, CH, 128))
         for now, later in ((s, s2), (s2, s)):
@@ -397,57 +417,64 @@
     return lax.ppermute(x, "tm", [(i, (i + by) % devices) for i in range(devices)])
 
 
-def swapped(off, inside):
+def far_swap(x):
     devices = lax.axis_size("space")
-    far = [(i, (i + 1) % devices) for i in range(1, devices, 2)]
-    near = [(i, i + 1) for i in range(0, devices, 2)]
-    both = [pairs + [(j, i) for i, j in pairs] for pairs in (far, near)]
-    return lax.ppermute(off, "space", both[0]), lax.ppermute(inside, "space", both[1])
+    pairs = [(i, (i + 1) % devices) for i in range(1, devices, 2)]
+    return lax.ppermute(x, "space", pairs + [(j, i) for i, j in pairs])
+
+
+def near_swap(x):
+    devices = lax.axis_size("space")
+    return lax.ppermute(x, "space", [(i, i ^ 1) for i in range(devices)])
 
 
 def per_device(thickness, bed_class, ice_mask, zone_index, bed_levels, balance_rates):
     place = lax.axis_index("tm").astype(jnp.int32).reshape(1)
     space = lax.axis_index("space").astype(jnp.int32).reshape(1)
     last = jnp.full((1,), lax.axis_size("space") - 1, jnp.int32)
-    raw = (space, thickness[0], bed_class, ice_mask, zone_index, bed_levels, balance_rates)
+    raw = (space,) + tuple(
+        pltpu.with_memory_space_constraint(x, HBM)
+        for x in (thickness[0], bed_class, ice_mask, zone_index, bed_levels, balance_rates)
+    )
     coarse_lines = CROWS * CCH
     tables = [pltpu.SMEM((16,), F32), pltpu.SMEM((8,), F32)]
-    maps = [pltpu.VMEM((16, 2048), t) for t in (F32, jnp.int32, jnp.int32, jnp.int32)]
-    whole = [pltpu.VMEM((ROWS, 2048), t) for t in (F32, jnp.int32, jnp.int32, jnp.int32)]
-    off, inside = call(
-        edge_kernel, "edges", raw, [lines(EDGE_LINES)] * 2,
-        maps + tables + [(2, 8 * CH, 128)] * 4 + [pltpu.SemaphoreType.DMA((10,))],
-        "shhhhhh", limit=54,
-    )
-    off, inside = swapped(off, inside)
-    own, mid, rims, cstate, soff, sinside = call(
-        inner_kernel, "inner", raw,
-        [lines(ROWS * CH), lines(16 * CH), jax.ShapeDtypeStruct((12, 2 * RIM, CH, 128), F32)]
-        + [jax.ShapeDtypeStruct((7, 24, CCH, 128), F32)] + [lines(STATIC_LINES)] * 2,
-        whole + tables + [(ROWS * CH, 128)] * 3 + [(12, WIN, CH, 128)] + [(WIN, CH, 128)] * 2 + [(ROWS * CH, 128), pltpu.SemaphoreType.DMA((18,))],
+    maps = [jax.ShapeDtypeStruct((ROWS, CH * 128), t) for t in (F32, jnp.int32, jnp.int32, jnp.int32)]
+    maps.append(lines(24))
+    off, inside, *maps = call(
+        edge_kernel, "edges", raw, [lines(EDGE_LINES)] * 2 + maps,
+        tables + [(2, 8 * CH, 128)] * 4 + [pltpu.SemaphoreType.DMA((14,))],
         "shhhhhh",
+    )
+    off, inside = far_swap(off), near_swap(inside)
+    own, mid, rims, cstate, soff = call(
+        inner_kernel, "inner", (space, *maps),
+        [lines(ROWS * CH), lines(16 * CH), jax.ShapeDtypeStruct((len(KEPT), 2 * RIM, CH, 128), F32)]
+        + [jax.ShapeDtypeStruct((7, 24, CCH, 128), F32)] + [lines(STATIC_LINES)],
+        [(ROWS * CH, 128)] * 3 + [(12, WIN, CH, 128)] + [(WIN, CH, 128)] * 2,
+        "svvvvv",
     )
     end, prev, payload = call(
         outer_kernel, "outer", (place, space, last, off, inside, mid, rims, cstate),
         [lines(ROWS * CH)] + [lines(coarse_lines)] * 2,
-        [(12, WIN, CH, 128), (7, 24, CCH, 128)] + [(WIN, CH, 128)] * 2 + [(ROWS * CH, 128)],
+        [(12, WIN, CH, 128), (7, 24, CCH, 128)] + [(WIN, CH, 128)] * 2,
         "sssvvvvv",
     )
+    soff = far_swap(soff)
     d1, d2, d3 = (shifted(payload, k) for k in (1, 2, 3))
+    d1, d2, d3, soff = lax.optimization_barrier((d1, d2, d3, soff))
     base, j1, j2, off, inside = call(
-        gather_kernel, "gather", (place, space, d1, d2, d3),
-        [lines(coarse_lines)] * 3 + [lines(JUMP_LINES)] * 2, (), "ssvvv",
-    )
-    before = shifted(lax.optimization_barrier((end, d1, d2, d3))[0], 1)
-    soff, sinside = swapped(soff, sinside)
-    off, inside = swapped(off, inside)
+        gather_kernel, "gather", (place, space, cstate, d1, d2, d3),
+        [lines(coarse_lines)] * 3 + [lines(JUMP_LINES), lines(JUMP_LINES + STATIC_LINES)], (), "ssvvvv",
+    )
+    before = shifted(end, 1)
+    off, inside = far_swap(off), near_swap(inside)
     out, nxt = call(
         chain_kernel, "chain",
-        (place, space, last, own, cstate, end, prev, before, base, j1, j2, off, inside, soff, sinside),
+        (place, space, last, own, cstate, end, prev, before, base, j1, j2, off, inside, soff),
         [jax.ShapeDtypeStruct((ROWS, CH * 128), F32)] * 2,
-        [(CWIN, CCH, 128)] * 10 + [(CROWS, CCH, 128)] * 2 + [(ROWS * CH, 128)] * 2
+        [(CWIN, CCH, 128)] * 10 + [(CROWS, CCH, 128)] * 2 + [(ROWS * CH, 128)]
         + [(ROWS, CH * 128)] * 2 + [pltpu.SemaphoreType.DMA((8,))],
-        "sss" + "v" * 12, out_space=HBM,
+        "sss" + "v" * 11, out_space=HBM,
     )
     return out[None], nxt[None]
 

time: 43.3 us -> 34.2 us (0.79)
  local copies, waits for them, and re-layouts: 6.4 us -> 0 us
  Pallas kernels: 11 us -> 8.47 us
  starting transfers between devices: 15.3 us -> 17.1 us
  waiting for transfers between devices: 9.57 us -> 7.86 us
    unnamed x20 -> x0, local copies, waits for them, and re-layouts: 6.4 us -> none
    pallas_call x5, Pallas kernels: 11 us -> 8.47 us  [call(): pl.pallas_call(kernel, out_shape=outs, in_specs=[pl.BlockSpec(memory_spac...]
    ppermute x4, waiting for transfers between devices: 5.81 us -> 3.46 us  [shifted(): lax.ppermute(x, 'tm', [(i, (i + by) % devices) for i in range(devices)])]
    ppermute x4, starting transfers between devices: 5.37 us -> 7.68 us  [shifted(): lax.ppermute(x, 'tm', [(i, (i + by) % devices) for i in range(devices)])]
    ppermute x6 -> x5, waiting for transfers between devices: 3.76 us -> 4.4 us  [the longest x3 4.4 us: far_swap(): return lax.ppermute(x, 'space', pairs + [(j, i) for i, j in pairs])]
    ppermute x6 -> x5, starting transfers between devices: 9.95 us -> 9.43 us  [the longest x3 9.34 us: far_swap(): return lax.ppermute(x, 'space', pairs + [(j, i) for i, j in pairs])]
  transfers between devices with their start and end apart: 10 -> 9, of which waited for: 6 -> 4; matrix products, arithmetic and copies ran while one was open for 0% -> 0% of each run, Pallas kernels for 10% -> 12%
where the time goes in v2:
time: 34.2 us; the launch traced here: 34.1 us
  starting transfers between devices  17.1 us (50%)
  Pallas kernels  8.47 us (25%)
  waiting for transfers between devices  7.86 us (23%)
  between operations  0.68 us (2%)
    ppermute x3, starting transfers between devices, far_swap(): return lax.ppermute(x, 'space', pairs + [(j, i) for i, j in pairs])  9.34 us
    pallas_call x5, Pallas kernels, call(): pl.pallas_call(kernel, out_shape=outs, in_specs=[pl.BlockSpec(memory_spac...  8.47 us
    ppermute x4, starting transfers between devices, shifted(): lax.ppermute(x, 'tm', [(i, (i + by) % devices) for i in range(devices)])  7.68 us
    ppermute x3, waiting for transfers between devices, far_swap(): return lax.ppermute(x, 'space', pairs + [(j, i) for i, j in pairs])  4.4 us
    ppermute x4, waiting for transfers between devices, shifted(): lax.ppermute(x, 'tm', [(i, (i + by) % devices) for i in range(devices)])  3.46 us
  transfers between devices with their start and end apart: 9, of which 4 were waited for; matrix products, arithmetic and copies ran while one was open for 0% of the time, Pallas kernels for 12%

profile of v2, /device:TPU:0, one launch (start us, length us, event | category | flops | bytes accessed | tf_op | source)
XLA Modules:
  0.0 34.1 jit_solution(2234911332651525103)
XLA Ops:
  0.6 1.5 %edges.1 = (f32[448,128]{1,0:T(8,128)S(1)}, f32[448,128]{1,0:T(8,128)S(1)}, f32[32,2048]{1,0:T(8,128)S(1)}, s32[32,2048]{1,0:T(8,128)S(1)}, s32[32,2048]{1,0:T(8...) custom-call(s32[1]{0:T(128)} %bitcast.1.space, f32[32,2048]{1,0:T(8,128)} %bitcast.5, s32[32,2048]{1,0:T(8,128)} %bed.1, ...), custom_call_target="tpu_custom_call" | custom-call | tf_op jit(solution)/shard_map/edges/pallas_call | solution.py:404
  2.1 4.8 %collective-permute-start = (f32[448,128]{1,0:T(8,128)S(1)}, f32[448,128]{1,0:T(8,128)S(1)}, u32[]{:S(2)}, u32[]{:S(2)}) collective-permute-start(f32[448,128]{1,0:T(8,128)S(1)} %get-tuple-element.35), channel_id=1, source_target_pairs={{1,2},{3,4},{5,6},{7,8},{9,10},{11,12},{13,14},{15,16},{17,18},{19... | collective-permute-start | bytes 688136 | tf_op jit(solution)/shard_map/ppermute | solution.py:423
  6.9 0.0 collective-permute-start.1
  6.9 2.5 %inner.1 = (f32[512,128]{1,0:T(8,128)S(1)}, f32[256,128]{1,0:T(8,128)S(1)}, f32[8,20,16,128]{3,2,1,0:T(8,128)S(1)}, f32[7,24,8,128]{3,2,1,0:T(8,128)S(1)}, f32[288,128]{1,0:T(8,128)}) custom-call(s32[1]{0:T(128)} %bitcast.1.space, f32[32,2048]{1,0:T(8,128)S(1)} %get-tuple-element.28.tv, s32[32,2048]{1,0:T(8,128)S(1)} %get-tuple-element.29.bv, ...), custom_call_target="tpu_custom_call" | custom-call | tf_op jit(solution)/shard_map/inner/pallas_call | solution.py:404
  9.5 0.9 %collective-permute-start.6 = (f32[288,128]{1,0:T(8,128)}, f32[288,128]{1,0:T(8,128)S(1)}, u32[]{:S(2)}, u32[]{:S(2)}) collective-permute-start(f32[288,128]{1,0:T(8,128)} %get-tuple-element.42), channel_id=1, source_target_pairs={{1,2},{3,4},{5,6},{7,8},{9,10},{11,12},{13,14},{15,16},{17,18},{19... | collective-permute-start | bytes 442376 | tf_op jit(solution)/shard_map/ppermute | solution.py:423
  10.4 0.5 %collective-permute-done.off = f32[448,128]{1,0:T(8,128)S(1)} collective-permute-done((f32[448,128]{1,0:T(8,128)S(1)}, f32[448,128]{1,0:T(8,128)S(1)}, u32[]{:S(2)}, u32[]{:S(2)}) %collective-permute-start) | collective-permute-done | bytes 229408 | tf_op jit(solution)/shard_map/ppermute | solution.py:423
  11.0 0.0 collective-permute-done.1.inside
  11.0 1.7 %outer.1 = (f32[512,128]{1,0:T(8,128)S(1)}, f32[128,128]{1,0:T(8,128)S(1)}, f32[128,128]{1,0:T(8,128)S(1)}) custom-call(s32[1]{0:T(128)} %bitcast.place, s32[1]{0:T(128)} %bitcast.1.space, s32[1]{0:T(128)} %constant.10.clone.1.last, f32[448,128]{1,0:T(8,128)S(1)} %collective-permute-done.off, f32[448,128]{1,0:T(8,128)S(1)} %collective-permute-done.1.inside, ...), custom_call_target="tpu_custom_call" | custom-call | tf_op jit(solution)/shard_map/outer/pallas_call | solution.py:404
  12.7 4.2 %collective-permute-start.5 = (f32[128,128]{1,0:T(8,128)S(1)}, f32[128,128]{1,0:T(8,128)S(1)}, u32[]{:S(2)}, u32[]{:S(2)}) collective-permute-start(f32[128,128]{1,0:T(8,128)S(1)} %get-tuple-element.41), channel_id=1, source_target_pairs={{0,96},{32,0},{64,32},{96,64},{1,97},{33,1},{65,33},{97,65},{2,98}... | collective-permute-start | bytes 196616 | tf_op jit(solution)/shard_map/ppermute | solution.py:417
  16.9 0.0 collective-permute-start.4
  16.9 1.3 %collective-permute-start.3 = (f32[128,128]{1,0:T(8,128)S(1)}, f32[128,128]{1,0:T(8,128)S(1)}, u32[]{:S(2)}, u32[]{:S(2)}) collective-permute-start(f32[128,128]{1,0:T(8,128)S(1)} %get-tuple-element.41), channel_id=1, source_target_pairs={{0,32},{32,64},{64,96},{96,0},{1,33},{33,65},{65,97},{97,1},{2,34}... | collective-permute-start | bytes 196616 | tf_op jit(solution)/shard_map/ppermute | solution.py:417
  18.1 2.2 %collective-permute-start.2 = (f32[512,128]{1,0:T(8,128)S(1)}, f32[512,128]{1,0:T(8,128)S(1)}, u32[]{:S(2)}, u32[]{:S(2)}) collective-permute-start(f32[512,128]{1,0:T(8,128)S(1)} %get-tuple-element.39.end), channel_id=1, source_target_pairs={{0,32},{32,64},{64,96},{96,0},{1,33},{33,65},{65,97},{97,1},{2,34}... | collective-permute-start | bytes 786440 | tf_op jit(solution)/shard_map/ppermute | solution.py:417
  20.3 0.0 collective-permute-done.6.soff
  20.3 0.0 collective-permute-done.5.d3
  20.3 3.0 %collective-permute-done.4.d2 = f32[128,128]{1,0:T(8,128)S(1)} collective-permute-done((f32[128,128]{1,0:T(8,128)S(1)}, f32[128,128]{1,0:T(8,128)S(1)}, u32[]{:S(2)}, u32[]{:S(2)}) %collective-permute-start.4) | collective-permute-done | bytes 65568 | tf_op jit(solution)/shard_map/ppermute | solution.py:417
  23.4 0.4 %collective-permute-done.3.d1 = f32[128,128]{1,0:T(8,128)S(1)} collective-permute-done((f32[128,128]{1,0:T(8,128)S(1)}, f32[128,128]{1,0:T(8,128)S(1)}, u32[]{:S(2)}, u32[]{:S(2)}) %collective-permute-start.3) | collective-permute-done | bytes 65568 | tf_op jit(solution)/shard_map/ppermute | solution.py:417
  23.8 0.1 collective-permute-start.8
  23.9 3.6 %collective-permute-start.7 = (f32[192,128]{1,0:T(8,128)S(1)}, f32[192,128]{1,0:T(8,128)S(1)}, u32[]{:S(2)}, u32[]{:S(2)}) collective-permute-start(f32[192,128]{1,0:T(8,128)S(1)} %get-tuple-element.49), channel_id=1, source_target_pairs={{1,2},{3,4},{5,6},{7,8},{9,10},{11,12},{13,14},{15,16},{17,18},{19... | collective-permute-start | bytes 294920 | tf_op jit(solution)/shard_map/ppermute | solution.py:423
  27.5 3.8 %collective-permute-done.7.off = f32[192,128]{1,0:T(8,128)S(1)} collective-permute-done((f32[192,128]{1,0:T(8,128)S(1)}, f32[192,128]{1,0:T(8,128)S(1)}, u32[]{:S(2)}, u32[]{:S(2)}) %collective-permute-start.7) | collective-permute-done | bytes 98336 | tf_op jit(solution)/shard_map/ppermute | solution.py:423
  31.4 0.0 collective-permute-done.2.before
  31.4 0.0 collective-permute-done.8.inside
  31.4 2.7 %chain.1 = (f32[32,2048]{1,0:T(8,128)}, f32[32,2048]{1,0:T(8,128)}) custom-call(s32[1]{0:T(128)} %bitcast.place, s32[1]{0:T(128)} %bitcast.1.space, s32[1]{0:T(128)} %constant.10.clone.1.last, f32[512,128]{1,0:T(8,128)S(1)} %get-tuple-element.33.own, f32[7,24,8,128]{3,2,1,0:T(8,128)S(1)} %get-tuple-element.34.cstate_in.cstate, ...), custom_call_target="tpu_custom_call" | custom-call | tf_op jit(solution)/shard_map/chain/pallas_call | solution.py:404
  (1 shorter events, 0.0 us)
Async XLA Ops:
  2.1 8.8 %collective-permute-start = (f32[448,128]{1,0:T(8,128)S(1)}, f32[448,128]{1,0:T(8,128)S(1)}, u32[]{:S(2)}, u32[]{:S(2)}) collective-permute-start(f32[448,128]{1,0:T(8,128)S(1)} %get-tuple-element.35), channel_id=1, source_target_pairs={{1,2},{3,4},{5,6},{7,8},{9,10},{11,12},{13,14},{15,16},{17,18},{19... | collective-permute-start | bytes 688136 | tf_op jit(solution)/shard_map/ppermute | solution.py:423
  6.9 4.0 %collective-permute-start.1 = (f32[448,128]{1,0:T(8,128)S(1)}, f32[448,128]{1,0:T(8,128)S(1)}, u32[]{:S(2)}, u32[]{:S(2)}) collective-permute-start(f32[448,128]{1,0:T(8,128)S(1)} %get-tuple-element.36), channel_id=1, source_target_pairs={{0,1},{1,0},{2,3},{3,2},{4,5},{5,4},{6,7},{7,6},{8,9},{9,8},{10,11... | collective-permute-start | bytes 688136 | tf_op jit(solution)/shard_map/ppermute | solution.py:428
  9.5 10.9 %collective-permute-start.6 = (f32[288,128]{1,0:T(8,128)}, f32[288,128]{1,0:T(8,128)S(1)}, u32[]{:S(2)}, u32[]{:S(2)}) collective-permute-start(f32[288,128]{1,0:T(8,128)} %get-tuple-element.42), channel_id=1, source_target_pairs={{1,2},{3,4},{5,6},{7,8},{9,10},{11,12},{13,14},{15,16},{17,18},{19... | collective-permute-start | bytes 442376 | tf_op jit(solution)/shard_map/ppermute | solution.py:423
  12.7 7.7 %collective-permute-start.5 = (f32[128,128]{1,0:T(8,128)S(1)}, f32[128,128]{1,0:T(8,128)S(1)}, u32[]{:S(2)}, u32[]{:S(2)}) collective-permute-start(f32[128,128]{1,0:T(8,128)S(1)} %get-tuple-element.41), channel_id=1, source_target_pairs={{0,96},{32,0},{64,32},{96,64},{1,97},{33,1},{65,33},{97,65},{2,98}... | collective-permute-start | bytes 196616 | tf_op jit(solution)/shard_map/ppermute | solution.py:417
  16.9 6.5 %collective-permute-start.4 = (f32[128,128]{1,0:T(8,128)S(1)}, f32[128,128]{1,0:T(8,128)S(1)}, u32[]{:S(2)}, u32[]{:S(2)}) collective-permute-start(f32[128,128]{1,0:T(8,128)S(1)} %get-tuple-element.41), channel_id=1, source_target_pairs={{0,64},{32,96},{64,0},{96,32},{1,65},{33,97},{65,1},{97,33},{2,66}... | collective-permute-start | bytes 196616 | tf_op jit(solution)/shard_map/ppermute | solution.py:417
  16.9 6.9 %collective-permute-start.3 = (f32[128,128]{1,0:T(8,128)S(1)}, f32[128,128]{1,0:T(8,128)S(1)}, u32[]{:S(2)}, u32[]{:S(2)}) collective-permute-start(f32[128,128]{1,0:T(8,128)S(1)} %get-tuple-element.41), channel_id=1, source_target_pairs={{0,32},{32,64},{64,96},{96,0},{1,33},{33,65},{65,97},{97,1},{2,34}... | collective-permute-start | bytes 196616 | tf_op jit(solution)/shard_map/ppermute | solution.py:417
  18.1 13.3 %collective-permute-start.2 = (f32[512,128]{1,0:T(8,128)S(1)}, f32[512,128]{1,0:T(8,128)S(1)}, u32[]{:S(2)}, u32[]{:S(2)}) collective-permute-start(f32[512,128]{1,0:T(8,128)S(1)} %get-tuple-element.39.end), channel_id=1, source_target_pairs={{0,32},{32,64},{64,96},{96,0},{1,33},{33,65},{65,97},{97,1},{2,34}... | collective-permute-start | bytes 786440 | tf_op jit(solution)/shard_map/ppermute | solution.py:417
  23.8 7.5 %collective-permute-start.8 = (f32[480,128]{1,0:T(8,128)S(1)}, f32[480,128]{1,0:T(8,128)S(1)}, u32[]{:S(2)}, u32[]{:S(2)}) collective-permute-start(f32[480,128]{1,0:T(8,128)S(1)} %get-tuple-element.50), channel_id=1, source_target_pairs={{0,1},{1,0},{2,3},{3,2},{4,5},{5,4},{6,7},{7,6},{8,9},{9,8},{10,11... | collective-permute-start | bytes 737288 | tf_op jit(solution)/shard_map/ppermute | solution.py:428
  23.9 7.4 %collective-permute-start.7 = (f32[192,128]{1,0:T(8,128)S(1)}, f32[192,128]{1,0:T(8,128)S(1)}, u32[]{:S(2)}, u32[]{:S(2)}) collective-permute-start(f32[192,128]{1,0:T(8,128)S(1)} %get-tuple-element.49), channel_id=1, source_target_pairs={{1,2},{3,4},{5,6},{7,8},{9,10},{11,12},{13,14},{15,16},{17,18},{19... | collective-permute-start | bytes 294920 | tf_op jit(solution)/shard_map/ppermute | solution.py:423

commit v3 on v2

--- a/solution.py
+++ b/solution.py
@@ -176,6 +176,7 @@
         off[at : at + n] = ref[odd, pl.ds(odd * skip, n)]
         inside[at : at + n] = ref[1 - odd, pl.ds((1 - odd) * skip, n)]
         at += n
+    inside[at : at + 8] = jnp.zeros((8, 128), F32)
     for copy in copies[10:]:
         copy.wait()
 
@@ -325,18 +326,21 @@
         ref[bottom : bottom + count] = jnp.where(odd == 1, far, near)
         return at + n
 
-    at = 0
-    for ref, slot in ((g, CG), (c, CC), (ta, CTA)):
-        at = window(ref, cstate[slot, 4:20], CHALO, soff, at, JUMP_LINES)
-    at = 0
-    for ref, held, count in zip((h, jump1, jump2), (base, j1, j2), JUMPS):
-        at = window(ref, held[...].reshape(CROWS, CCH, 128), count, off, at, 0)
-    s[...] = g[...] + h[...]
+    @pl.when(m > 0)
+    def _():
+        at = 0
+        for ref, slot in ((g, CG), (c, CC), (ta, CTA)):
+            at = window(ref, cstate[slot, 4:20], CHALO, soff, at, JUMP_LINES)
+        at = 0
+        for ref, held, count in zip((h, jump1, jump2), (base, j1, j2), JUMPS):
+            at = window(ref, held[...].reshape(CROWS, CCH, 128), count, off, at, 0)
+        s[...] = g[...] + h[...]
+        now_m[...] = h[CHALO:bottom]
+
     masks = column_masks(CCH)
     mats = restrict_mats()
     mine = slice(CHALO, bottom)
     fix[...] = jnp.zeros_like(fix)
-    now_m[...] = h[mine]
     lo_mat, hi_mat = prolong_mats()
 
     def spread_out(value, field, target, target_hbm, first, keep=None):
@@ -363,29 +367,35 @@
             coarse_before = restrict(before[...].reshape(ROWS, CH, 128), mats)
             waits += spread_out(now_m[...] - coarse_before, before, nxt, nxt_hbm, 0,
                                 own[...].reshape(ROWS, CH, 128))
-        for now, later in ((s, s2), (s2, s)):
-            edge += 2
-
-            def emit(a, b, value, later=later):
-                h[a:b] = value
-                later[a:b] = value + g[a:b]
-
-            flow(h, now, g, c, ta, d, dy, edge, CWIN - edge, masks, COARSE_GAIN, COARSE_CAP, 8, emit)
-
-        @pl.when(m == k)
-        def _():
-            fix[...] = h[mine] - prev[...].reshape(CROWS, CCH, 128)
-
-        if jump is not None:
-            for a in range(edge, CWIN - edge, 8):
-                b = min(a + 8, CWIN - edge)
-                emit_value = h[a:b] + jump[a:b]
-                h[a:b] = emit_value
-                s[a:b] = emit_value + g[a:b]
-
-            @pl.when(m == k + 1)
+        first_edge = edge
+        edge += 4
+
+        @pl.when(m >= k)
+        def _(k=k, jump=jump, first_edge=first_edge):
+            for step, (now, later) in enumerate(((s, s2), (s2, s))):
+                lo = first_edge + 2 * (step + 1)
+
+                def emit(a, b, value, later=later):
+                    h[a:b] = value
+                    later[a:b] = value + g[a:b]
+
+                flow(h, now, g, c, ta, d, dy, lo, CWIN - lo, masks, COARSE_GAIN, COARSE_CAP, 8, emit)
+
+            @pl.when(m == k)
             def _():
-                now_m[...] = h[mine]
+                fix[...] = h[mine] - prev[...].reshape(CROWS, CCH, 128)
+
+            if jump is not None:
+                lo = first_edge + 4
+                for a in range(lo, CWIN - lo, 8):
+                    b = min(a + 8, CWIN - lo)
+                    value = h[a:b] + jump[a:b]
+                    h[a:b] = value
+                    s[a:b] = value + g[a:b]
+
+                @pl.when(m == k + 1)
+                def _():
+                    now_m[...] = h[mine]
 
     waits += spread_out(fix[...], end, out, out_hbm, 4)
     for copy in waits:
@@ -441,7 +451,7 @@
     maps = [jax.ShapeDtypeStruct((ROWS, CH * 128), t) for t in (F32, jnp.int32, jnp.int32, jnp.int32)]
     maps.append(lines(24))
     off, inside, *maps = call(
-        edge_kernel, "edges", raw, [lines(EDGE_LINES)] * 2 + maps,
+        edge_kernel, "edges", raw, [lines(EDGE_LINES), lines(EDGE_LINES + 8)] + maps,
         tables + [(2, 8 * CH, 128)] * 4 + [pltpu.SemaphoreType.DMA((14,))],
         "shhhhhh",
     )

time: 34.2 us -> 32.6 us (0.953)
  waiting for transfers between devices: 7.86 us -> 6.41 us
  Pallas kernels: 8.47 us -> 7.29 us
  starting transfers between devices: 17.1 us -> 18 us
    pallas_call x5, Pallas kernels: 8.47 us -> 7.29 us  [call(): pl.pallas_call(kernel, out_shape=outs, in_specs=[pl.BlockSpec(memory_spac...]
    ppermute x3, starting transfers between devices: 9.34 us -> 10.3 us  [far_swap(): return lax.ppermute(x, 'space', pairs + [(j, i) for i, j in pairs])]
    ppermute x4, waiting for transfers between devices: 3.46 us -> 2.69 us  [shifted(): lax.ppermute(x, 'tm', [(i, (i + by) % devices) for i in range(devices)])]
    ppermute x3, waiting for transfers between devices: 4.4 us -> 3.72 us  [far_swap(): return lax.ppermute(x, 'space', pairs + [(j, i) for i, j in pairs])]
  transfers between devices with their start and end apart: 9 -> 9, of which waited for: 4 -> 4; matrix products, arithmetic and copies ran while one was open for 0% -> 0% of each run, Pallas kernels for 12% -> 13%
where the time goes in v3:
time: 32.6 us; the launch traced here: 32.4 us
  starting transfers between devices  18 us (55%)
  Pallas kernels  7.29 us (22%)
  waiting for transfers between devices  6.41 us (20%)
  between operations  0.7 us (2%)
    ppermute x3, starting transfers between devices, far_swap(): return lax.ppermute(x, 'space', pairs + [(j, i) for i, j in pairs])  10.3 us
    ppermute x4, starting transfers between devices, shifted(): lax.ppermute(x, 'tm', [(i, (i + by) % devices) for i in range(devices)])  7.59 us
    pallas_call x5, Pallas kernels, call(): pl.pallas_call(kernel, out_shape=outs, in_specs=[pl.BlockSpec(memory_spac...  7.29 us
    ppermute x3, waiting for transfers between devices, far_swap(): return lax.ppermute(x, 'space', pairs + [(j, i) for i, j in pairs])  3.72 us
    ppermute x4, waiting for transfers between devices, shifted(): lax.ppermute(x, 'tm', [(i, (i + by) % devices) for i in range(devices)])  2.69 us
  transfers between devices with their start and end apart: 9, of which 4 were waited for; matrix products, arithmetic and copies ran while one was open for 0% of the time, Pallas kernels for 13%

profile of v3, /device:TPU:0, one launch (start us, length us, event | category | flops | bytes accessed | tf_op | source)
XLA Modules:
  0.0 32.4 jit_solution(15756634432310307946)
XLA Ops:
  0.6 1.5 %edges.1 = (f32[448,128]{1,0:T(8,128)S(1)}, f32[456,128]{1,0:T(8,128)S(1)}, f32[32,2048]{1,0:T(8,128)S(1)}, s32[32,2048]{1,0:T(8,128)S(1)}, s32[32,2048]{1,0:T(8...) custom-call(s32[1]{0:T(128)} %bitcast.1.space, f32[32,2048]{1,0:T(8,128)} %bitcast.5, s32[32,2048]{1,0:T(8,128)} %bed.1, ...), custom_call_target="tpu_custom_call" | custom-call | tf_op jit(solution)/shard_map/edges/pallas_call | solution.py:414
  2.1 0.1 collective-permute-start.1
  2.2 5.4 %collective-permute-start = (f32[448,128]{1,0:T(8,128)S(1)}, f32[448,128]{1,0:T(8,128)S(1)}, u32[]{:S(2)}, u32[]{:S(2)}) collective-permute-start(f32[448,128]{1,0:T(8,128)S(1)} %get-tuple-element.35), channel_id=1, source_target_pairs={{1,2},{3,4},{5,6},{7,8},{9,10},{11,12},{13,14},{15,16},{17,18},{19... | collective-permute-start | bytes 688136 | tf_op jit(solution)/shard_map/ppermute | solution.py:433
  7.6 2.5 %inner.1 = (f32[512,128]{1,0:T(8,128)S(1)}, f32[256,128]{1,0:T(8,128)S(1)}, f32[8,20,16,128]{3,2,1,0:T(8,128)S(1)}, f32[7,24,8,128]{3,2,1,0:T(8,128)S(1)}, f32[288,128]{1,0:T(8,128)}) custom-call(s32[1]{0:T(128)} %bitcast.1.space, f32[32,2048]{1,0:T(8,128)S(1)} %get-tuple-element.28.tv, s32[32,2048]{1,0:T(8,128)S(1)} %get-tuple-element.29.bv, ...), custom_call_target="tpu_custom_call" | custom-call | tf_op jit(solution)/shard_map/inner/pallas_call | solution.py:414
  10.2 0.1 collective-permute-start.6
  10.3 1.1 %collective-permute-done.off = f32[448,128]{1,0:T(8,128)S(1)} collective-permute-done((f32[448,128]{1,0:T(8,128)S(1)}, f32[448,128]{1,0:T(8,128)S(1)}, u32[]{:S(2)}, u32[]{:S(2)}) %collective-permute-start) | collective-permute-done | bytes 229408 | tf_op jit(solution)/shard_map/ppermute | solution.py:433
  11.3 0.0 collective-permute-done.1.inside
  11.3 1.7 %outer.1 = (f32[512,128]{1,0:T(8,128)S(1)}, f32[128,128]{1,0:T(8,128)S(1)}, f32[128,128]{1,0:T(8,128)S(1)}) custom-call(s32[1]{0:T(128)} %bitcast.place, s32[1]{0:T(128)} %bitcast.1.space, s32[1]{0:T(128)} %constant.10.clone.1.last, f32[448,128]{1,0:T(8,128)S(1)} %collective-permute-done.off, f32[456,128]{1,0:T(8,128)S(1)} %collective-permute-done.1.inside, ...), custom_call_target="tpu_custom_call" | custom-call | tf_op jit(solution)/shard_map/outer/pallas_call | solution.py:414
  13.0 4.1 %collective-permute-start.5 = (f32[128,128]{1,0:T(8,128)S(1)}, f32[128,128]{1,0:T(8,128)S(1)}, u32[]{:S(2)}, u32[]{:S(2)}) collective-permute-start(f32[128,128]{1,0:T(8,128)S(1)} %get-tuple-element.41), channel_id=1, source_target_pairs={{0,96},{32,0},{64,32},{96,64},{1,97},{33,1},{65,33},{97,65},{2,98}... | collective-permute-start | bytes 196616 | tf_op jit(solution)/shard_map/ppermute | solution.py:427
  17.1 0.0 collective-permute-start.4
  17.1 1.3 %collective-permute-start.3 = (f32[128,128]{1,0:T(8,128)S(1)}, f32[128,128]{1,0:T(8,128)S(1)}, u32[]{:S(2)}, u32[]{:S(2)}) collective-permute-start(f32[128,128]{1,0:T(8,128)S(1)} %get-tuple-element.41), channel_id=1, source_target_pairs={{0,32},{32,64},{64,96},{96,0},{1,33},{33,65},{65,97},{97,1},{2,34}... | collective-permute-start | bytes 196616 | tf_op jit(solution)/shard_map/ppermute | solution.py:427
  18.4 2.2 %collective-permute-start.2 = (f32[512,128]{1,0:T(8,128)S(1)}, f32[512,128]{1,0:T(8,128)S(1)}, u32[]{:S(2)}, u32[]{:S(2)}) collective-permute-start(f32[512,128]{1,0:T(8,128)S(1)} %get-tuple-element.39.end), channel_id=1, source_target_pairs={{0,32},{32,64},{64,96},{96,0},{1,33},{33,65},{65,97},{97,1},{2,34}... | collective-permute-start | bytes 786440 | tf_op jit(solution)/shard_map/ppermute | solution.py:427
  20.6 0.0 collective-permute-done.6.soff
  20.6 0.0 collective-permute-done.5.d3
  20.6 2.4 %collective-permute-done.4.d2 = f32[128,128]{1,0:T(8,128)S(1)} collective-permute-done((f32[128,128]{1,0:T(8,128)S(1)}, f32[128,128]{1,0:T(8,128)S(1)}, u32[]{:S(2)}, u32[]{:S(2)}) %collective-permute-start.4) | collective-permute-done | bytes 65568 | tf_op jit(solution)/shard_map/ppermute | solution.py:427
  23.0 0.3 collective-permute-done.3.d1
  23.3 0.1 collective-permute-start.8
  23.4 4.8 %collective-permute-start.7 = (f32[192,128]{1,0:T(8,128)S(1)}, f32[192,128]{1,0:T(8,128)S(1)}, u32[]{:S(2)}, u32[]{:S(2)}) collective-permute-start(f32[192,128]{1,0:T(8,128)S(1)} %get-tuple-element.49), channel_id=1, source_target_pairs={{1,2},{3,4},{5,6},{7,8},{9,10},{11,12},{13,14},{15,16},{17,18},{19... | collective-permute-start | bytes 294920 | tf_op jit(solution)/shard_map/ppermute | solution.py:433
  28.2 2.7 %collective-permute-done.7.off = f32[192,128]{1,0:T(8,128)S(1)} collective-permute-done((f32[192,128]{1,0:T(8,128)S(1)}, f32[192,128]{1,0:T(8,128)S(1)}, u32[]{:S(2)}, u32[]{:S(2)}) %collective-permute-start.7) | collective-permute-done | bytes 98336 | tf_op jit(solution)/shard_map/ppermute | solution.py:433
  30.9 0.0 collective-permute-done.2.before
  30.9 0.0 collective-permute-done.8.inside
  30.9 1.5 %chain.1 = (f32[32,2048]{1,0:T(8,128)}, f32[32,2048]{1,0:T(8,128)}) custom-call(s32[1]{0:T(128)} %bitcast.place, s32[1]{0:T(128)} %bitcast.1.space, s32[1]{0:T(128)} %constant.10.clone.1.last, f32[512,128]{1,0:T(8,128)S(1)} %get-tuple-element.33.own, f32[7,24,8,128]{3,2,1,0:T(8,128)S(1)} %get-tuple-element.34.cstate_in.cstate, ...), custom_call_target="tpu_custom_call" | custom-call | tf_op jit(solution)/shard_map/chain/pallas_call | solution.py:414
  (1 shorter events, 0.0 us)
Async XLA Ops:
  2.1 9.2 %collective-permute-start.1 = (f32[456,128]{1,0:T(8,128)S(1)}, f32[456,128]{1,0:T(8,128)S(1)}, u32[]{:S(2)}, u32[]{:S(2)}) collective-permute-start(f32[456,128]{1,0:T(8,128)S(1)} %get-tuple-element.36), channel_id=1, source_target_pairs={{0,1},{1,0},{2,3},{3,2},{4,5},{5,4},{6,7},{7,6},{8,9},{9,8},{10,11... | collective-permute-start | bytes 700424 | tf_op jit(solution)/shard_map/ppermute | solution.py:438
  2.2 9.1 %collective-permute-start = (f32[448,128]{1,0:T(8,128)S(1)}, f32[448,128]{1,0:T(8,128)S(1)}, u32[]{:S(2)}, u32[]{:S(2)}) collective-permute-start(f32[448,128]{1,0:T(8,128)S(1)} %get-tuple-element.35), channel_id=1, source_target_pairs={{1,2},{3,4},{5,6},{7,8},{9,10},{11,12},{13,14},{15,16},{17,18},{19... | collective-permute-start | bytes 688136 | tf_op jit(solution)/shard_map/ppermute | solution.py:433
  10.2 10.4 %collective-permute-start.6 = (f32[288,128]{1,0:T(8,128)}, f32[288,128]{1,0:T(8,128)S(1)}, u32[]{:S(2)}, u32[]{:S(2)}) collective-permute-start(f32[288,128]{1,0:T(8,128)} %get-tuple-element.42), channel_id=1, source_target_pairs={{1,2},{3,4},{5,6},{7,8},{9,10},{11,12},{13,14},{15,16},{17,18},{19... | collective-permute-start | bytes 442376 | tf_op jit(solution)/shard_map/ppermute | solution.py:433
  13.0 7.6 %collective-permute-start.5 = (f32[128,128]{1,0:T(8,128)S(1)}, f32[128,128]{1,0:T(8,128)S(1)}, u32[]{:S(2)}, u32[]{:S(2)}) collective-permute-start(f32[128,128]{1,0:T(8,128)S(1)} %get-tuple-element.41), channel_id=1, source_target_pairs={{0,96},{32,0},{64,32},{96,64},{1,97},{33,1},{65,33},{97,65},{2,98}... | collective-permute-start | bytes 196616 | tf_op jit(solution)/shard_map/ppermute | solution.py:427
  17.1 5.9 %collective-permute-start.4 = (f32[128,128]{1,0:T(8,128)S(1)}, f32[128,128]{1,0:T(8,128)S(1)}, u32[]{:S(2)}, u32[]{:S(2)}) collective-permute-start(f32[128,128]{1,0:T(8,128)S(1)} %get-tuple-element.41), channel_id=1, source_target_pairs={{0,64},{32,96},{64,0},{96,32},{1,65},{33,97},{65,1},{97,33},{2,66}... | collective-permute-start | bytes 196616 | tf_op jit(solution)/shard_map/ppermute | solution.py:427
  17.1 6.2 %collective-permute-start.3 = (f32[128,128]{1,0:T(8,128)S(1)}, f32[128,128]{1,0:T(8,128)S(1)}, u32[]{:S(2)}, u32[]{:S(2)}) collective-permute-start(f32[128,128]{1,0:T(8,128)S(1)} %get-tuple-element.41), channel_id=1, source_target_pairs={{0,32},{32,64},{64,96},{96,0},{1,33},{33,65},{65,97},{97,1},{2,34}... | collective-permute-start | bytes 196616 | tf_op jit(solution)/shard_map/ppermute | solution.py:427
  18.4 12.5 %collective-permute-start.2 = (f32[512,128]{1,0:T(8,128)S(1)}, f32[512,128]{1,0:T(8,128)S(1)}, u32[]{:S(2)}, u32[]{:S(2)}) collective-permute-start(f32[512,128]{1,0:T(8,128)S(1)} %get-tuple-element.39.end), channel_id=1, source_target_pairs={{0,32},{32,64},{64,96},{96,0},{1,33},{33,65},{65,97},{97,1},{2,34}... | collective-permute-start | bytes 786440 | tf_op jit(solution)/shard_map/ppermute | solution.py:427
  23.3 7.5 %collective-permute-start.8 = (f32[480,128]{1,0:T(8,128)S(1)}, f32[480,128]{1,0:T(8,128)S(1)}, u32[]{:S(2)}, u32[]{:S(2)}) collective-permute-start(f32[480,128]{1,0:T(8,128)S(1)} %get-tuple-element.50), channel_id=1, source_target_pairs={{0,1},{1,0},{2,3},{3,2},{4,5},{5,4},{6,7},{7,6},{8,9},{9,8},{10,11... | collective-permute-start | bytes 737288 | tf_op jit(solution)/shard_map/ppermute | solution.py:438
  23.4 7.4 %collective-permute-start.7 = (f32[192,128]{1,0:T(8,128)S(1)}, f32[192,128]{1,0:T(8,128)S(1)}, u32[]{:S(2)}, u32[]{:S(2)}) collective-permute-start(f32[192,128]{1,0:T(8,128)S(1)} %get-tuple-element.49), channel_id=1, source_target_pairs={{1,2},{3,4},{5,6},{7,8},{9,10},{11,12},{13,14},{15,16},{17,18},{19... | collective-permute-start | bytes 294920 | tf_op jit(solution)/shard_map/ppermute | solution.py:433

commit v4 on v3

--- a/solution.py
+++ b/solution.py
@@ -428,9 +428,10 @@
 
 
 def far_swap(x):
-    devices = lax.axis_size("space")
-    pairs = [(i, (i + 1) % devices) for i in range(1, devices, 2)]
-    return lax.ppermute(x, "space", pairs + [(j, i) for i, j in pairs])
+    slices, devices = lax.axis_size("tm"), lax.axis_size("space")
+    pairs = [(m * devices + i, m * devices + i + 1) for m in range(slices) for i in range(1, devices - 1, 2)]
+    pairs += [(m * devices + i, (m + 1) * devices + i) for m in range(0, slices, 2) for i in (0, devices - 1)]
+    return lax.ppermute(x, ("tm", "space"), pairs + [(j, i) for i, j in pairs])
 
 
 def near_swap(x):

time: 32.6 us -> 30.7 us (0.942)
  the two profiles are of different devices: /device:TPU:0 before, /device:TPU:2 now
where the time goes in v4:
time: 30.7 us; the launch traced here: 30.5 us
  starting transfers between devices  13.7 us (45%)
  waiting for transfers between devices  8.84 us (29%)
  Pallas kernels  7.3 us (24%)
  between operations  0.69 us (2%)
    ppermute x4, starting transfers between devices, shifted(): lax.ppermute(x, 'tm', [(i, (i + by) % devices) for i in range(devices)])  7.59 us
    pallas_call x5, Pallas kernels, call(): pl.pallas_call(kernel, out_shape=outs, in_specs=[pl.BlockSpec(memory_spac...  7.3 us
    ppermute x3, starting transfers between devices, far_swap(): return lax.ppermute(x, ('tm', 'space'), pairs + [(j, i) for i, j in pairs])  5.94 us
    ppermute x3, waiting for transfers between devices, far_swap(): return lax.ppermute(x, ('tm', 'space'), pairs + [(j, i) for i, j in pairs])  5.38 us
    ppermute x4, waiting for transfers between devices, shifted(): lax.ppermute(x, 'tm', [(i, (i + by) % devices) for i in range(devices)])  3.46 us
  transfers between devices with their start and end apart: 9, of which 4 were waited for; matrix products, arithmetic and copies ran while one was open for 0% of the time, Pallas kernels for 14%

profile of v4, /device:TPU:2, one launch (start us, length us, event | category | flops | bytes accessed | tf_op | source)
XLA Modules:
  0.0 30.5 jit_solution(710393934407168059)
XLA Ops:
  0.6 1.5 %edges.1 = (f32[448,128]{1,0:T(8,128)S(1)}, f32[456,128]{1,0:T(8,128)S(1)}, f32[32,2048]{1,0:T(8,128)S(1)}, s32[32,2048]{1,0:T(8,128)S(1)}, s32[32,2048]{1,0:T(8...) custom-call(s32[1]{0:T(128)} %bitcast.1.space, f32[32,2048]{1,0:T(8,128)} %bitcast.5, s32[32,2048]{1,0:T(8,128)} %bed.1, ...), custom_call_target="tpu_custom_call" | custom-call | tf_op jit(solution)/shard_map/edges/pallas_call | solution.py:414
  2.1 0.1 collective-permute-start.1
  2.2 3.1 %collective-permute-start = (f32[448,128]{1,0:T(8,128)S(1)}, f32[448,128]{1,0:T(8,128)S(1)}, u32[]{:S(2)}, u32[]{:S(2)}) collective-permute-start(f32[448,128]{1,0:T(8,128)S(1)} %get-tuple-element.35), channel_id=1, source_target_pairs={{1,2},{3,4},{5,6},{7,8},{9,10},{11,12},{13,14},{15,16},{17,18},{19... | collective-permute-start | bytes 688136 | tf_op jit(solution)/shard_map/ppermute | solution.py:434
  5.3 2.5 %inner.1 = (f32[512,128]{1,0:T(8,128)S(1)}, f32[256,128]{1,0:T(8,128)S(1)}, f32[8,20,16,128]{3,2,1,0:T(8,128)S(1)}, f32[7,24,8,128]{3,2,1,0:T(8,128)S(1)}, f32[288,128]{1,0:T(8,128)}) custom-call(s32[1]{0:T(128)} %bitcast.1.space, f32[32,2048]{1,0:T(8,128)S(1)} %get-tuple-element.28.tv, s32[32,2048]{1,0:T(8,128)S(1)} %get-tuple-element.29.bv, ...), custom_call_target="tpu_custom_call" | custom-call | tf_op jit(solution)/shard_map/inner/pallas_call | solution.py:414
  7.9 0.9 %collective-permute-start.6 = (f32[288,128]{1,0:T(8,128)}, f32[288,128]{1,0:T(8,128)S(1)}, u32[]{:S(2)}, u32[]{:S(2)}) collective-permute-start(f32[288,128]{1,0:T(8,128)} %get-tuple-element.42), channel_id=1, source_target_pairs={{1,2},{3,4},{5,6},{7,8},{9,10},{11,12},{13,14},{15,16},{17,18},{19... | collective-permute-start | bytes 442376 | tf_op jit(solution)/shard_map/ppermute | solution.py:434
  8.8 1.1 %collective-permute-done.off = f32[448,128]{1,0:T(8,128)S(1)} collective-permute-done((f32[448,128]{1,0:T(8,128)S(1)}, f32[448,128]{1,0:T(8,128)S(1)}, u32[]{:S(2)}, u32[]{:S(2)}) %collective-permute-start) | collective-permute-done | bytes 229408 | tf_op jit(solution)/shard_map/ppermute | solution.py:434
  9.9 0.0 collective-permute-done.1.inside
  9.9 1.7 %outer.1 = (f32[512,128]{1,0:T(8,128)S(1)}, f32[128,128]{1,0:T(8,128)S(1)}, f32[128,128]{1,0:T(8,128)S(1)}) custom-call(s32[1]{0:T(128)} %bitcast.place, s32[1]{0:T(128)} %bitcast.1.space, s32[1]{0:T(128)} %constant.10.clone.1.last, f32[448,128]{1,0:T(8,128)S(1)} %collective-permute-done.off, f32[456,128]{1,0:T(8,128)S(1)} %collective-permute-done.1.inside, ...), custom_call_target="tpu_custom_call" | custom-call | tf_op jit(solution)/shard_map/outer/pallas_call | solution.py:414
  11.6 4.1 %collective-permute-start.5 = (f32[128,128]{1,0:T(8,128)S(1)}, f32[128,128]{1,0:T(8,128)S(1)}, u32[]{:S(2)}, u32[]{:S(2)}) collective-permute-start(f32[128,128]{1,0:T(8,128)S(1)} %get-tuple-element.41), channel_id=1, source_target_pairs={{0,96},{32,0},{64,32},{96,64},{1,97},{33,1},{65,33},{97,65},{2,98}... | collective-permute-start | bytes 196616 | tf_op jit(solution)/shard_map/ppermute | solution.py:427
  15.7 0.0 collective-permute-start.4
  15.7 1.3 %collective-permute-start.3 = (f32[128,128]{1,0:T(8,128)S(1)}, f32[128,128]{1,0:T(8,128)S(1)}, u32[]{:S(2)}, u32[]{:S(2)}) collective-permute-start(f32[128,128]{1,0:T(8,128)S(1)} %get-tuple-element.41), channel_id=1, source_target_pairs={{0,32},{32,64},{64,96},{96,0},{1,33},{33,65},{65,97},{97,1},{2,34}... | collective-permute-start | bytes 196616 | tf_op jit(solution)/shard_map/ppermute | solution.py:427
  16.9 2.2 %collective-permute-start.2 = (f32[512,128]{1,0:T(8,128)S(1)}, f32[512,128]{1,0:T(8,128)S(1)}, u32[]{:S(2)}, u32[]{:S(2)}) collective-permute-start(f32[512,128]{1,0:T(8,128)S(1)} %get-tuple-element.39.end), channel_id=1, source_target_pairs={{0,32},{32,64},{64,96},{96,0},{1,33},{33,65},{65,97},{97,1},{2,34}... | collective-permute-start | bytes 786440 | tf_op jit(solution)/shard_map/ppermute | solution.py:427
  19.2 0.0 collective-permute-done.6.soff
  19.2 0.0 collective-permute-done.5.d3
  19.2 3.0 %collective-permute-done.4.d2 = f32[128,128]{1,0:T(8,128)S(1)} collective-permute-done((f32[128,128]{1,0:T(8,128)S(1)}, f32[128,128]{1,0:T(8,128)S(1)}, u32[]{:S(2)}, u32[]{:S(2)}) %collective-permute-start.4) | collective-permute-done | bytes 65568 | tf_op jit(solution)/shard_map/ppermute | solution.py:427
  22.2 0.4 %collective-permute-done.3.d1 = f32[128,128]{1,0:T(8,128)S(1)} collective-permute-done((f32[128,128]{1,0:T(8,128)S(1)}, f32[128,128]{1,0:T(8,128)S(1)}, u32[]{:S(2)}, u32[]{:S(2)}) %collective-permute-start.3) | collective-permute-done | bytes 65568 | tf_op jit(solution)/shard_map/ppermute | solution.py:427
  22.7 0.1 collective-permute-start.8
  22.7 1.9 %collective-permute-start.7 = (f32[192,128]{1,0:T(8,128)S(1)}, f32[192,128]{1,0:T(8,128)S(1)}, u32[]{:S(2)}, u32[]{:S(2)}) collective-permute-start(f32[192,128]{1,0:T(8,128)S(1)} %get-tuple-element.49), channel_id=1, source_target_pairs={{1,2},{3,4},{5,6},{7,8},{9,10},{11,12},{13,14},{15,16},{17,18},{19... | collective-permute-start | bytes 294920 | tf_op jit(solution)/shard_map/ppermute | solution.py:434
  24.7 4.3 %collective-permute-done.7.off = f32[192,128]{1,0:T(8,128)S(1)} collective-permute-done((f32[192,128]{1,0:T(8,128)S(1)}, f32[192,128]{1,0:T(8,128)S(1)}, u32[]{:S(2)}, u32[]{:S(2)}) %collective-permute-start.7) | collective-permute-done | bytes 98336 | tf_op jit(solution)/shard_map/ppermute | solution.py:434
  29.0 0.0 collective-permute-done.2.before
  29.0 0.0 collective-permute-done.8.inside
  29.0 1.5 %chain.1 = (f32[32,2048]{1,0:T(8,128)}, f32[32,2048]{1,0:T(8,128)}) custom-call(s32[1]{0:T(128)} %bitcast.place, s32[1]{0:T(128)} %bitcast.1.space, s32[1]{0:T(128)} %constant.10.clone.1.last, f32[512,128]{1,0:T(8,128)S(1)} %get-tuple-element.33.own, f32[7,24,8,128]{3,2,1,0:T(8,128)S(1)} %get-tuple-element.34.cstate_in.cstate, ...), custom_call_target="tpu_custom_call" | custom-call | tf_op jit(solution)/shard_map/chain/pallas_call | solution.py:414
  (1 shorter events, 0.0 us)
Async XLA Ops:
  2.1 7.7 %collective-permute-start.1 = (f32[456,128]{1,0:T(8,128)S(1)}, f32[456,128]{1,0:T(8,128)S(1)}, u32[]{:S(2)}, u32[]{:S(2)}) collective-permute-start(f32[456,128]{1,0:T(8,128)S(1)} %get-tuple-element.36), channel_id=1, source_target_pairs={{0,1},{1,0},{2,3},{3,2},{4,5},{5,4},{6,7},{7,6},{8,9},{9,8},{10,11... | collective-permute-start | bytes 700424 | tf_op jit(solution)/shard_map/ppermute | solution.py:439
  2.2 7.6 %collective-permute-start = (f32[448,128]{1,0:T(8,128)S(1)}, f32[448,128]{1,0:T(8,128)S(1)}, u32[]{:S(2)}, u32[]{:S(2)}) collective-permute-start(f32[448,128]{1,0:T(8,128)S(1)} %get-tuple-element.35), channel_id=1, source_target_pairs={{1,2},{3,4},{5,6},{7,8},{9,10},{11,12},{13,14},{15,16},{17,18},{19... | collective-permute-start | bytes 688136 | tf_op jit(solution)/shard_map/ppermute | solution.py:434
  7.9 11.3 %collective-permute-start.6 = (f32[288,128]{1,0:T(8,128)}, f32[288,128]{1,0:T(8,128)S(1)}, u32[]{:S(2)}, u32[]{:S(2)}) collective-permute-start(f32[288,128]{1,0:T(8,128)} %get-tuple-element.42), channel_id=1, source_target_pairs={{1,2},{3,4},{5,6},{7,8},{9,10},{11,12},{13,14},{15,16},{17,18},{19... | collective-permute-start | bytes 442376 | tf_op jit(solution)/shard_map/ppermute | solution.py:434
  11.6 7.6 %collective-permute-start.5 = (f32[128,128]{1,0:T(8,128)S(1)}, f32[128,128]{1,0:T(8,128)S(1)}, u32[]{:S(2)}, u32[]{:S(2)}) collective-permute-start(f32[128,128]{1,0:T(8,128)S(1)} %get-tuple-element.41), channel_id=1, source_target_pairs={{0,96},{32,0},{64,32},{96,64},{1,97},{33,1},{65,33},{97,65},{2,98}... | collective-permute-start | bytes 196616 | tf_op jit(solution)/shard_map/ppermute | solution.py:427
  15.7 6.5 %collective-permute-start.4 = (f32[128,128]{1,0:T(8,128)S(1)}, f32[128,128]{1,0:T(8,128)S(1)}, u32[]{:S(2)}, u32[]{:S(2)}) collective-permute-start(f32[128,128]{1,0:T(8,128)S(1)} %get-tuple-element.41), channel_id=1, source_target_pairs={{0,64},{32,96},{64,0},{96,32},{1,65},{33,97},{65,1},{97,33},{2,66}... | collective-permute-start | bytes 196616 | tf_op jit(solution)/shard_map/ppermute | solution.py:427
  15.7 6.9 %collective-permute-start.3 = (f32[128,128]{1,0:T(8,128)S(1)}, f32[128,128]{1,0:T(8,128)S(1)}, u32[]{:S(2)}, u32[]{:S(2)}) collective-permute-start(f32[128,128]{1,0:T(8,128)S(1)} %get-tuple-element.41), channel_id=1, source_target_pairs={{0,32},{32,64},{64,96},{96,0},{1,33},{33,65},{65,97},{97,1},{2,34}... | collective-permute-start | bytes 196616 | tf_op jit(solution)/shard_map/ppermute | solution.py:427
  16.9 12.1 %collective-permute-start.2 = (f32[512,128]{1,0:T(8,128)S(1)}, f32[512,128]{1,0:T(8,128)S(1)}, u32[]{:S(2)}, u32[]{:S(2)}) collective-permute-start(f32[512,128]{1,0:T(8,128)S(1)} %get-tuple-element.39.end), channel_id=1, source_target_pairs={{0,32},{32,64},{64,96},{96,0},{1,33},{33,65},{65,97},{97,1},{2,34}... | collective-permute-start | bytes 786440 | tf_op jit(solution)/shard_map/ppermute | solution.py:427
  22.7 6.3 %collective-permute-start.8 = (f32[480,128]{1,0:T(8,128)S(1)}, f32[480,128]{1,0:T(8,128)S(1)}, u32[]{:S(2)}, u32[]{:S(2)}) collective-permute-start(f32[480,128]{1,0:T(8,128)S(1)} %get-tuple-element.50), channel_id=1, source_target_pairs={{0,1},{1,0},{2,3},{3,2},{4,5},{5,4},{6,7},{7,6},{8,9},{9,8},{10,11... | collective-permute-start | bytes 737288 | tf_op jit(solution)/shard_map/ppermute | solution.py:439
  22.7 6.2 %collective-permute-start.7 = (f32[192,128]{1,0:T(8,128)S(1)}, f32[192,128]{1,0:T(8,128)S(1)}, u32[]{:S(2)}, u32[]{:S(2)}) collective-permute-start(f32[192,128]{1,0:T(8,128)S(1)} %get-tuple-element.49), channel_id=1, source_target_pairs={{1,2},{3,4},{5,6},{7,8},{9,10},{11,12},{13,14},{15,16},{17,18},{19... | collective-permute-start | bytes 294920 | tf_op jit(solution)/shard_map/ppermute | solution.py:434

commit v5 on v4

--- a/solution.py
+++ b/solution.py
@@ -434,6 +434,14 @@
     return lax.ppermute(x, ("tm", "space"), pairs + [(j, i) for i, j in pairs])
 
 
+def far_swap_later(x):
+    slices, devices = lax.axis_size("tm"), lax.axis_size("space")
+    pairs = [(m * devices + i, m * devices + i + 1) for m in range(1, slices) for i in range(1, devices - 1, 2)]
+    pairs += [(i, i + 1) for i in range(0, devices, 2)]
+    ring = [(m * devices + i, (m % (slices - 1) + 1) * devices + i) for m in range(1, slices) for i in (0, devices - 1)]
+    return lax.ppermute(x, ("tm", "space"), pairs + [(j, i) for i, j in pairs] + ring)
+
+
 def near_swap(x):
     devices = lax.axis_size("space")
     return lax.ppermute(x, "space", [(i, i ^ 1) for i in range(devices)])
@@ -470,7 +478,7 @@
         [(12, WIN, CH, 128), (7, 24, CCH, 128)] + [(WIN, CH, 128)] * 2,
         "sssvvvvv",
     )
-    soff = far_swap(soff)
+    soff = far_swap_later(soff)
     d1, d2, d3 = (shifted(payload, k) for k in (1, 2, 3))
     d1, d2, d3, soff = lax.optimization_barrier((d1, d2, d3, soff))
     base, j1, j2, off, inside = call(
@@ -478,7 +486,7 @@
         [lines(coarse_lines)] * 3 + [lines(JUMP_LINES), lines(JUMP_LINES + STATIC_LINES)], (), "ssvvvv",
     )
     before = shifted(end, 1)
-    off, inside = far_swap(off), near_swap(inside)
+    off, inside = far_swap_later(off), near_swap(inside)
     out, nxt = call(
         chain_kernel, "chain",
         (place, space, last, own, cstate, end, prev, before, base, j1, j2, off, inside, soff),

time: 30.7 us -> 29.9 us (0.974)
  the two profiles are of different devices: /device:TPU:2 before, /device:TPU:66 now
where the time goes in v5:
time: 29.9 us; the launch traced here: 29.5 us
  starting transfers between devices  10.7 us (36%)
  waiting for transfers between devices  9.57 us (32%)
  Pallas kernels  8.53 us (29%)
  between operations  0.69 us (2%)
    pallas_call x5, Pallas kernels, call(): pl.pallas_call(kernel, out_shape=outs, in_specs=[pl.BlockSpec(memory_spac...  8.53 us
    ppermute x4, starting transfers between devices, shifted(): lax.ppermute(x, 'tm', [(i, (i + by) % devices) for i in range(devices)])  4.93 us
    ppermute x2, waiting for transfers between devices, far_swap_later(): lax.ppermute(x, ('tm', 'space'), pairs + [(j, i) for i, j in pairs] + ring)  4.63 us
    ppermute x4, waiting for transfers between devices, shifted(): lax.ppermute(x, 'tm', [(i, (i + by) % devices) for i in range(devices)])  3.86 us
    ppermute x1, starting transfers between devices, far_swap(): return lax.ppermute(x, ('tm', 'space'), pairs + [(j, i) for i, j in pairs])  3.09 us
    ppermute x2, starting transfers between devices, far_swap_later(): lax.ppermute(x, ('tm', 'space'), pairs + [(j, i) for i, j in pairs] + ring)  2.5 us
    ppermute x1, waiting for transfers between devices, far_swap(): return lax.ppermute(x, ('tm', 'space'), pairs + [(j, i) for i, j in pairs])  1.09 us
  transfers between devices with their start and end apart: 9, of which 4 were waited for; matrix products, arithmetic and copies ran while one was open for 0% of the time, Pallas kernels for 14%

profile of v5, /device:TPU:66, one launch (start us, length us, event | category | flops | bytes accessed | tf_op | source)
XLA Modules:
  0.0 29.5 jit_solution(3744246291272994296)
XLA Ops:
  0.6 1.5 %edges.1 = (f32[448,128]{1,0:T(8,128)S(1)}, f32[456,128]{1,0:T(8,128)S(1)}, f32[32,2048]{1,0:T(8,128)S(1)}, s32[32,2048]{1,0:T(8,128)S(1)}, s32[32,2048]{1,0:T(8...) custom-call(s32[1]{0:T(128)} %bitcast.1.space, f32[32,2048]{1,0:T(8,128)} %bitcast.5, s32[32,2048]{1,0:T(8,128)} %bed.1, ...), custom_call_target="tpu_custom_call" | custom-call | tf_op jit(solution)/shard_map/edges/pallas_call | solution.py:414
  2.1 0.1 collective-permute-start.1
  2.2 3.1 %collective-permute-start = (f32[448,128]{1,0:T(8,128)S(1)}, f32[448,128]{1,0:T(8,128)S(1)}, u32[]{:S(2)}, u32[]{:S(2)}) collective-permute-start(f32[448,128]{1,0:T(8,128)S(1)} %get-tuple-element.35), channel_id=1, source_target_pairs={{1,2},{3,4},{5,6},{7,8},{9,10},{11,12},{13,14},{15,16},{17,18},{19... | collective-permute-start | bytes 688136 | tf_op jit(solution)/shard_map/ppermute | solution.py:434
  5.3 2.5 %inner.1 = (f32[512,128]{1,0:T(8,128)S(1)}, f32[256,128]{1,0:T(8,128)S(1)}, f32[8,20,16,128]{3,2,1,0:T(8,128)S(1)}, f32[7,24,8,128]{3,2,1,0:T(8,128)S(1)}, f32[288,128]{1,0:T(8,128)}) custom-call(s32[1]{0:T(128)} %bitcast.1.space, f32[32,2048]{1,0:T(8,128)S(1)} %get-tuple-element.28.tv, s32[32,2048]{1,0:T(8,128)S(1)} %get-tuple-element.29.bv, ...), custom_call_target="tpu_custom_call" | custom-call | tf_op jit(solution)/shard_map/inner/pallas_call | solution.py:414
  7.9 0.9 %collective-permute-start.6 = (f32[288,128]{1,0:T(8,128)}, f32[288,128]{1,0:T(8,128)S(1)}, u32[]{:S(2)}, u32[]{:S(2)}) collective-permute-start(f32[288,128]{1,0:T(8,128)} %get-tuple-element.42), channel_id=1, source_target_pairs={{33,34},{35,36},{37,38},{39,40},{41,42},{43,44},{45,46},{47,48},{4... | collective-permute-start | bytes 442376 | tf_op jit(solution)/shard_map/ppermute | solution.py:442
  8.8 1.1 %collective-permute-done.off = f32[448,128]{1,0:T(8,128)S(1)} collective-permute-done((f32[448,128]{1,0:T(8,128)S(1)}, f32[448,128]{1,0:T(8,128)S(1)}, u32[]{:S(2)}, u32[]{:S(2)}) %collective-permute-start) | collective-permute-done | bytes 229408 | tf_op jit(solution)/shard_map/ppermute | solution.py:434
  9.9 0.0 collective-permute-done.1.inside
  9.9 1.7 %outer.1 = (f32[512,128]{1,0:T(8,128)S(1)}, f32[128,128]{1,0:T(8,128)S(1)}, f32[128,128]{1,0:T(8,128)S(1)}) custom-call(s32[1]{0:T(128)} %bitcast.place, s32[1]{0:T(128)} %bitcast.1.space, s32[1]{0:T(128)} %constant.10.clone.1.last, f32[448,128]{1,0:T(8,128)S(1)} %collective-permute-done.off, f32[456,128]{1,0:T(8,128)S(1)} %collective-permute-done.1.inside, ...), custom_call_target="tpu_custom_call" | custom-call | tf_op jit(solution)/shard_map/outer/pallas_call | solution.py:414
  11.6 0.2 collective-permute-start.5
  11.7 3.6 %collective-permute-start.4 = (f32[128,128]{1,0:T(8,128)S(1)}, f32[128,128]{1,0:T(8,128)S(1)}, u32[]{:S(2)}, u32[]{:S(2)}) collective-permute-start(f32[128,128]{1,0:T(8,128)S(1)} %get-tuple-element.41), channel_id=1, source_target_pairs={{0,64},{32,96},{64,0},{96,32},{1,65},{33,97},{65,1},{97,33},{2,66}... | collective-permute-start | bytes 196616 | tf_op jit(solution)/shard_map/ppermute | solution.py:427
  15.3 0.0 collective-permute-start.3
  15.3 1.2 %collective-permute-start.2 = (f32[512,128]{1,0:T(8,128)S(1)}, f32[512,128]{1,0:T(8,128)S(1)}, u32[]{:S(2)}, u32[]{:S(2)}) collective-permute-start(f32[512,128]{1,0:T(8,128)S(1)} %get-tuple-element.39.end), channel_id=1, source_target_pairs={{0,32},{32,64},{64,96},{96,0},{1,33},{33,65},{65,97},{97,1},{2,34}... | collective-permute-start | bytes 786440 | tf_op jit(solution)/shard_map/ppermute | solution.py:427
  16.5 0.0 collective-permute-done.6.soff
  16.5 0.0 collective-permute-done.5.d3
  16.5 1.5 %collective-permute-done.4.d2 = f32[128,128]{1,0:T(8,128)S(1)} collective-permute-done((f32[128,128]{1,0:T(8,128)S(1)}, f32[128,128]{1,0:T(8,128)S(1)}, u32[]{:S(2)}, u32[]{:S(2)}) %collective-permute-start.4) | collective-permute-done | bytes 65568 | tf_op jit(solution)/shard_map/ppermute | solution.py:427
  18.0 2.4 %collective-permute-done.3.d1 = f32[128,128]{1,0:T(8,128)S(1)} collective-permute-done((f32[128,128]{1,0:T(8,128)S(1)}, f32[128,128]{1,0:T(8,128)S(1)}, u32[]{:S(2)}, u32[]{:S(2)}) %collective-permute-start.3) | collective-permute-done | bytes 65568 | tf_op jit(solution)/shard_map/ppermute | solution.py:427
  20.4 0.1 collective-permute-start.8
  20.5 1.6 %collective-permute-start.7 = (f32[192,128]{1,0:T(8,128)S(1)}, f32[192,128]{1,0:T(8,128)S(1)}, u32[]{:S(2)}, u32[]{:S(2)}) collective-permute-start(f32[192,128]{1,0:T(8,128)S(1)} %get-tuple-element.49), channel_id=1, source_target_pairs={{33,34},{35,36},{37,38},{39,40},{41,42},{43,44},{45,46},{47,48},{4... | collective-permute-start | bytes 294920 | tf_op jit(solution)/shard_map/ppermute | solution.py:442
  22.1 4.6 %collective-permute-done.7.off = f32[192,128]{1,0:T(8,128)S(1)} collective-permute-done((f32[192,128]{1,0:T(8,128)S(1)}, f32[192,128]{1,0:T(8,128)S(1)}, u32[]{:S(2)}, u32[]{:S(2)}) %collective-permute-start.7) | collective-permute-done | bytes 98336 | tf_op jit(solution)/shard_map/ppermute | solution.py:442
  26.7 0.0 collective-permute-done.2.before
  26.7 0.0 collective-permute-done.8.inside
  26.7 2.8 %chain.1 = (f32[32,2048]{1,0:T(8,128)}, f32[32,2048]{1,0:T(8,128)}) custom-call(s32[1]{0:T(128)} %bitcast.place, s32[1]{0:T(128)} %bitcast.1.space, s32[1]{0:T(128)} %constant.10.clone.1.last, f32[512,128]{1,0:T(8,128)S(1)} %get-tuple-element.33.own, f32[7,24,8,128]{3,2,1,0:T(8,128)S(1)} %get-tuple-element.34.cstate_in.cstate, ...), custom_call_target="tpu_custom_call" | custom-call | tf_op jit(solution)/shard_map/chain/pallas_call | solution.py:414
  (1 shorter events, 0.0 us)
Async XLA Ops:
  2.1 7.7 %collective-permute-start.1 = (f32[456,128]{1,0:T(8,128)S(1)}, f32[456,128]{1,0:T(8,128)S(1)}, u32[]{:S(2)}, u32[]{:S(2)}) collective-permute-start(f32[456,128]{1,0:T(8,128)S(1)} %get-tuple-element.36), channel_id=1, source_target_pairs={{0,1},{1,0},{2,3},{3,2},{4,5},{5,4},{6,7},{7,6},{8,9},{9,8},{10,11... | collective-permute-start | bytes 700424 | tf_op jit(solution)/shard_map/ppermute | solution.py:447
  2.2 7.6 %collective-permute-start = (f32[448,128]{1,0:T(8,128)S(1)}, f32[448,128]{1,0:T(8,128)S(1)}, u32[]{:S(2)}, u32[]{:S(2)}) collective-permute-start(f32[448,128]{1,0:T(8,128)S(1)} %get-tuple-element.35), channel_id=1, source_target_pairs={{1,2},{3,4},{5,6},{7,8},{9,10},{11,12},{13,14},{15,16},{17,18},{19... | collective-permute-start | bytes 688136 | tf_op jit(solution)/shard_map/ppermute | solution.py:434
  7.9 8.6 %collective-permute-start.6 = (f32[288,128]{1,0:T(8,128)}, f32[288,128]{1,0:T(8,128)S(1)}, u32[]{:S(2)}, u32[]{:S(2)}) collective-permute-start(f32[288,128]{1,0:T(8,128)} %get-tuple-element.42), channel_id=1, source_target_pairs={{33,34},{35,36},{37,38},{39,40},{41,42},{43,44},{45,46},{47,48},{4... | collective-permute-start | bytes 442376 | tf_op jit(solution)/shard_map/ppermute | solution.py:442
  11.6 4.9 %collective-permute-start.5 = (f32[128,128]{1,0:T(8,128)S(1)}, f32[128,128]{1,0:T(8,128)S(1)}, u32[]{:S(2)}, u32[]{:S(2)}) collective-permute-start(f32[128,128]{1,0:T(8,128)S(1)} %get-tuple-element.41), channel_id=1, source_target_pairs={{0,96},{32,0},{64,32},{96,64},{1,97},{33,1},{65,33},{97,65},{2,98}... | collective-permute-start | bytes 196616 | tf_op jit(solution)/shard_map/ppermute | solution.py:427
  11.7 6.2 %collective-permute-start.4 = (f32[128,128]{1,0:T(8,128)S(1)}, f32[128,128]{1,0:T(8,128)S(1)}, u32[]{:S(2)}, u32[]{:S(2)}) collective-permute-start(f32[128,128]{1,0:T(8,128)S(1)} %get-tuple-element.41), channel_id=1, source_target_pairs={{0,64},{32,96},{64,0},{96,32},{1,65},{33,97},{65,1},{97,33},{2,66}... | collective-permute-start | bytes 196616 | tf_op jit(solution)/shard_map/ppermute | solution.py:427
  15.3 5.0 %collective-permute-start.3 = (f32[128,128]{1,0:T(8,128)S(1)}, f32[128,128]{1,0:T(8,128)S(1)}, u32[]{:S(2)}, u32[]{:S(2)}) collective-permute-start(f32[128,128]{1,0:T(8,128)S(1)} %get-tuple-element.41), channel_id=1, source_target_pairs={{0,32},{32,64},{64,96},{96,0},{1,33},{33,65},{65,97},{97,1},{2,34}... | collective-permute-start | bytes 196616 | tf_op jit(solution)/shard_map/ppermute | solution.py:427
  15.3 11.4 %collective-permute-start.2 = (f32[512,128]{1,0:T(8,128)S(1)}, f32[512,128]{1,0:T(8,128)S(1)}, u32[]{:S(2)}, u32[]{:S(2)}) collective-permute-start(f32[512,128]{1,0:T(8,128)S(1)} %get-tuple-element.39.end), channel_id=1, source_target_pairs={{0,32},{32,64},{64,96},{96,0},{1,33},{33,65},{65,97},{97,1},{2,34}... | collective-permute-start | bytes 786440 | tf_op jit(solution)/shard_map/ppermute | solution.py:427
  20.4 6.3 %collective-permute-start.8 = (f32[480,128]{1,0:T(8,128)S(1)}, f32[480,128]{1,0:T(8,128)S(1)}, u32[]{:S(2)}, u32[]{:S(2)}) collective-permute-start(f32[480,128]{1,0:T(8,128)S(1)} %get-tuple-element.50), channel_id=1, source_target_pairs={{0,1},{1,0},{2,3},{3,2},{4,5},{5,4},{6,7},{7,6},{8,9},{9,8},{10,11... | collective-permute-start | bytes 737288 | tf_op jit(solution)/shard_map/ppermute | solution.py:447
  20.5 6.2 %collective-permute-start.7 = (f32[192,128]{1,0:T(8,128)S(1)}, f32[192,128]{1,0:T(8,128)S(1)}, u32[]{:S(2)}, u32[]{:S(2)}) collective-permute-start(f32[192,128]{1,0:T(8,128)S(1)} %get-tuple-element.49), channel_id=1, source_target_pairs={{33,34},{35,36},{37,38},{39,40},{41,42},{43,44},{45,46},{47,48},{4... | collective-permute-start | bytes 294920 | tf_op jit(solution)/shard_map/ppermute | solution.py:442

commit v6 on v5

--- a/solution.py
+++ b/solution.py
@@ -291,11 +291,11 @@
     target[...] = source[...]
 
 
-def gather_kernel(place, space, cstate, d1, d2, d3, base, j1, j2, off, inside):
+def gather_kernel(place, space, cstate, near1, near2, far, base, j1, j2, off, inside):
     m = place[0]
-    base[...] = jnp.where(m == 1, d1[...], jnp.where(m == 2, d2[...], d3[...]))
-    j1[...] = jnp.where(m == 2, d1[...], d2[...])
-    j2[...] = d1[...]
+    base[...] = jnp.where(m == 1, near1[...], jnp.where(m == 2, near2[...], far[...]))
+    j1[...] = jnp.where(m == 2, far[...], near2[...])
+    j2[...] = near1[...]
     odd = space[0] & 1
     at = 0
     for ref, count in zip((base, j1, j2), JUMPS):
@@ -479,10 +479,10 @@
         "sssvvvvv",
     )
     soff = far_swap_later(soff)
-    d1, d2, d3 = (shifted(payload, k) for k in (1, 2, 3))
-    d1, d2, d3, soff = lax.optimization_barrier((d1, d2, d3, soff))
+    rounds = [lax.ppermute(payload, "tm", [(i, i ^ k) for i in range(lax.axis_size("tm"))]) for k in (1, 2, 3)]
+    *rounds, soff = lax.optimization_barrier((*rounds, soff))
     base, j1, j2, off, inside = call(
-        gather_kernel, "gather", (place, space, cstate, d1, d2, d3),
+        gather_kernel, "gather", (place, space, cstate, *rounds),
         [lines(coarse_lines)] * 3 + [lines(JUMP_LINES), lines(JUMP_LINES + STATIC_LINES)], (), "ssvvvv",
     )
     before = shifted(end, 1)

time: 29.9 us -> 29.9 us (level)
  the two profiles are of different devices: /device:TPU:66 before, /device:TPU:102 now
where the time goes in v6:
time: 29.9 us; the launch traced here: 29.7 us
  starting transfers between devices  10.2 us (34%)
  waiting for transfers between devices  9.83 us (33%)
  Pallas kernels  9.04 us (30%)
  between operations  0.69 us (2%)
    pallas_call x5, Pallas kernels, call(): pl.pallas_call(kernel, out_shape=outs, in_specs=[pl.BlockSpec(memory_spac...  9.04 us
    ppermute x2, waiting for transfers between devices, far_swap_later(): lax.ppermute(x, ('tm', 'space'), pairs + [(j, i) for i, j in pairs] + ring)  4.47 us
    ppermute x3, waiting for transfers between devices, per_device(): lax.ppermute(payload, 'tm', [(i, i ^ k) for i in range(lax.axis_size('tm'...  4.27 us
    ppermute x3, starting transfers between devices, per_device(): lax.ppermute(payload, 'tm', [(i, i ^ k) for i in range(lax.axis_size('tm'...  4.17 us
    ppermute x1, starting transfers between devices, far_swap(): return lax.ppermute(x, ('tm', 'space'), pairs + [(j, i) for i, j in pairs])  3.38 us
    ppermute x2, starting transfers between devices, far_swap_later(): lax.ppermute(x, ('tm', 'space'), pairs + [(j, i) for i, j in pairs] + ring)  2.36 us
    ppermute x1, waiting for transfers between devices, far_swap(): return lax.ppermute(x, ('tm', 'space'), pairs + [(j, i) for i, j in pairs])  1.09 us
  transfers between devices with their start and end apart: 9, of which 4 were waited for; matrix products, arithmetic and copies ran while one was open for 0% of the time, Pallas kernels for 14%

profile of v6, /device:TPU:102, one launch (start us, length us, event | category | flops | bytes accessed | tf_op | source)
XLA Modules:
  0.0 29.7 jit_solution(10252129732321108288)
XLA Ops:
  0.6 1.5 %edges.1 = (f32[448,128]{1,0:T(8,128)S(1)}, f32[456,128]{1,0:T(8,128)S(1)}, f32[32,2048]{1,0:T(8,128)S(1)}, s32[32,2048]{1,0:T(8,128)S(1)}, s32[32,2048]{1,0:T(8...) custom-call(s32[1]{0:T(128)} %bitcast.1.space, f32[32,2048]{1,0:T(8,128)} %bitcast.5, s32[32,2048]{1,0:T(8,128)} %bed.1, ...), custom_call_target="tpu_custom_call" | custom-call | tf_op jit(solution)/shard_map/edges/pallas_call | solution.py:414
  2.1 0.1 collective-permute-start.1
  2.2 3.4 %collective-permute-start = (f32[448,128]{1,0:T(8,128)S(1)}, f32[448,128]{1,0:T(8,128)S(1)}, u32[]{:S(2)}, u32[]{:S(2)}) collective-permute-start(f32[448,128]{1,0:T(8,128)S(1)} %get-tuple-element.35), channel_id=1, source_target_pairs={{1,2},{3,4},{5,6},{7,8},{9,10},{11,12},{13,14},{15,16},{17,18},{19... | collective-permute-start | bytes 688136 | tf_op jit(solution)/shard_map/ppermute | solution.py:434
  5.6 2.5 %inner.1 = (f32[512,128]{1,0:T(8,128)S(1)}, f32[256,128]{1,0:T(8,128)S(1)}, f32[8,20,16,128]{3,2,1,0:T(8,128)S(1)}, f32[7,24,8,128]{3,2,1,0:T(8,128)S(1)}, f32[288,128]{1,0:T(8,128)}) custom-call(s32[1]{0:T(128)} %bitcast.1.space, f32[32,2048]{1,0:T(8,128)S(1)} %get-tuple-element.28.tv, s32[32,2048]{1,0:T(8,128)S(1)} %get-tuple-element.29.bv, ...), custom_call_target="tpu_custom_call" | custom-call | tf_op jit(solution)/shard_map/inner/pallas_call | solution.py:414
  8.2 0.6 %collective-permute-start.6 = (f32[288,128]{1,0:T(8,128)}, f32[288,128]{1,0:T(8,128)S(1)}, u32[]{:S(2)}, u32[]{:S(2)}) collective-permute-start(f32[288,128]{1,0:T(8,128)} %get-tuple-element.42), channel_id=1, source_target_pairs={{33,34},{35,36},{37,38},{39,40},{41,42},{43,44},{45,46},{47,48},{4... | collective-permute-start | bytes 442376 | tf_op jit(solution)/shard_map/ppermute | solution.py:442
  8.8 1.1 %collective-permute-done.off = f32[448,128]{1,0:T(8,128)S(1)} collective-permute-done((f32[448,128]{1,0:T(8,128)S(1)}, f32[448,128]{1,0:T(8,128)S(1)}, u32[]{:S(2)}, u32[]{:S(2)}) %collective-permute-start) | collective-permute-done | bytes 229408 | tf_op jit(solution)/shard_map/ppermute | solution.py:434
  9.9 0.0 collective-permute-done.1.inside
  9.9 1.7 %outer.1 = (f32[512,128]{1,0:T(8,128)S(1)}, f32[128,128]{1,0:T(8,128)S(1)}, f32[128,128]{1,0:T(8,128)S(1)}) custom-call(s32[1]{0:T(128)} %bitcast.place, s32[1]{0:T(128)} %bitcast.1.space, s32[1]{0:T(128)} %constant.10.clone.1.last, f32[448,128]{1,0:T(8,128)S(1)} %collective-permute-done.off, f32[456,128]{1,0:T(8,128)S(1)} %collective-permute-done.1.inside, ...), custom_call_target="tpu_custom_call" | custom-call | tf_op jit(solution)/shard_map/outer/pallas_call | solution.py:414
  11.6 0.1 collective-permute-start.5
  11.7 2.5 %collective-permute-start.4 = (f32[128,128]{1,0:T(8,128)S(1)}, f32[128,128]{1,0:T(8,128)S(1)}, u32[]{:S(2)}, u32[]{:S(2)}) collective-permute-start(f32[128,128]{1,0:T(8,128)S(1)} %get-tuple-element.41), channel_id=1, source_target_pairs={{0,64},{32,96},{64,0},{96,32},{1,65},{33,97},{65,1},{97,33},{2,66}... | collective-permute-start | bytes 196616 | tf_op jit(solution)/shard_map/ppermute | solution.py:482
  14.1 1.6 %collective-permute-start.3 = (f32[128,128]{1,0:T(8,128)S(1)}, f32[128,128]{1,0:T(8,128)S(1)}, u32[]{:S(2)}, u32[]{:S(2)}) collective-permute-start(f32[128,128]{1,0:T(8,128)S(1)} %get-tuple-element.41), channel_id=1, source_target_pairs={{0,32},{32,0},{64,96},{96,64},{1,33},{33,1},{65,97},{97,65},{2,34}... | collective-permute-start | bytes 196616 | tf_op jit(solution)/shard_map/ppermute | solution.py:482
  15.7 0.1 collective-permute-start.2
  15.8 0.0 collective-permute-done.6.soff
  15.8 2.0 %collective-permute-done.5.far = f32[128,128]{1,0:T(8,128)S(1)} collective-permute-done((f32[128,128]{1,0:T(8,128)S(1)}, f32[128,128]{1,0:T(8,128)S(1)}, u32[]{:S(2)}, u32[]{:S(2)}) %collective-permute-start.5) | collective-permute-done | bytes 65568 | tf_op jit(solution)/shard_map/ppermute | solution.py:482
  17.8 0.0 collective-permute-done.4.near2
  17.8 2.3 %collective-permute-done.3.near1 = f32[128,128]{1,0:T(8,128)S(1)} collective-permute-done((f32[128,128]{1,0:T(8,128)S(1)}, f32[128,128]{1,0:T(8,128)S(1)}, u32[]{:S(2)}, u32[]{:S(2)}) %collective-permute-start.3) | collective-permute-done | bytes 65568 | tf_op jit(solution)/shard_map/ppermute | solution.py:482
  20.1 0.1 collective-permute-start.8
  20.2 1.7 %collective-permute-start.7 = (f32[192,128]{1,0:T(8,128)S(1)}, f32[192,128]{1,0:T(8,128)S(1)}, u32[]{:S(2)}, u32[]{:S(2)}) collective-permute-start(f32[192,128]{1,0:T(8,128)S(1)} %get-tuple-element.49), channel_id=1, source_target_pairs={{33,34},{35,36},{37,38},{39,40},{41,42},{43,44},{45,46},{47,48},{4... | collective-permute-start | bytes 294920 | tf_op jit(solution)/shard_map/ppermute | solution.py:442
  22.0 4.5 %collective-permute-done.7.off = f32[192,128]{1,0:T(8,128)S(1)} collective-permute-done((f32[192,128]{1,0:T(8,128)S(1)}, f32[192,128]{1,0:T(8,128)S(1)}, u32[]{:S(2)}, u32[]{:S(2)}) %collective-permute-start.7) | collective-permute-done | bytes 98336 | tf_op jit(solution)/shard_map/ppermute | solution.py:442
  26.5 0.0 collective-permute-done.2.before
  26.5 0.0 collective-permute-done.8.inside
  26.5 3.3 %chain.1 = (f32[32,2048]{1,0:T(8,128)}, f32[32,2048]{1,0:T(8,128)}) custom-call(s32[1]{0:T(128)} %bitcast.place, s32[1]{0:T(128)} %bitcast.1.space, s32[1]{0:T(128)} %constant.10.clone.1.last, f32[512,128]{1,0:T(8,128)S(1)} %get-tuple-element.33.own, f32[7,24,8,128]{3,2,1,0:T(8,128)S(1)} %get-tuple-element.34.cstate_in.cstate, ...), custom_call_target="tpu_custom_call" | custom-call | tf_op jit(solution)/shard_map/chain/pallas_call | solution.py:414
  (1 shorter events, 0.0 us)
Async XLA Ops:
  2.1 7.7 %collective-permute-start.1 = (f32[456,128]{1,0:T(8,128)S(1)}, f32[456,128]{1,0:T(8,128)S(1)}, u32[]{:S(2)}, u32[]{:S(2)}) collective-permute-start(f32[456,128]{1,0:T(8,128)S(1)} %get-tuple-element.36), channel_id=1, source_target_pairs={{0,1},{1,0},{2,3},{3,2},{4,5},{5,4},{6,7},{7,6},{8,9},{9,8},{10,11... | collective-permute-start | bytes 700424 | tf_op jit(solution)/shard_map/ppermute | solution.py:447
  2.2 7.6 %collective-permute-start = (f32[448,128]{1,0:T(8,128)S(1)}, f32[448,128]{1,0:T(8,128)S(1)}, u32[]{:S(2)}, u32[]{:S(2)}) collective-permute-start(f32[448,128]{1,0:T(8,128)S(1)} %get-tuple-element.35), channel_id=1, source_target_pairs={{1,2},{3,4},{5,6},{7,8},{9,10},{11,12},{13,14},{15,16},{17,18},{19... | collective-permute-start | bytes 688136 | tf_op jit(solution)/shard_map/ppermute | solution.py:434
  8.2 7.7 %collective-permute-start.6 = (f32[288,128]{1,0:T(8,128)}, f32[288,128]{1,0:T(8,128)S(1)}, u32[]{:S(2)}, u32[]{:S(2)}) collective-permute-start(f32[288,128]{1,0:T(8,128)} %get-tuple-element.42), channel_id=1, source_target_pairs={{33,34},{35,36},{37,38},{39,40},{41,42},{43,44},{45,46},{47,48},{4... | collective-permute-start | bytes 442376 | tf_op jit(solution)/shard_map/ppermute | solution.py:442
  11.6 6.3 %collective-permute-start.5 = (f32[128,128]{1,0:T(8,128)S(1)}, f32[128,128]{1,0:T(8,128)S(1)}, u32[]{:S(2)}, u32[]{:S(2)}) collective-permute-start(f32[128,128]{1,0:T(8,128)S(1)} %get-tuple-element.41), channel_id=1, source_target_pairs={{0,96},{32,64},{64,32},{96,0},{1,97},{33,65},{65,33},{97,1},{2,98}... | collective-permute-start | bytes 196616 | tf_op jit(solution)/shard_map/ppermute | solution.py:482
  11.7 6.2 %collective-permute-start.4 = (f32[128,128]{1,0:T(8,128)S(1)}, f32[128,128]{1,0:T(8,128)S(1)}, u32[]{:S(2)}, u32[]{:S(2)}) collective-permute-start(f32[128,128]{1,0:T(8,128)S(1)} %get-tuple-element.41), channel_id=1, source_target_pairs={{0,64},{32,96},{64,0},{96,32},{1,65},{33,97},{65,1},{97,33},{2,66}... | collective-permute-start | bytes 196616 | tf_op jit(solution)/shard_map/ppermute | solution.py:482
  14.1 6.0 %collective-permute-start.3 = (f32[128,128]{1,0:T(8,128)S(1)}, f32[128,128]{1,0:T(8,128)S(1)}, u32[]{:S(2)}, u32[]{:S(2)}) collective-permute-start(f32[128,128]{1,0:T(8,128)S(1)} %get-tuple-element.41), channel_id=1, source_target_pairs={{0,32},{32,0},{64,96},{96,64},{1,33},{33,1},{65,97},{97,65},{2,34}... | collective-permute-start | bytes 196616 | tf_op jit(solution)/shard_map/ppermute | solution.py:482
  15.7 10.7 %collective-permute-start.2 = (f32[512,128]{1,0:T(8,128)S(1)}, f32[512,128]{1,0:T(8,128)S(1)}, u32[]{:S(2)}, u32[]{:S(2)}) collective-permute-start(f32[512,128]{1,0:T(8,128)S(1)} %get-tuple-element.39.end), channel_id=1, source_target_pairs={{0,32},{32,64},{64,96},{96,0},{1,33},{33,65},{65,97},{97,1},{2,34}... | collective-permute-start | bytes 786440 | tf_op jit(solution)/shard_map/ppermute | solution.py:427
  20.1 6.3 %collective-permute-start.8 = (f32[480,128]{1,0:T(8,128)S(1)}, f32[480,128]{1,0:T(8,128)S(1)}, u32[]{:S(2)}, u32[]{:S(2)}) collective-permute-start(f32[480,128]{1,0:T(8,128)S(1)} %get-tuple-element.50), channel_id=1, source_target_pairs={{0,1},{1,0},{2,3},{3,2},{4,5},{5,4},{6,7},{7,6},{8,9},{9,8},{10,11... | collective-permute-start | bytes 737288 | tf_op jit(solution)/shard_map/ppermute | solution.py:447
  20.2 6.2 %collective-permute-start.7 = (f32[192,128]{1,0:T(8,128)S(1)}, f32[192,128]{1,0:T(8,128)S(1)}, u32[]{:S(2)}, u32[]{:S(2)}) collective-permute-start(f32[192,128]{1,0:T(8,128)S(1)} %get-tuple-element.49), channel_id=1, source_target_pairs={{33,34},{35,36},{37,38},{39,40},{41,42},{43,44},{45,46},{47,48},{4... | collective-permute-start | bytes 294920 | tf_op jit(solution)/shard_map/ppermute | solution.py:442

commit v7 on v6

--- a/solution.py
+++ b/solution.py
@@ -291,7 +291,7 @@
     target[...] = source[...]
 
 
-def gather_kernel(place, space, cstate, near1, near2, far, base, j1, j2, off, inside):
+def gather_kernel(place, space, cstate, far, near2, near1, base, j1, j2, off, inside):
     m = place[0]
     base[...] = jnp.where(m == 1, near1[...], jnp.where(m == 2, near2[...], far[...]))
     j1[...] = jnp.where(m == 2, far[...], near2[...])
@@ -479,7 +479,7 @@
         "sssvvvvv",
     )
     soff = far_swap_later(soff)
-    rounds = [lax.ppermute(payload, "tm", [(i, i ^ k) for i in range(lax.axis_size("tm"))]) for k in (1, 2, 3)]
+    rounds = [lax.ppermute(payload, "tm", [(i, i ^ k) for i in range(lax.axis_size("tm"))]) for k in (3, 2, 1)]
     *rounds, soff = lax.optimization_barrier((*rounds, soff))
     base, j1, j2, off, inside = call(
         gather_kernel, "gather", (place, space, cstate, *rounds),

time: 29.9 us -> 29.1 us (0.973)
  the two profiles are of different devices: /device:TPU:102 before, /device:TPU:66 now
where the time goes in v7:
time: 29.1 us; the launch traced here: 28.9 us
  starting transfers between devices  12.2 us (42%)
  Pallas kernels  8.53 us (29%)
  waiting for transfers between devices  7.54 us (26%)
  between operations  0.69 us (2%)
    pallas_call x5, Pallas kernels, call(): pl.pallas_call(kernel, out_shape=outs, in_specs=[pl.BlockSpec(memory_spac...  8.53 us
    ppermute x2, waiting for transfers between devices, far_swap_later(): lax.ppermute(x, ('tm', 'space'), pairs + [(j, i) for i, j in pairs] + ring)  4.61 us
    ppermute x3, starting transfers between devices, per_device(): lax.ppermute(payload, 'tm', [(i, i ^ k) for i in range(lax.axis_size('tm'...  3.57 us
    ppermute x1, starting transfers between devices, far_swap(): return lax.ppermute(x, ('tm', 'space'), pairs + [(j, i) for i, j in pairs])  3.09 us
    ppermute x1, starting transfers between devices, shifted(): lax.ppermute(x, 'tm', [(i, (i + by) % devices) for i in range(devices)])  2.83 us
    ppermute x2, starting transfers between devices, far_swap_later(): lax.ppermute(x, ('tm', 'space'), pairs + [(j, i) for i, j in pairs] + ring)  2.52 us
    ppermute x3, waiting for transfers between devices, per_device(): lax.ppermute(payload, 'tm', [(i, i ^ k) for i in range(lax.axis_size('tm'...  1.84 us
    ppermute x1, waiting for transfers between devices, far_swap(): return lax.ppermute(x, ('tm', 'space'), pairs + [(j, i) for i, j in pairs])  1.09 us
  transfers between devices with their start and end apart: 9, of which 3 were waited for; matrix products, arithmetic and copies ran while one was open for 0% of the time, Pallas kernels for 15%

profile of v7, /device:TPU:66, one launch (start us, length us, event | category | flops | bytes accessed | tf_op | source)
XLA Modules:
  0.0 28.9 jit_solution(1482337321610236956)
XLA Ops:
  0.6 1.5 %edges.1 = (f32[448,128]{1,0:T(8,128)S(1)}, f32[456,128]{1,0:T(8,128)S(1)}, f32[32,2048]{1,0:T(8,128)S(1)}, s32[32,2048]{1,0:T(8,128)S(1)}, s32[32,2048]{1,0:T(8...) custom-call(s32[1]{0:T(128)} %bitcast.1.space, f32[32,2048]{1,0:T(8,128)} %bitcast.5, s32[32,2048]{1,0:T(8,128)} %bed.1, ...), custom_call_target="tpu_custom_call" | custom-call | tf_op jit(solution)/shard_map/edges/pallas_call | solution.py:414
  2.1 0.1 collective-permute-start.1
  2.2 3.1 %collective-permute-start = (f32[448,128]{1,0:T(8,128)S(1)}, f32[448,128]{1,0:T(8,128)S(1)}, u32[]{:S(2)}, u32[]{:S(2)}) collective-permute-start(f32[448,128]{1,0:T(8,128)S(1)} %get-tuple-element.35), channel_id=1, source_target_pairs={{1,2},{3,4},{5,6},{7,8},{9,10},{11,12},{13,14},{15,16},{17,18},{19... | collective-permute-start | bytes 688136 | tf_op jit(solution)/shard_map/ppermute | solution.py:434
  5.3 2.5 %inner.1 = (f32[512,128]{1,0:T(8,128)S(1)}, f32[256,128]{1,0:T(8,128)S(1)}, f32[8,20,16,128]{3,2,1,0:T(8,128)S(1)}, f32[7,24,8,128]{3,2,1,0:T(8,128)S(1)}, f32[288,128]{1,0:T(8,128)}) custom-call(s32[1]{0:T(128)} %bitcast.1.space, f32[32,2048]{1,0:T(8,128)S(1)} %get-tuple-element.28.tv, s32[32,2048]{1,0:T(8,128)S(1)} %get-tuple-element.29.bv, ...), custom_call_target="tpu_custom_call" | custom-call | tf_op jit(solution)/shard_map/inner/pallas_call | solution.py:414
  7.9 0.9 %collective-permute-start.6 = (f32[288,128]{1,0:T(8,128)}, f32[288,128]{1,0:T(8,128)S(1)}, u32[]{:S(2)}, u32[]{:S(2)}) collective-permute-start(f32[288,128]{1,0:T(8,128)} %get-tuple-element.42), channel_id=1, source_target_pairs={{33,34},{35,36},{37,38},{39,40},{41,42},{43,44},{45,46},{47,48},{4... | collective-permute-start | bytes 442376 | tf_op jit(solution)/shard_map/ppermute | solution.py:442
  8.8 1.1 %collective-permute-done.off = f32[448,128]{1,0:T(8,128)S(1)} collective-permute-done((f32[448,128]{1,0:T(8,128)S(1)}, f32[448,128]{1,0:T(8,128)S(1)}, u32[]{:S(2)}, u32[]{:S(2)}) %collective-permute-start) | collective-permute-done | bytes 229408 | tf_op jit(solution)/shard_map/ppermute | solution.py:434
  9.9 0.0 collective-permute-done.1.inside
  9.9 1.7 %outer.1 = (f32[512,128]{1,0:T(8,128)S(1)}, f32[128,128]{1,0:T(8,128)S(1)}, f32[128,128]{1,0:T(8,128)S(1)}) custom-call(s32[1]{0:T(128)} %bitcast.place, s32[1]{0:T(128)} %bitcast.1.space, s32[1]{0:T(128)} %constant.10.clone.1.last, f32[448,128]{1,0:T(8,128)S(1)} %collective-permute-done.off, f32[456,128]{1,0:T(8,128)S(1)} %collective-permute-done.1.inside, ...), custom_call_target="tpu_custom_call" | custom-call | tf_op jit(solution)/shard_map/outer/pallas_call | solution.py:414
  11.6 1.7 %collective-permute-start.5 = (f32[128,128]{1,0:T(8,128)S(1)}, f32[128,128]{1,0:T(8,128)S(1)}, u32[]{:S(2)}, u32[]{:S(2)}) collective-permute-start(f32[128,128]{1,0:T(8,128)S(1)} %get-tuple-element.41), channel_id=1, source_target_pairs={{0,32},{32,0},{64,96},{96,64},{1,33},{33,1},{65,97},{97,65},{2,34}... | collective-permute-start | bytes 196616 | tf_op jit(solution)/shard_map/ppermute | solution.py:482
  13.3 0.0 collective-permute-start.4
  13.3 1.9 %collective-permute-start.3 = (f32[128,128]{1,0:T(8,128)S(1)}, f32[128,128]{1,0:T(8,128)S(1)}, u32[]{:S(2)}, u32[]{:S(2)}) collective-permute-start(f32[128,128]{1,0:T(8,128)S(1)} %get-tuple-element.41), channel_id=1, source_target_pairs={{0,96},{32,64},{64,32},{96,0},{1,97},{33,65},{65,33},{97,1},{2,98}... | collective-permute-start | bytes 196616 | tf_op jit(solution)/shard_map/ppermute | solution.py:482
  15.1 2.8 %collective-permute-start.2 = (f32[512,128]{1,0:T(8,128)S(1)}, f32[512,128]{1,0:T(8,128)S(1)}, u32[]{:S(2)}, u32[]{:S(2)}) collective-permute-start(f32[512,128]{1,0:T(8,128)S(1)} %get-tuple-element.39.end), channel_id=1, source_target_pairs={{0,32},{32,64},{64,96},{96,0},{1,33},{33,65},{65,97},{97,1},{2,34}... | collective-permute-start | bytes 786440 | tf_op jit(solution)/shard_map/ppermute | solution.py:427
  18.0 0.0 collective-permute-done.6.soff
  18.0 0.0 collective-permute-done.5.near1
  18.0 1.8 %collective-permute-done.4.near2 = f32[128,128]{1,0:T(8,128)S(1)} collective-permute-done((f32[128,128]{1,0:T(8,128)S(1)}, f32[128,128]{1,0:T(8,128)S(1)}, u32[]{:S(2)}, u32[]{:S(2)}) %collective-permute-start.4) | collective-permute-done | bytes 65568 | tf_op jit(solution)/shard_map/ppermute | solution.py:482
  19.8 0.0 collective-permute-done.3.far
  19.9 0.1 collective-permute-start.8
  19.9 1.6 %collective-permute-start.7 = (f32[192,128]{1,0:T(8,128)S(1)}, f32[192,128]{1,0:T(8,128)S(1)}, u32[]{:S(2)}, u32[]{:S(2)}) collective-permute-start(f32[192,128]{1,0:T(8,128)S(1)} %get-tuple-element.49), channel_id=1, source_target_pairs={{33,34},{35,36},{37,38},{39,40},{41,42},{43,44},{45,46},{47,48},{4... | collective-permute-start | bytes 294920 | tf_op jit(solution)/shard_map/ppermute | solution.py:442
  21.6 4.6 %collective-permute-done.7.off = f32[192,128]{1,0:T(8,128)S(1)} collective-permute-done((f32[192,128]{1,0:T(8,128)S(1)}, f32[192,128]{1,0:T(8,128)S(1)}, u32[]{:S(2)}, u32[]{:S(2)}) %collective-permute-start.7) | collective-permute-done | bytes 98336 | tf_op jit(solution)/shard_map/ppermute | solution.py:442
  26.2 0.0 collective-permute-done.2.before
  26.2 0.0 collective-permute-done.8.inside
  26.2 2.8 %chain.1 = (f32[32,2048]{1,0:T(8,128)}, f32[32,2048]{1,0:T(8,128)}) custom-call(s32[1]{0:T(128)} %bitcast.place, s32[1]{0:T(128)} %bitcast.1.space, s32[1]{0:T(128)} %constant.10.clone.1.last, f32[512,128]{1,0:T(8,128)S(1)} %get-tuple-element.33.own, f32[7,24,8,128]{3,2,1,0:T(8,128)S(1)} %get-tuple-element.34.cstate_in.cstate, ...), custom_call_target="tpu_custom_call" | custom-call | tf_op jit(solution)/shard_map/chain/pallas_call | solution.py:414
  (1 shorter events, 0.0 us)
Async XLA Ops:
  2.1 7.7 %collective-permute-start.1 = (f32[456,128]{1,0:T(8,128)S(1)}, f32[456,128]{1,0:T(8,128)S(1)}, u32[]{:S(2)}, u32[]{:S(2)}) collective-permute-start(f32[456,128]{1,0:T(8,128)S(1)} %get-tuple-element.36), channel_id=1, source_target_pairs={{0,1},{1,0},{2,3},{3,2},{4,5},{5,4},{6,7},{7,6},{8,9},{9,8},{10,11... | collective-permute-start | bytes 700424 | tf_op jit(solution)/shard_map/ppermute | solution.py:447
  2.2 7.6 %collective-permute-start = (f32[448,128]{1,0:T(8,128)S(1)}, f32[448,128]{1,0:T(8,128)S(1)}, u32[]{:S(2)}, u32[]{:S(2)}) collective-permute-start(f32[448,128]{1,0:T(8,128)S(1)} %get-tuple-element.35), channel_id=1, source_target_pairs={{1,2},{3,4},{5,6},{7,8},{9,10},{11,12},{13,14},{15,16},{17,18},{19... | collective-permute-start | bytes 688136 | tf_op jit(solution)/shard_map/ppermute | solution.py:434
  7.9 10.1 %collective-permute-start.6 = (f32[288,128]{1,0:T(8,128)}, f32[288,128]{1,0:T(8,128)S(1)}, u32[]{:S(2)}, u32[]{:S(2)}) collective-permute-start(f32[288,128]{1,0:T(8,128)} %get-tuple-element.42), channel_id=1, source_target_pairs={{33,34},{35,36},{37,38},{39,40},{41,42},{43,44},{45,46},{47,48},{4... | collective-permute-start | bytes 442376 | tf_op jit(solution)/shard_map/ppermute | solution.py:442
  11.6 6.4 %collective-permute-start.5 = (f32[128,128]{1,0:T(8,128)S(1)}, f32[128,128]{1,0:T(8,128)S(1)}, u32[]{:S(2)}, u32[]{:S(2)}) collective-permute-start(f32[128,128]{1,0:T(8,128)S(1)} %get-tuple-element.41), channel_id=1, source_target_pairs={{0,32},{32,0},{64,96},{96,64},{1,33},{33,1},{65,97},{97,65},{2,34}... | collective-permute-start | bytes 196616 | tf_op jit(solution)/shard_map/ppermute | solution.py:482
  13.3 6.5 %collective-permute-start.4 = (f32[128,128]{1,0:T(8,128)S(1)}, f32[128,128]{1,0:T(8,128)S(1)}, u32[]{:S(2)}, u32[]{:S(2)}) collective-permute-start(f32[128,128]{1,0:T(8,128)S(1)} %get-tuple-element.41), channel_id=1, source_target_pairs={{0,64},{32,96},{64,0},{96,32},{1,65},{33,97},{65,1},{97,33},{2,66}... | collective-permute-start | bytes 196616 | tf_op jit(solution)/shard_map/ppermute | solution.py:482
  13.3 6.5 %collective-permute-start.3 = (f32[128,128]{1,0:T(8,128)S(1)}, f32[128,128]{1,0:T(8,128)S(1)}, u32[]{:S(2)}, u32[]{:S(2)}) collective-permute-start(f32[128,128]{1,0:T(8,128)S(1)} %get-tuple-element.41), channel_id=1, source_target_pairs={{0,96},{32,64},{64,32},{96,0},{1,97},{33,65},{65,33},{97,1},{2,98}... | collective-permute-start | bytes 196616 | tf_op jit(solution)/shard_map/ppermute | solution.py:482
  15.1 11.0 %collective-permute-start.2 = (f32[512,128]{1,0:T(8,128)S(1)}, f32[512,128]{1,0:T(8,128)S(1)}, u32[]{:S(2)}, u32[]{:S(2)}) collective-permute-start(f32[512,128]{1,0:T(8,128)S(1)} %get-tuple-element.39.end), channel_id=1, source_target_pairs={{0,32},{32,64},{64,96},{96,0},{1,33},{33,65},{65,97},{97,1},{2,34}... | collective-permute-start | bytes 786440 | tf_op jit(solution)/shard_map/ppermute | solution.py:427
  19.9 6.3 %collective-permute-start.8 = (f32[480,128]{1,0:T(8,128)S(1)}, f32[480,128]{1,0:T(8,128)S(1)}, u32[]{:S(2)}, u32[]{:S(2)}) collective-permute-start(f32[480,128]{1,0:T(8,128)S(1)} %get-tuple-element.50), channel_id=1, source_target_pairs={{0,1},{1,0},{2,3},{3,2},{4,5},{5,4},{6,7},{7,6},{8,9},{9,8},{10,11... | collective-permute-start | bytes 737288 | tf_op jit(solution)/shard_map/ppermute | solution.py:447
  19.9 6.2 %collective-permute-start.7 = (f32[192,128]{1,0:T(8,128)S(1)}, f32[192,128]{1,0:T(8,128)S(1)}, u32[]{:S(2)}, u32[]{:S(2)}) collective-permute-start(f32[192,128]{1,0:T(8,128)S(1)} %get-tuple-element.49), channel_id=1, source_target_pairs={{33,34},{35,36},{37,38},{39,40},{41,42},{43,44},{45,46},{47,48},{4... | collective-permute-start | bytes 294920 | tf_op jit(solution)/shard_map/ppermute | solution.py:442

commit v8 on v7

--- a/solution.py
+++ b/solution.py
@@ -176,7 +176,6 @@
         off[at : at + n] = ref[odd, pl.ds(odd * skip, n)]
         inside[at : at + n] = ref[1 - odd, pl.ds((1 - odd) * skip, n)]
         at += n
-    inside[at : at + 8] = jnp.zeros((8, 128), F32)
     for copy in copies[10:]:
         copy.wait()
 
@@ -460,7 +459,7 @@
     maps = [jax.ShapeDtypeStruct((ROWS, CH * 128), t) for t in (F32, jnp.int32, jnp.int32, jnp.int32)]
     maps.append(lines(24))
     off, inside, *maps = call(
-        edge_kernel, "edges", raw, [lines(EDGE_LINES), lines(EDGE_LINES + 8)] + maps,
+        edge_kernel, "edges", raw, [lines(EDGE_LINES)] * 2 + maps,
         tables + [(2, 8 * CH, 128)] * 4 + [pltpu.SemaphoreType.DMA((14,))],
         "shhhhhh",
     )

time: 29.1 us -> 29 us (level)
  starting transfers between devices: 12.2 us -> 11.4 us
  waiting for transfers between devices: 7.54 us -> 8.29 us
    ppermute x2, waiting for transfers between devices: 4.61 us -> 5.32 us  [far_swap_later(): lax.ppermute(x, ('tm', 'space'), pairs + [(j, i) for i, j in pairs] + ring)]
    ppermute x1, starting transfers between devices: 3.09 us -> 2.51 us  [far_swap(): return lax.ppermute(x, ('tm', 'space'), pairs + [(j, i) for i, j in pairs])]
where the time goes in v8:
time: 29 us; the launch traced here: 28.9 us
  starting transfers between devices  11.4 us (39%)
  Pallas kernels  8.51 us (29%)
  waiting for transfers between devices  8.29 us (29%)
  between operations  0.68 us (2%)
    pallas_call x5, Pallas kernels, call(): pl.pallas_call(kernel, out_shape=outs, in_specs=[pl.BlockSpec(memory_spac...  8.51 us
    ppermute x2, waiting for transfers between devices, far_swap_later(): lax.ppermute(x, ('tm', 'space'), pairs + [(j, i) for i, j in pairs] + ring)  5.32 us
    ppermute x3, starting transfers between devices, per_device(): lax.ppermute(payload, 'tm', [(i, i ^ k) for i in range(lax.axis_size('tm'...  3.57 us
    ppermute x1, starting transfers between devices, shifted(): lax.ppermute(x, 'tm', [(i, (i + by) % devices) for i in range(devices)])  2.83 us
    ppermute x1, starting transfers between devices, far_swap(): return lax.ppermute(x, ('tm', 'space'), pairs + [(j, i) for i, j in pairs])  2.51 us
    ppermute x2, starting transfers between devices, far_swap_later(): lax.ppermute(x, ('tm', 'space'), pairs + [(j, i) for i, j in pairs] + ring)  2.39 us
    ppermute x3, waiting for transfers between devices, per_device(): lax.ppermute(payload, 'tm', [(i, i ^ k) for i in range(lax.axis_size('tm'...  1.88 us
    ppermute x1, waiting for transfers between devices, far_swap(): return lax.ppermute(x, ('tm', 'space'), pairs + [(j, i) for i, j in pairs])  1.09 us
  transfers between devices with their start and end apart: 9, of which 3 were waited for; matrix products, arithmetic and copies ran while one was open for 0% of the time, Pallas kernels for 15%

profile of v8, /device:TPU:66, one launch (start us, length us, event | category | flops | bytes accessed | tf_op | source)
XLA Modules:
  0.0 28.9 jit_solution(12406487115936590991)
XLA Ops:
  0.6 1.5 %edges.1 = (f32[448,128]{1,0:T(8,128)S(1)}, f32[448,128]{1,0:T(8,128)S(1)}, f32[32,2048]{1,0:T(8,128)S(1)}, s32[32,2048]{1,0:T(8,128)S(1)}, s32[32,2048]{1,0:T(8...) custom-call(s32[1]{0:T(128)} %bitcast.1.space, f32[32,2048]{1,0:T(8,128)} %bitcast.5, s32[32,2048]{1,0:T(8,128)} %bed.1, ...), custom_call_target="tpu_custom_call" | custom-call | tf_op jit(solution)/shard_map/edges/pallas_call | solution.py:413
  2.1 2.5 %collective-permute-start = (f32[448,128]{1,0:T(8,128)S(1)}, f32[448,128]{1,0:T(8,128)S(1)}, u32[]{:S(2)}, u32[]{:S(2)}) collective-permute-start(f32[448,128]{1,0:T(8,128)S(1)} %get-tuple-element.35), channel_id=1, source_target_pairs={{1,2},{3,4},{5,6},{7,8},{9,10},{11,12},{13,14},{15,16},{17,18},{19... | collective-permute-start | bytes 688136 | tf_op jit(solution)/shard_map/ppermute | solution.py:433
  4.6 0.0 collective-permute-start.1
  4.6 2.5 %inner.1 = (f32[512,128]{1,0:T(8,128)S(1)}, f32[256,128]{1,0:T(8,128)S(1)}, f32[8,20,16,128]{3,2,1,0:T(8,128)S(1)}, f32[7,24,8,128]{3,2,1,0:T(8,128)S(1)}, f32[288,128]{1,0:T(8,128)}) custom-call(s32[1]{0:T(128)} %bitcast.1.space, f32[32,2048]{1,0:T(8,128)S(1)} %get-tuple-element.28.tv, s32[32,2048]{1,0:T(8,128)S(1)} %get-tuple-element.29.bv, ...), custom_call_target="tpu_custom_call" | custom-call | tf_op jit(solution)/shard_map/inner/pallas_call | solution.py:413
  7.2 1.5 %collective-permute-start.6 = (f32[288,128]{1,0:T(8,128)}, f32[288,128]{1,0:T(8,128)S(1)}, u32[]{:S(2)}, u32[]{:S(2)}) collective-permute-start(f32[288,128]{1,0:T(8,128)} %get-tuple-element.42), channel_id=1, source_target_pairs={{33,34},{35,36},{37,38},{39,40},{41,42},{43,44},{45,46},{47,48},{4... | collective-permute-start | bytes 442376 | tf_op jit(solution)/shard_map/ppermute | solution.py:441
  8.7 1.1 %collective-permute-done.off = f32[448,128]{1,0:T(8,128)S(1)} collective-permute-done((f32[448,128]{1,0:T(8,128)S(1)}, f32[448,128]{1,0:T(8,128)S(1)}, u32[]{:S(2)}, u32[]{:S(2)}) %collective-permute-start) | collective-permute-done | bytes 229408 | tf_op jit(solution)/shard_map/ppermute | solution.py:433
  9.8 0.0 collective-permute-done.1.inside
  9.8 1.7 %outer.1 = (f32[512,128]{1,0:T(8,128)S(1)}, f32[128,128]{1,0:T(8,128)S(1)}, f32[128,128]{1,0:T(8,128)S(1)}) custom-call(s32[1]{0:T(128)} %bitcast.place, s32[1]{0:T(128)} %bitcast.1.space, s32[1]{0:T(128)} %constant.10.clone.1.last, f32[448,128]{1,0:T(8,128)S(1)} %collective-permute-done.off, f32[448,128]{1,0:T(8,128)S(1)} %collective-permute-done.1.inside, ...), custom_call_target="tpu_custom_call" | custom-call | tf_op jit(solution)/shard_map/outer/pallas_call | solution.py:413
  11.5 1.7 %collective-permute-start.5 = (f32[128,128]{1,0:T(8,128)S(1)}, f32[128,128]{1,0:T(8,128)S(1)}, u32[]{:S(2)}, u32[]{:S(2)}) collective-permute-start(f32[128,128]{1,0:T(8,128)S(1)} %get-tuple-element.41), channel_id=1, source_target_pairs={{0,32},{32,0},{64,96},{96,64},{1,33},{33,1},{65,97},{97,65},{2,34}... | collective-permute-start | bytes 196616 | tf_op jit(solution)/shard_map/ppermute | solution.py:481
  13.2 0.0 collective-permute-start.4
  13.2 1.9 %collective-permute-start.3 = (f32[128,128]{1,0:T(8,128)S(1)}, f32[128,128]{1,0:T(8,128)S(1)}, u32[]{:S(2)}, u32[]{:S(2)}) collective-permute-start(f32[128,128]{1,0:T(8,128)S(1)} %get-tuple-element.41), channel_id=1, source_target_pairs={{0,96},{32,64},{64,32},{96,0},{1,97},{33,65},{65,33},{97,1},{2,98}... | collective-permute-start | bytes 196616 | tf_op jit(solution)/shard_map/ppermute | solution.py:481
  15.0 2.8 %collective-permute-start.2 = (f32[512,128]{1,0:T(8,128)S(1)}, f32[512,128]{1,0:T(8,128)S(1)}, u32[]{:S(2)}, u32[]{:S(2)}) collective-permute-start(f32[512,128]{1,0:T(8,128)S(1)} %get-tuple-element.39.end), channel_id=1, source_target_pairs={{0,32},{32,64},{64,96},{96,0},{1,33},{33,65},{65,97},{97,1},{2,34}... | collective-permute-start | bytes 786440 | tf_op jit(solution)/shard_map/ppermute | solution.py:426
  17.9 0.0 collective-permute-done.6.soff
  17.9 0.0 collective-permute-done.5.near1
  17.9 1.9 %collective-permute-done.4.near2 = f32[128,128]{1,0:T(8,128)S(1)} collective-permute-done((f32[128,128]{1,0:T(8,128)S(1)}, f32[128,128]{1,0:T(8,128)S(1)}, u32[]{:S(2)}, u32[]{:S(2)}) %collective-permute-start.4) | collective-permute-done | bytes 65568 | tf_op jit(solution)/shard_map/ppermute | solution.py:481
  19.7 0.0 collective-permute-done.3.far
  19.8 0.1 collective-permute-start.8
  19.9 0.9 %collective-permute-start.7 = (f32[192,128]{1,0:T(8,128)S(1)}, f32[192,128]{1,0:T(8,128)S(1)}, u32[]{:S(2)}, u32[]{:S(2)}) collective-permute-start(f32[192,128]{1,0:T(8,128)S(1)} %get-tuple-element.49), channel_id=1, source_target_pairs={{33,34},{35,36},{37,38},{39,40},{41,42},{43,44},{45,46},{47,48},{4... | collective-permute-start | bytes 294920 | tf_op jit(solution)/shard_map/ppermute | solution.py:441
  20.8 5.3 %collective-permute-done.7.off = f32[192,128]{1,0:T(8,128)S(1)} collective-permute-done((f32[192,128]{1,0:T(8,128)S(1)}, f32[192,128]{1,0:T(8,128)S(1)}, u32[]{:S(2)}, u32[]{:S(2)}) %collective-permute-start.7) | collective-permute-done | bytes 98336 | tf_op jit(solution)/shard_map/ppermute | solution.py:441
  26.1 0.0 collective-permute-done.2.before
  26.1 0.0 collective-permute-done.8.inside
  26.1 2.8 %chain.1 = (f32[32,2048]{1,0:T(8,128)}, f32[32,2048]{1,0:T(8,128)}) custom-call(s32[1]{0:T(128)} %bitcast.place, s32[1]{0:T(128)} %bitcast.1.space, s32[1]{0:T(128)} %constant.10.clone.1.last, f32[512,128]{1,0:T(8,128)S(1)} %get-tuple-element.33.own, f32[7,24,8,128]{3,2,1,0:T(8,128)S(1)} %get-tuple-element.34.cstate_in.cstate, ...), custom_call_target="tpu_custom_call" | custom-call | tf_op jit(solution)/shard_map/chain/pallas_call | solution.py:413
  (1 shorter events, 0.0 us)
Async XLA Ops:
  2.1 7.6 %collective-permute-start = (f32[448,128]{1,0:T(8,128)S(1)}, f32[448,128]{1,0:T(8,128)S(1)}, u32[]{:S(2)}, u32[]{:S(2)}) collective-permute-start(f32[448,128]{1,0:T(8,128)S(1)} %get-tuple-element.35), channel_id=1, source_target_pairs={{1,2},{3,4},{5,6},{7,8},{9,10},{11,12},{13,14},{15,16},{17,18},{19... | collective-permute-start | bytes 688136 | tf_op jit(solution)/shard_map/ppermute | solution.py:433
  4.6 5.1 %collective-permute-start.1 = (f32[448,128]{1,0:T(8,128)S(1)}, f32[448,128]{1,0:T(8,128)S(1)}, u32[]{:S(2)}, u32[]{:S(2)}) collective-permute-start(f32[448,128]{1,0:T(8,128)S(1)} %get-tuple-element.36), channel_id=1, source_target_pairs={{0,1},{1,0},{2,3},{3,2},{4,5},{5,4},{6,7},{7,6},{8,9},{9,8},{10,11... | collective-permute-start | bytes 688136 | tf_op jit(solution)/shard_map/ppermute | solution.py:446
  7.2 10.7 %collective-permute-start.6 = (f32[288,128]{1,0:T(8,128)}, f32[288,128]{1,0:T(8,128)S(1)}, u32[]{:S(2)}, u32[]{:S(2)}) collective-permute-start(f32[288,128]{1,0:T(8,128)} %get-tuple-element.42), channel_id=1, source_target_pairs={{33,34},{35,36},{37,38},{39,40},{41,42},{43,44},{45,46},{47,48},{4... | collective-permute-start | bytes 442376 | tf_op jit(solution)/shard_map/ppermute | solution.py:441
  11.5 6.4 %collective-permute-start.5 = (f32[128,128]{1,0:T(8,128)S(1)}, f32[128,128]{1,0:T(8,128)S(1)}, u32[]{:S(2)}, u32[]{:S(2)}) collective-permute-start(f32[128,128]{1,0:T(8,128)S(1)} %get-tuple-element.41), channel_id=1, source_target_pairs={{0,32},{32,0},{64,96},{96,64},{1,33},{33,1},{65,97},{97,65},{2,34}... | collective-permute-start | bytes 196616 | tf_op jit(solution)/shard_map/ppermute | solution.py:481
  13.2 6.6 %collective-permute-start.4 = (f32[128,128]{1,0:T(8,128)S(1)}, f32[128,128]{1,0:T(8,128)S(1)}, u32[]{:S(2)}, u32[]{:S(2)}) collective-permute-start(f32[128,128]{1,0:T(8,128)S(1)} %get-tuple-element.41), channel_id=1, source_target_pairs={{0,64},{32,96},{64,0},{96,32},{1,65},{33,97},{65,1},{97,33},{2,66}... | collective-permute-start | bytes 196616 | tf_op jit(solution)/shard_map/ppermute | solution.py:481
  13.2 6.6 %collective-permute-start.3 = (f32[128,128]{1,0:T(8,128)S(1)}, f32[128,128]{1,0:T(8,128)S(1)}, u32[]{:S(2)}, u32[]{:S(2)}) collective-permute-start(f32[128,128]{1,0:T(8,128)S(1)} %get-tuple-element.41), channel_id=1, source_target_pairs={{0,96},{32,64},{64,32},{96,0},{1,97},{33,65},{65,33},{97,1},{2,98}... | collective-permute-start | bytes 196616 | tf_op jit(solution)/shard_map/ppermute | solution.py:481
  15.0 11.1 %collective-permute-start.2 = (f32[512,128]{1,0:T(8,128)S(1)}, f32[512,128]{1,0:T(8,128)S(1)}, u32[]{:S(2)}, u32[]{:S(2)}) collective-permute-start(f32[512,128]{1,0:T(8,128)S(1)} %get-tuple-element.39.end), channel_id=1, source_target_pairs={{0,32},{32,64},{64,96},{96,0},{1,33},{33,65},{65,97},{97,1},{2,34}... | collective-permute-start | bytes 786440 | tf_op jit(solution)/shard_map/ppermute | solution.py:426
  19.8 6.3 %collective-permute-start.8 = (f32[480,128]{1,0:T(8,128)S(1)}, f32[480,128]{1,0:T(8,128)S(1)}, u32[]{:S(2)}, u32[]{:S(2)}) collective-permute-start(f32[480,128]{1,0:T(8,128)S(1)} %get-tuple-element.50), channel_id=1, source_target_pairs={{0,1},{1,0},{2,3},{3,2},{4,5},{5,4},{6,7},{7,6},{8,9},{9,8},{10,11... | collective-permute-start | bytes 737288 | tf_op jit(solution)/shard_map/ppermute | solution.py:446
  19.9 6.2 %collective-permute-start.7 = (f32[192,128]{1,0:T(8,128)S(1)}, f32[192,128]{1,0:T(8,128)S(1)}, u32[]{:S(2)}, u32[]{:S(2)}) collective-permute-start(f32[192,128]{1,0:T(8,128)S(1)} %get-tuple-element.49), channel_id=1, source_target_pairs={{33,34},{35,36},{37,38},{39,40},{41,42},{43,44},{45,46},{47,48},{4... | collective-permute-start | bytes 294920 | tf_op jit(solution)/shard_map/ppermute | solution.py:441

commit v9 on v8

--- a/solution.py
+++ b/solution.py
@@ -207,8 +207,8 @@
     state[S0, mine] = state[G, mine] + state[H0, mine]
     for at, cslot in enumerate((CG, CC, CTA)):
         off[at * n : at * n + n] = cstate[cslot, pl.ds(4 + odd * (CROWS - CHALO), CHALO)].reshape(n, 128)
-    coarse_steps(cstate, d, dy, ((6, 18), (8, 16)))
-    fine_steps(state, d, dy, [(HALO + 2 * k, WIN - HALO - 2 * k) for k in (1, 2, 3, 4)])
+    coarse_steps(cstate, d, dy, ((0, 6, 18), (1, 8, 16)))
+    fine_steps(state, d, dy, [(k - 1, HALO + 2 * k, WIN - HALO - 2 * k) for k in (1, 2, 3, 4)])
     mid[...] = state[H0 + 4, 2 * HALO : WIN - 2 * HALO].reshape(16 * CH, 128)
     for at, slot in enumerate(KEPT):
         rims[at, 0:RIM] = state[slot, HALO : HALO + RIM]
@@ -218,7 +218,7 @@
 def coarse_steps(cstate, d, dy, spans):
     masks = column_masks(CCH)
     cd, cdy = d.at[0:24, 0:CCH], dy.at[0:24, 0:CCH]
-    for step, (lo, hi) in enumerate(spans):
+    for step, lo, hi in spans:
 
         def emit(a, b, value, step=step):
             if step == 0:
@@ -233,7 +233,7 @@
 
 def fine_steps(state, d, dy, spans):
     masks = column_masks(CH)
-    for step, (lo, hi) in enumerate(spans):
+    for step, lo, hi in spans:
 
         def emit(a, b, value, step=step):
             state[H0 + step + 1, a:b] = value
@@ -274,11 +274,12 @@
     for lo, clo in ((4, 2), (40, 20)):
         cstate[CC, clo : clo + 2] = restrict(state[C, lo : lo + 4], mats)
         cstate[CTA, clo : clo + 2] = restrict(state[TA, lo : lo + 4], mats) * ratio
-    coarse_steps(cstate, d, dy, ((2, 6), (4, 8)))
-    coarse_steps(cstate, d, dy, ((18, 22), (16, 20)))
+    coarse_steps(cstate, d, dy, ((0, 2, 6), (0, 18, 22), (1, 4, 8), (1, 16, 20)))
     prev[...] = cstate[CH0, 4:20].reshape(CROWS * CCH, 128)
-    fine_steps(state, d, dy, [(2 * k, HALO + 2 * k) for k in (1, 2, 3, 4)])
-    fine_steps(state, d, dy, [(WIN - HALO - 2 * k, WIN - 2 * k) for k in (1, 2, 3, 4)])
+    spans = []
+    for k in (1, 2, 3, 4):
+        spans += [(k - 1, 2 * k, HALO + 2 * k), (k - 1, WIN - HALO - 2 * k, WIN - 2 * k)]
+    fine_steps(state, d, dy, spans)
     end[0 : 8 * CH] = state[H0 + 4, 8:16].reshape(8 * CH, 128)
     end[8 * CH : 24 * CH] = mid[...]
     end[24 * CH : 32 * CH] = state[H0 + 4, 32:40].reshape(8 * CH, 128)

time: 29 us -> 29 us (level)
  no operation moved by 1% of the time
where the time goes in v9:
time: 29 us; the launch traced here: 28.9 us
  starting transfers between devices  11.4 us (39%)
  Pallas kernels  8.5 us (29%)
  waiting for transfers between devices  8.28 us (29%)
  between operations  0.68 us (2%)
    pallas_call x5, Pallas kernels, call(): pl.pallas_call(kernel, out_shape=outs, in_specs=[pl.BlockSpec(memory_spac...  8.5 us
    ppermute x2, waiting for transfers between devices, far_swap_later(): lax.ppermute(x, ('tm', 'space'), pairs + [(j, i) for i, j in pairs] + ring)  5.31 us
    ppermute x3, starting transfers between devices, per_device(): lax.ppermute(payload, 'tm', [(i, i ^ k) for i in range(lax.axis_size('tm'...  3.57 us
    ppermute x1, starting transfers between devices, shifted(): lax.ppermute(x, 'tm', [(i, (i + by) % devices) for i in range(devices)])  2.83 us
    ppermute x1, starting transfers between devices, far_swap(): return lax.ppermute(x, ('tm', 'space'), pairs + [(j, i) for i, j in pairs])  2.51 us
    ppermute x2, starting transfers between devices, far_swap_later(): lax.ppermute(x, ('tm', 'space'), pairs + [(j, i) for i, j in pairs] + ring)  2.4 us
    ppermute x3, waiting for transfers between devices, per_device(): lax.ppermute(payload, 'tm', [(i, i ^ k) for i in range(lax.axis_size('tm'...  1.87 us
    ppermute x1, waiting for transfers between devices, far_swap(): return lax.ppermute(x, ('tm', 'space'), pairs + [(j, i) for i, j in pairs])  1.09 us
  transfers between devices with their start and end apart: 9, of which 3 were waited for; matrix products, arithmetic and copies ran while one was open for 0% of the time, Pallas kernels for 15%

profile of v9, /device:TPU:66, one launch (start us, length us, event | category | flops | bytes accessed | tf_op | source)
XLA Modules:
  0.0 28.9 jit_solution(10256477373045150037)
XLA Ops:
  0.6 1.5 %edges.1 = (f32[448,128]{1,0:T(8,128)S(1)}, f32[448,128]{1,0:T(8,128)S(1)}, f32[32,2048]{1,0:T(8,128)S(1)}, s32[32,2048]{1,0:T(8,128)S(1)}, s32[32,2048]{1,0:T(8...) custom-call(s32[1]{0:T(128)} %bitcast.1.space, f32[32,2048]{1,0:T(8,128)} %bitcast.5, s32[32,2048]{1,0:T(8,128)} %bed.1, ...), custom_call_target="tpu_custom_call" | custom-call | tf_op jit(solution)/shard_map/edges/pallas_call | solution.py:414
  2.1 2.5 %collective-permute-start = (f32[448,128]{1,0:T(8,128)S(1)}, f32[448,128]{1,0:T(8,128)S(1)}, u32[]{:S(2)}, u32[]{:S(2)}) collective-permute-start(f32[448,128]{1,0:T(8,128)S(1)} %get-tuple-element.35), channel_id=1, source_target_pairs={{1,2},{3,4},{5,6},{7,8},{9,10},{11,12},{13,14},{15,16},{17,18},{19... | collective-permute-start | bytes 688136 | tf_op jit(solution)/shard_map/ppermute | solution.py:434
  4.6 0.0 collective-permute-start.1
  4.6 2.5 %inner.1 = (f32[512,128]{1,0:T(8,128)S(1)}, f32[256,128]{1,0:T(8,128)S(1)}, f32[8,20,16,128]{3,2,1,0:T(8,128)S(1)}, f32[7,24,8,128]{3,2,1,0:T(8,128)S(1)}, f32[288,128]{1,0:T(8,128)}) custom-call(s32[1]{0:T(128)} %bitcast.1.space, f32[32,2048]{1,0:T(8,128)S(1)} %get-tuple-element.28.tv, s32[32,2048]{1,0:T(8,128)S(1)} %get-tuple-element.29.bv, ...), custom_call_target="tpu_custom_call" | custom-call | tf_op jit(solution)/shard_map/inner/pallas_call | solution.py:414
  7.2 1.5 %collective-permute-start.6 = (f32[288,128]{1,0:T(8,128)}, f32[288,128]{1,0:T(8,128)S(1)}, u32[]{:S(2)}, u32[]{:S(2)}) collective-permute-start(f32[288,128]{1,0:T(8,128)} %get-tuple-element.42), channel_id=1, source_target_pairs={{33,34},{35,36},{37,38},{39,40},{41,42},{43,44},{45,46},{47,48},{4... | collective-permute-start | bytes 442376 | tf_op jit(solution)/shard_map/ppermute | solution.py:442
  8.7 1.1 %collective-permute-done.off = f32[448,128]{1,0:T(8,128)S(1)} collective-permute-done((f32[448,128]{1,0:T(8,128)S(1)}, f32[448,128]{1,0:T(8,128)S(1)}, u32[]{:S(2)}, u32[]{:S(2)}) %collective-permute-start) | collective-permute-done | bytes 229408 | tf_op jit(solution)/shard_map/ppermute | solution.py:434
  9.8 0.0 collective-permute-done.1.inside
  9.8 1.7 %outer.1 = (f32[512,128]{1,0:T(8,128)S(1)}, f32[128,128]{1,0:T(8,128)S(1)}, f32[128,128]{1,0:T(8,128)S(1)}) custom-call(s32[1]{0:T(128)} %bitcast.place, s32[1]{0:T(128)} %bitcast.1.space, s32[1]{0:T(128)} %constant.10.clone.1.last, f32[448,128]{1,0:T(8,128)S(1)} %collective-permute-done.off, f32[448,128]{1,0:T(8,128)S(1)} %collective-permute-done.1.inside, ...), custom_call_target="tpu_custom_call" | custom-call | tf_op jit(solution)/shard_map/outer/pallas_call | solution.py:414
  11.4 1.7 %collective-permute-start.5 = (f32[128,128]{1,0:T(8,128)S(1)}, f32[128,128]{1,0:T(8,128)S(1)}, u32[]{:S(2)}, u32[]{:S(2)}) collective-permute-start(f32[128,128]{1,0:T(8,128)S(1)} %get-tuple-element.41), channel_id=1, source_target_pairs={{0,32},{32,0},{64,96},{96,64},{1,33},{33,1},{65,97},{97,65},{2,34}... | collective-permute-start | bytes 196616 | tf_op jit(solution)/shard_map/ppermute | solution.py:482
  13.1 0.0 collective-permute-start.4
  13.1 1.9 %collective-permute-start.3 = (f32[128,128]{1,0:T(8,128)S(1)}, f32[128,128]{1,0:T(8,128)S(1)}, u32[]{:S(2)}, u32[]{:S(2)}) collective-permute-start(f32[128,128]{1,0:T(8,128)S(1)} %get-tuple-element.41), channel_id=1, source_target_pairs={{0,96},{32,64},{64,32},{96,0},{1,97},{33,65},{65,33},{97,1},{2,98}... | collective-permute-start | bytes 196616 | tf_op jit(solution)/shard_map/ppermute | solution.py:482
  15.0 2.8 %collective-permute-start.2 = (f32[512,128]{1,0:T(8,128)S(1)}, f32[512,128]{1,0:T(8,128)S(1)}, u32[]{:S(2)}, u32[]{:S(2)}) collective-permute-start(f32[512,128]{1,0:T(8,128)S(1)} %get-tuple-element.39.end), channel_id=1, source_target_pairs={{0,32},{32,64},{64,96},{96,0},{1,33},{33,65},{65,97},{97,1},{2,34}... | collective-permute-start | bytes 786440 | tf_op jit(solution)/shard_map/ppermute | solution.py:427
  17.8 0.0 collective-permute-done.6.soff
  17.8 0.0 collective-permute-done.5.near1
  17.9 1.9 %collective-permute-done.4.near2 = f32[128,128]{1,0:T(8,128)S(1)} collective-permute-done((f32[128,128]{1,0:T(8,128)S(1)}, f32[128,128]{1,0:T(8,128)S(1)}, u32[]{:S(2)}, u32[]{:S(2)}) %collective-permute-start.4) | collective-permute-done | bytes 65568 | tf_op jit(solution)/shard_map/ppermute | solution.py:482
  19.7 0.0 collective-permute-done.3.far
  19.8 0.1 collective-permute-start.8
  19.9 0.9 %collective-permute-start.7 = (f32[192,128]{1,0:T(8,128)S(1)}, f32[192,128]{1,0:T(8,128)S(1)}, u32[]{:S(2)}, u32[]{:S(2)}) collective-permute-start(f32[192,128]{1,0:T(8,128)S(1)} %get-tuple-element.49), channel_id=1, source_target_pairs={{33,34},{35,36},{37,38},{39,40},{41,42},{43,44},{45,46},{47,48},{4... | collective-permute-start | bytes 294920 | tf_op jit(solution)/shard_map/ppermute | solution.py:442
  20.8 5.3 %collective-permute-done.7.off = f32[192,128]{1,0:T(8,128)S(1)} collective-permute-done((f32[192,128]{1,0:T(8,128)S(1)}, f32[192,128]{1,0:T(8,128)S(1)}, u32[]{:S(2)}, u32[]{:S(2)}) %collective-permute-start.7) | collective-permute-done | bytes 98336 | tf_op jit(solution)/shard_map/ppermute | solution.py:442
  26.1 0.0 collective-permute-done.2.before
  26.1 0.0 collective-permute-done.8.inside
  26.1 2.8 %chain.1 = (f32[32,2048]{1,0:T(8,128)}, f32[32,2048]{1,0:T(8,128)}) custom-call(s32[1]{0:T(128)} %bitcast.place, s32[1]{0:T(128)} %bitcast.1.space, s32[1]{0:T(128)} %constant.10.clone.1.last, f32[512,128]{1,0:T(8,128)S(1)} %get-tuple-element.33.own, f32[7,24,8,128]{3,2,1,0:T(8,128)S(1)} %get-tuple-element.34.cstate_in.cstate, ...), custom_call_target="tpu_custom_call" | custom-call | tf_op jit(solution)/shard_map/chain/pallas_call | solution.py:414
  (1 shorter events, 0.0 us)
Async XLA Ops:
  2.1 7.6 %collective-permute-start = (f32[448,128]{1,0:T(8,128)S(1)}, f32[448,128]{1,0:T(8,128)S(1)}, u32[]{:S(2)}, u32[]{:S(2)}) collective-permute-start(f32[448,128]{1,0:T(8,128)S(1)} %get-tuple-element.35), channel_id=1, source_target_pairs={{1,2},{3,4},{5,6},{7,8},{9,10},{11,12},{13,14},{15,16},{17,18},{19... | collective-permute-start | bytes 688136 | tf_op jit(solution)/shard_map/ppermute | solution.py:434
  4.6 5.1 %collective-permute-start.1 = (f32[448,128]{1,0:T(8,128)S(1)}, f32[448,128]{1,0:T(8,128)S(1)}, u32[]{:S(2)}, u32[]{:S(2)}) collective-permute-start(f32[448,128]{1,0:T(8,128)S(1)} %get-tuple-element.36), channel_id=1, source_target_pairs={{0,1},{1,0},{2,3},{3,2},{4,5},{5,4},{6,7},{7,6},{8,9},{9,8},{10,11... | collective-permute-start | bytes 688136 | tf_op jit(solution)/shard_map/ppermute | solution.py:447
  7.2 10.7 %collective-permute-start.6 = (f32[288,128]{1,0:T(8,128)}, f32[288,128]{1,0:T(8,128)S(1)}, u32[]{:S(2)}, u32[]{:S(2)}) collective-permute-start(f32[288,128]{1,0:T(8,128)} %get-tuple-element.42), channel_id=1, source_target_pairs={{33,34},{35,36},{37,38},{39,40},{41,42},{43,44},{45,46},{47,48},{4... | collective-permute-start | bytes 442376 | tf_op jit(solution)/shard_map/ppermute | solution.py:442
  11.4 6.4 %collective-permute-start.5 = (f32[128,128]{1,0:T(8,128)S(1)}, f32[128,128]{1,0:T(8,128)S(1)}, u32[]{:S(2)}, u32[]{:S(2)}) collective-permute-start(f32[128,128]{1,0:T(8,128)S(1)} %get-tuple-element.41), channel_id=1, source_target_pairs={{0,32},{32,0},{64,96},{96,64},{1,33},{33,1},{65,97},{97,65},{2,34}... | collective-permute-start | bytes 196616 | tf_op jit(solution)/shard_map/ppermute | solution.py:482
  13.1 6.6 %collective-permute-start.4 = (f32[128,128]{1,0:T(8,128)S(1)}, f32[128,128]{1,0:T(8,128)S(1)}, u32[]{:S(2)}, u32[]{:S(2)}) collective-permute-start(f32[128,128]{1,0:T(8,128)S(1)} %get-tuple-element.41), channel_id=1, source_target_pairs={{0,64},{32,96},{64,0},{96,32},{1,65},{33,97},{65,1},{97,33},{2,66}... | collective-permute-start | bytes 196616 | tf_op jit(solution)/shard_map/ppermute | solution.py:482
  13.1 6.6 %collective-permute-start.3 = (f32[128,128]{1,0:T(8,128)S(1)}, f32[128,128]{1,0:T(8,128)S(1)}, u32[]{:S(2)}, u32[]{:S(2)}) collective-permute-start(f32[128,128]{1,0:T(8,128)S(1)} %get-tuple-element.41), channel_id=1, source_target_pairs={{0,96},{32,64},{64,32},{96,0},{1,97},{33,65},{65,33},{97,1},{2,98}... | collective-permute-start | bytes 196616 | tf_op jit(solution)/shard_map/ppermute | solution.py:482
  15.0 11.1 %collective-permute-start.2 = (f32[512,128]{1,0:T(8,128)S(1)}, f32[512,128]{1,0:T(8,128)S(1)}, u32[]{:S(2)}, u32[]{:S(2)}) collective-permute-start(f32[512,128]{1,0:T(8,128)S(1)} %get-tuple-element.39.end), channel_id=1, source_target_pairs={{0,32},{32,64},{64,96},{96,0},{1,33},{33,65},{65,97},{97,1},{2,34}... | collective-permute-start | bytes 786440 | tf_op jit(solution)/shard_map/ppermute | solution.py:427
  19.8 6.3 %collective-permute-start.8 = (f32[480,128]{1,0:T(8,128)S(1)}, f32[480,128]{1,0:T(8,128)S(1)}, u32[]{:S(2)}, u32[]{:S(2)}) collective-permute-start(f32[480,128]{1,0:T(8,128)S(1)} %get-tuple-element.50), channel_id=1, source_target_pairs={{0,1},{1,0},{2,3},{3,2},{4,5},{5,4},{6,7},{7,6},{8,9},{9,8},{10,11... | collective-permute-start | bytes 737288 | tf_op jit(solution)/shard_map/ppermute | solution.py:447
  19.9 6.2 %collective-permute-start.7 = (f32[192,128]{1,0:T(8,128)S(1)}, f32[192,128]{1,0:T(8,128)S(1)}, u32[]{:S(2)}, u32[]{:S(2)}) collective-permute-start(f32[192,128]{1,0:T(8,128)S(1)} %get-tuple-element.49), channel_id=1, source_target_pairs={{33,34},{35,36},{37,38},{39,40},{41,42},{43,44},{45,46},{47,48},{4... | collective-permute-start | bytes 294920 | tf_op jit(solution)/shard_map/ppermute | solution.py:442
